TPU v7x, 128 devices: a whole 4x4x4 slice. The times are simulated.
128 devices in a mesh: replica: 4 (over z), shard: 32 (over x, y, core).
Axes of the slice: x: 4, y: 4, z: 4, core: 2. Of those that a mesh axis runs over, the one named last changes fastest.
Arguments:
- grads: bfloat16 [4, 2048, 28672], P('replica', 'shard'), may hold values from -3 to 3
- owner_map: int32 [4, 56], replicated, may hold values from 0 to 95, as said below
- factor_left: float32 [128, 3, 512, 512], P(('replica', 'shard')), may hold values from -1 to 7
- factor_right: float32 [128, 3, 512, 512], P(('replica', 'shard')), may hold values from -1 to 7
- left_inverse_roots: bfloat16 [128, 3, 512, 512], P(('replica', 'shard')), may hold values from -1 to 7
- right_inverse_roots: bfloat16 [128, 3, 512, 512], P(('replica', 'shard')), may hold values from -1 to 7
Outputs:
- new_left: float32 [128, 3, 512, 512], P(('replica', 'shard'))
- new_right: float32 [128, 3, 512, 512], P(('replica', 'shard'))
- update: bfloat16 [2048, 28672], P('shard')
Inputs may be any that keep to these rules, and one draw needn't show every extreme that they name: `owner_map`: within one block row and one replica's 14 block columns no two blocks name the same owner; within one replica's 14 block columns no two blocks share an entry; some owner holds 3 blocks in every draw.
All inputs are finite; a program needn't handle non-finite values.
Results may differ from a plain program's by a relative error of at most 0.0058.
Values may be sent and summed in bfloat16 or wider, within the bound.
No kernel may reach another device: no remote copies, remote signals or barrier semaphores. Data moves between devices by JAX's collectives and lax.ppermute only.
A program may use at most 128 MiB of HBM per device.

v0:
```python
import jax
import jax.numpy as jnp
from jax import lax
from jax.sharding import PartitionSpec as P


def precondition(
    row_blocks, slot_rows, factor_left, factor_right, left_inverse_roots, right_inverse_roots
):
    block_size = row_blocks.shape[1]
    collected_blocks = jnp.einsum(
        "ti,iab->tab", slot_rows, row_blocks, preferred_element_type=jnp.float32
    ).astype(jnp.bfloat16)
    left_gram_matrix = jnp.einsum(
        "zqw,zfw->zqf", collected_blocks, collected_blocks, preferred_element_type=jnp.float32
    )
    right_gram_matrix = jnp.einsum(
        "iyj,iyv->ijv", collected_blocks, collected_blocks, preferred_element_type=jnp.float32
    )
    new_left = 0.9 * factor_left[0] + 0.1 / block_size * left_gram_matrix
    new_right = 0.9 * factor_right[0] + 0.1 / block_size * right_gram_matrix
    preconditioned_update = jnp.einsum(
        "ivp,ips->ivs", left_inverse_roots[0], collected_blocks, preferred_element_type=jnp.float32
    ).astype(jnp.bfloat16)
    product = jnp.einsum(
        "ivp,ips->ivs",
        preconditioned_update,
        right_inverse_roots[0],
        preferred_element_type=jnp.float32,
    ).astype(jnp.bfloat16)
    by_rows = jnp.einsum(
        "ti,tab->iab", slot_rows, product, preferred_element_type=jnp.float32
    ).astype(jnp.bfloat16)
    return (new_left[None], new_right[None], by_rows)


def body(grads, owner_map, factor_left, factor_right, left_inverse_roots, right_inverse_roots):
    num_replicas = lax.axis_size("replica")
    num_shards = lax.axis_size("shard")
    replica_at = lax.axis_index("replica")
    shard_at = lax.axis_index("shard")
    strip_rows = grads.shape[1]
    columns = grads.shape[2]
    capacity = factor_left.shape[1]
    block_size = factor_left.shape[2]
    block_rows = owner_map.shape[0]
    block_cols = owner_map.shape[1]
    per_group = block_cols // num_replicas
    row_index = shard_at * strip_rows // block_size
    row_entries = lax.dynamic_index_in_dim(owner_map, row_index, 0, keepdims=False)
    group_entries = lax.dynamic_slice_in_dim(owner_map, replica_at * per_group, per_group, 1)
    targets = shard_at * capacity + jnp.arange(capacity, dtype=jnp.int32)
    slot_rows = jnp.sum(
        (group_entries[None, :, :] == targets[:, None, None]).astype(jnp.float32), axis=2
    ).astype(jnp.bfloat16)
    pieces = grads[0].reshape(strip_rows, block_cols, block_size).transpose(1, 0, 2)
    column_ids = jnp.arange(block_cols, dtype=jnp.int32)
    owner_dev = column_ids // per_group * num_shards + row_entries // capacity
    device_ids = jnp.arange(num_replicas * num_shards, dtype=jnp.int32)
    destination = (owner_dev[None, :] == device_ids[:, None]).astype(jnp.bfloat16)
    outgoing = jnp.einsum(
        "dk,kab->dab", destination, pieces, preferred_element_type=jnp.float32
    ).astype(jnp.bfloat16)
    incoming = lax.all_to_all(
        outgoing, ("replica", "shard"), split_axis=0, concat_axis=0, tiled=True
    )
    summed = jnp.sum(
        incoming.reshape(num_replicas, num_shards, strip_rows, block_size),
        axis=0,
        dtype=jnp.float32,
    )
    row_blocks = summed.astype(jnp.bfloat16).reshape(block_rows, block_size, block_size)
    new_left, new_right, by_rows = precondition(
        row_blocks, slot_rows, factor_left, factor_right, left_inverse_roots, right_inverse_roots
    )
    tiled = jnp.broadcast_to(
        by_rows.reshape(1, num_shards, strip_rows, block_size),
        (num_replicas, num_shards, strip_rows, block_size),
    )
    returned = lax.all_to_all(
        tiled.reshape(num_replicas * num_shards, strip_rows, block_size),
        ("replica", "shard"),
        split_axis=0,
        concat_axis=0,
        tiled=True,
    )
    own_pieces = jnp.einsum(
        "dk,dab->kab", destination, returned, preferred_element_type=jnp.float32
    ).astype(jnp.bfloat16)
    update = own_pieces.transpose(1, 0, 2).reshape(strip_rows, columns)
    return (new_left, new_right, update)


def solution(mesh):
    in_specs = (
        P("replica", "shard", None),
        P(),
        P(("replica", "shard"), None, None, None),
        P(("replica", "shard"), None, None, None),
        P(("replica", "shard"), None, None, None),
        P(("replica", "shard"), None, None, None),
    )
    out_specs = (
        P(("replica", "shard"), None, None, None),
        P(("replica", "shard"), None, None, None),
        P("shard", None),
    )
    return jax.shard_map(body, mesh=mesh, in_specs=in_specs, out_specs=out_specs, check_vma=False)
```

profile of v0, /device:TPU:0, one launch (start us, length us, event | category | flops | bytes accessed | tf_op | source)
XLA Modules:
  0.0 283.9 jit_solution(17241799139106609699)
XLA Ops:
  0.6 0.0 copy-start
  0.7 0.0 copy-start.4
  0.7 5.4 %copy.68 = bf16[8,8,56,512]{3,2,1,0:T(8,128)(2,1)} copy(bf16[8,8,56,512]{3,1,2,0:T(8,128)(2,1)} %bitcast.49) | data formatting | bytes 7340032
  6.1 0.0 copy-done.4
  6.1 7.7 %convolution_convert_fusion = bf16[128,64,512]{2,0,1:T(8,128)(2,1)} fusion(bf16[64,56,512]{2,1,0:T(8,128)(2,1)} %bitcast.46, s32[56]{0:T(128)S(1)} %fusion.28), kind=kOutput, calls=%fused_computation.2 | convolution fusion | flops 473963520 | bytes 12058848 | tf_op jit(solution)/shard_map/dk,kab->dab/dot_general | solution.py:61
  13.8 11.3 %copy.50 = bf16[128,64,512]{2,1,0:T(8,128)(2,1)} copy(bf16[128,64,512]{2,0,1:T(8,128)(2,1)} %convolution_convert_fusion) | data formatting | bytes 16777216 | tf_op jit(solution)/shard_map/convert_element_type | solution.py:63
  25.1 11.9 %all-to-all-start = ((bf16[128,64,512]{2,1,0:T(8,128)(2,1)}), bf16[128,64,512]{2,1,0:T(8,128)(2,1)}, u32[]{:S(2)}, u32[]{:S(2)}) async-start(bf16[128,64,512]{2,1,0:T(8,128)(2,1)} %copy.50), calls=%async_computation | async-start | bytes 16777216 | tf_op jit(solution)/shard_map/all_to_all | solution.py:64
  37.0 0.1 constant_dynamic-slice_fusion
  37.1 0.2 convert_reduce_fusion
  37.2 97.7 %all-to-all-done = bf16[128,64,512]{2,1,0:T(8,128)(2,1)} async-done(((bf16[128,64,512]{2,1,0:T(8,128)(2,1)}), bf16[128,64,512]{2,1,0:T(8,128)(2,1)}, u32[]{:S(2)}, u32[]{:S(2)}) %all-to-all-start) | async-done | bytes 8388640 | tf_op jit(solution)/shard_map/all_to_all | solution.py:64
  134.9 6.9 %reduce_sum.22 = bf16[32,64,512]{2,1,0:T(8,128)(2,1)} reduce(bf16[4,32,64,512]{3,2,1,0:T(8,128)(2,1)} %bitcast.5, bf16[]{:T(256)} %constant.57.clone.1), dimensions={0}, to_apply=%region_1.2 | reduce | flops 3145728 | bytes 10485762 | tf_op jit(solution)/shard_map/reduce_sum | solution.py:67
  141.8 0.0 copy-start.5
  141.8 4.7 %fusion.10 = bf16[3,512,512]{2,0,1:T(4,128)(2,1)} fusion(bf16[4,512,512]{2,1,0:T(8,128)(2,1)} %bitcast.51, bf16[3,4]{1,0:T(4,128)(2,1)S(1)} %convert_reduce_fusion), kind=kOutput, calls=%fused_computation.12 | convolution fusion | flops 6291456 | bytes 3670040 | tf_op jit(solution)/shard_map/ti,iab->tab/dot_general | solution.py:11
  146.5 0.0 copy-done
  146.5 0.0 copy-done.5
  146.6 4.9 %convolution_convert_fusion.1 = bf16[3,512,512]{2,1,0:T(8,128)(2,1)} fusion(bf16[1,3,512,512]{3,2,1,0:T(8,128)(2,1)S(1)} %copy-done, bf16[1,3,512,512]{3,2,1,0:T(8,128)(2,1)S(1)} %copy-done.5, bf16[3,512,512]{2,0,1:T(4,128)(2,1)} %fusion.10), kind=kOutput, calls=%fused_computation.15 | convolution fusion | flops 1612185600 | bytes 6291456 | tf_op jit(solution)/shard_map/ivp,ips->ivs/dot_general | solution.py:25
  151.5 3.5 %fusion.12 = bf16[4,512,512]{2,0,1:T(4,128)(2,1)S(1)} fusion(bf16[3,512,512]{2,1,0:T(8,128)(2,1)} %convolution_convert_fusion.1, bf16[3,4]{1,0:T(4,128)(2,1)S(1)} %convert_reduce_fusion), kind=kOutput, calls=%fused_computation.14 | convolution fusion | flops 7340032 | bytes 3670040 | tf_op jit(solution)/shard_map/ti,tab->iab/dot_general | solution.py:31
  154.9 0.4 copy.60
  155.3 4.4 %broadcast_in_dim.20 = bf16[4,32,64,512]{3,2,1,0:T(8,128)(2,1)} broadcast(bf16[32,64,512]{2,1,0:T(8,128)(2,1)S(1)} %bitcast.48), dimensions={1,2,3} | broadcast | bytes 10485760 | tf_op jit(solution)/shard_map/broadcast_in_dim | solution.py:76
  159.8 9.7 %all-to-all-start.1 = ((bf16[128,64,512]{2,1,0:T(8,128)(2,1)}), bf16[128,64,512]{2,1,0:T(8,128)(2,1)}, u32[]{:S(2)}, u32[]{:S(2)}) async-start(bf16[128,64,512]{2,1,0:T(8,128)(2,1)} %bitcast.45), calls=%async_computation.1 | async-start | bytes 16777216 | tf_op jit(solution)/shard_map/all_to_all | solution.py:80
  169.5 0.0 copy-start.2
  169.5 0.0 copy-start.3
  169.5 6.5 %fusion.3 = f32[1,3,512,512]{3,2,1,0:T(8,128)} fusion(f32[1,3,512,512]{3,2,1,0:T(8,128)} %param.9, bf16[3,512,512]{2,0,1:T(4,128)(2,1)} %fusion.10), kind=kOutput, calls=%fused_computation.5 | convolution fusion | flops 807665664 | bytes 7864320 | tf_op jit(solution)/shard_map/iyj,iyv->ijv/dot_general | solution.py:17
  176.0 0.0 copy-done.2
  176.0 0.0 copy-done.3
  176.0 3.0 %fusion.4 = f32[1,3,512,512]{3,2,1,0:T(8,128)} fusion(f32[1,3,512,512]{3,2,1,0:T(8,128)S(1)} %copy-done.3, bf16[3,512,512]{2,0,1:T(4,128)(2,1)S(1)} %copy-done.2), kind=kOutput, calls=%fused_computation.7 | convolution fusion | flops 807665664 | bytes 7864320 | tf_op jit(solution)/shard_map/zqw,zfw->zqf/dot_general | solution.py:14
  179.1 88.4 %all-to-all-done.1 = bf16[128,64,512]{2,1,0:T(8,128)(2,1)} async-done(((bf16[128,64,512]{2,1,0:T(8,128)(2,1)}), bf16[128,64,512]{2,1,0:T(8,128)(2,1)}, u32[]{:S(2)}, u32[]{:S(2)}) %all-to-all-start.1) | async-done | bytes 8388640 | tf_op jit(solution)/shard_map/all_to_all | solution.py:80
  267.4 13.1 %fusion.5 = bf16[56,64,512]{2,0,1:T(8,128)(2,1)S(1)} fusion(bf16[128,64,512]{2,1,0:T(8,128)(2,1)} %all-to-all-done.1, s32[56]{0:T(128)S(1)} %fusion.28), kind=kOutput, calls=%fused_computation.9 | convolution fusion | flops 471604224 | bytes 12058848 | tf_op jit(solution)/shard_map/dk,dab->kab/dot_general | solution.py:87
  280.6 0.0 copy-start.1
  280.6 3.3 %copy.69 = bf16[8,8,56,512]{3,1,2,0:T(8,128)(2,1)} copy(bf16[8,8,56,512]{3,2,1,0:T(8,128)(2,1)S(1)} %bitcast.47) | data formatting | bytes 7340032
  283.9 0.0 copy-done.1
  (2 shorter events, 0.0 us)
Async XLA Ops:
  0.6 145.9 %copy-start = (bf16[1,3,512,512]{3,2,1,0:T(8,128)(2,1)S(1)}, bf16[1,3,512,512]{3,2,1,0:T(8,128)(2,1)}, u32[]{:S(2)}) copy-start(bf16[1,3,512,512]{3,2,1,0:T(8,128)(2,1)} %param.11) | copy-start | bytes 4718596
  0.7 5.4 %copy-start.4 = (s32[4,56]{1,0:T(4,128)S(1)}, s32[4,56]{1,0:T(4,128)}, u32[]{:S(2)}) copy-start(s32[4,56]{1,0:T(4,128)} %param.7) | copy-start | bytes 2692
  25.1 109.8 %all-to-all-start = ((bf16[128,64,512]{2,1,0:T(8,128)(2,1)}), bf16[128,64,512]{2,1,0:T(8,128)(2,1)}, u32[]{:S(2)}, u32[]{:S(2)}) async-start(bf16[128,64,512]{2,1,0:T(8,128)(2,1)} %copy.50), calls=%async_computation | async-start | bytes 16777216 | tf_op jit(solution)/shard_map/all_to_all | solution.py:64
  141.8 4.7 %copy-start.5 = (bf16[1,3,512,512]{3,2,1,0:T(8,128)(2,1)S(1)}, bf16[1,3,512,512]{3,2,1,0:T(8,128)(2,1)}, u32[]{:S(2)}) copy-start(bf16[1,3,512,512]{3,2,1,0:T(8,128)(2,1)} %param.10) | copy-start | bytes 4718596
  159.8 107.6 %all-to-all-start.1 = ((bf16[128,64,512]{2,1,0:T(8,128)(2,1)}), bf16[128,64,512]{2,1,0:T(8,128)(2,1)}, u32[]{:S(2)}, u32[]{:S(2)}) async-start(bf16[128,64,512]{2,1,0:T(8,128)(2,1)} %bitcast.45), calls=%async_computation.1 | async-start | bytes 16777216 | tf_op jit(solution)/shard_map/all_to_all | solution.py:80
  169.5 6.6 %copy-start.2 = (bf16[3,512,512]{2,0,1:T(4,128)(2,1)S(1)}, bf16[3,512,512]{2,0,1:T(4,128)(2,1)}, u32[]{:S(2)}) copy-start(bf16[3,512,512]{2,0,1:T(4,128)(2,1)} %fusion.10) | copy-start | bytes 4718596
  169.5 6.5 %copy-start.3 = (f32[1,3,512,512]{3,2,1,0:T(8,128)S(1)}, f32[1,3,512,512]{3,2,1,0:T(8,128)}, u32[]{:S(2)}) copy-start(f32[1,3,512,512]{3,2,1,0:T(8,128)} %param.8) | copy-start | bytes 9437188
  280.6 3.3 %copy-start.1 = (bf16[1,3,512,512]{3,2,1,0:T(8,128)(2,1)S(1)}, bf16[1,3,512,512]{3,2,1,0:T(8,128)(2,1)}, u32[]{:S(2)}) copy-start(bf16[1,3,512,512]{3,2,1,0:T(8,128)(2,1)} %param.11) | copy-start | bytes 4718596
where the time goes:
time: 285 us; the launch traced here: 284 us
  waiting for transfers between devices  186 us (65%)
  matrix products  43.5 us (15%)
  local copies, waits for them, and re-layouts  24.9 us (9%)
  starting transfers between devices  21.5 us (8%)
  other arithmetic  7.08 us (2%)
    all_to_all x1, waiting for transfers between devices, body(): lax.all_to_all(outgoing, ('replica', 'shard'), split_axis=0, concat_axis=...  97.7 us
    all_to_all x1, waiting for transfers between devices, body(): lax.all_to_all(tiled.reshape(num_replicas * num_shards, strip_rows, block...  88.4 us
    dot_general x1, matrix products, body(): jnp.einsum('dk,dab->kab', destination, returned, preferred_element_type=j...  13.1 us
    all_to_all x1, starting transfers between devices, body(): lax.all_to_all(outgoing, ('replica', 'shard'), split_axis=0, concat_axis=...  11.9 us
    convert_element_type x1, local copies, waits for them, and re-layouts, body(): outgoing = jnp.einsum('dk,kab->dab', destination, pieces, preferred_eleme...  11.3 us
    all_to_all x1, starting transfers between devices, body(): lax.all_to_all(tiled.reshape(num_replicas * num_shards, strip_rows, block...  9.69 us
    unnamed x14, local copies, waits for them, and re-layouts  8.68 us
    dot_general x1, matrix products, body(): jnp.einsum('dk,kab->dab', destination, pieces, preferred_element_type=jnp...  7.7 us
  transfers between devices with their start and end apart: 2, of which 2 were waited for; matrix products, arithmetic and copies ran while one was open for 3% of the time, Pallas kernels for 0%

commit v1 on v0

v1 whole, which is shorter than its diff:
```python
import functools

import jax
import jax.numpy as jnp
from jax import lax
from jax.experimental import pallas as pl
from jax.experimental.pallas import tpu as pltpu
from jax.sharding import PartitionSpec as P

FORWARD = (64,)
BACKWARD = (64,)


def offsets(parts):
    return [sum(parts[:at]) for at in range(len(parts))]


def any_spec():
    return pl.BlockSpec(memory_space=pl.ANY)


def vmem_spec():
    return pl.BlockSpec(memory_space=pltpu.VMEM)


def params():
    return pltpu.CompilerParams(vmem_limit_bytes=48 * 1024 * 1024)


def slot_kernel(block_size, owners, own, left, right, out, held, sems):
    count = held.shape[0]
    copies = []
    for at in range(count):
        columns = slice(at * block_size, (at + 1) * block_size)
        total = (
            own[:, columns].astype(jnp.float32)
            + left[:, columns].astype(jnp.float32)
            + right[:, columns].astype(jnp.float32)
        )
        held[at] = total.astype(jnp.bfloat16)
        copy = pltpu.make_async_copy(held.at[at], out.at[owners[at]], sems.at[at])
        copy.start()
        copies.append(copy)
    for copy in copies:
        copy.wait()


def to_slots(owners, own, left, right, num_shards, block_size):
    rows, columns = own.shape
    count = columns // block_size
    return pl.pallas_call(
        functools.partial(slot_kernel, block_size),
        out_shape=jax.ShapeDtypeStruct((num_shards, rows, block_size), jnp.bfloat16),
        in_specs=[pl.BlockSpec(memory_space=pltpu.SMEM)] + [vmem_spec()] * 3,
        out_specs=any_spec(),
        scratch_shapes=[
            pltpu.VMEM((count, rows, block_size), jnp.bfloat16),
            pltpu.SemaphoreType.DMA((count,)),
        ],
        compiler_params=params(),
        cost_estimate=pl.CostEstimate(
            flops=3 * rows * columns, bytes_accessed=8 * rows * columns, transcendentals=0
        ),
        name="to_slots",
    )(owners, own, left, right)


def whole_block(parts):
    joined = jnp.concatenate([part[0] for part in parts], axis=1)
    return joined.reshape(joined.shape[0] * joined.shape[1], joined.shape[2])


def update_kernel(num_parts, bounds, rows_of, *refs):
    parts = refs[:num_parts]
    left_root, right_root = refs[num_parts], refs[num_parts + 1]
    outs = refs[num_parts + 2 :]
    block = whole_block(parts)
    applied = jnp.dot(left_root[0], block, preferred_element_type=jnp.float32).astype(jnp.bfloat16)
    product = jnp.dot(applied, right_root[0], preferred_element_type=jnp.float32).astype(jnp.bfloat16)
    product = product.reshape(parts[0].shape[1], -1, product.shape[1])
    for out, (start, rows) in zip(outs, bounds, strict=True):
        out[0] = product[:, start : start + rows]


def updates(rows_of, parts, left_roots, right_roots, back):
    capacity, block_size = left_roots.shape[0], left_roots.shape[1]
    block_rows, strips = parts[0].shape[:2]
    bounds = list(zip(offsets(back), back, strict=True))
    at_row = lambda t, rows_of: (rows_of[t], 0, 0, 0)
    root = pl.BlockSpec((1, block_size, block_size), lambda t, rows_of: (t, 0, 0))
    return pl.pallas_call(
        functools.partial(update_kernel, len(parts), bounds),
        grid_spec=pltpu.PrefetchScalarGridSpec(
            num_scalar_prefetch=1,
            grid=(capacity,),
            in_specs=[pl.BlockSpec((1,) + part.shape[1:], at_row) for part in parts] + [root, root],
            out_specs=[pl.BlockSpec((1, strips, rows, block_size), at_row) for rows in back],
        ),
        out_shape=[
            jax.ShapeDtypeStruct((block_rows, strips, rows, block_size), jnp.bfloat16)
            for rows in back
        ],
        compiler_params=params(),
        cost_estimate=pl.CostEstimate(
            flops=4 * capacity * block_size**3,
            bytes_accessed=8 * capacity * block_size**2,
            transcendentals=0,
        ),
        name="updates",
    )(rows_of, *parts, left_roots, right_roots)


def gram_kernel(num_parts, rows_of, named, *refs):
    parts = refs[:num_parts]
    left, right, new_left, new_right = refs[num_parts:]
    block = whole_block(parts)
    size = block.shape[0]
    holds = named[pl.program_id(0)] > 0
    scale = 0.1 / size
    gram = lax.dot_general(block, block, (((1,), (1,)), ((), ())), preferred_element_type=jnp.float32)
    new_left[0] = 0.9 * left[0] + jnp.where(holds, scale * gram, 0.0)
    gram = lax.dot_general(block, block, (((0,), (0,)), ((), ())), preferred_element_type=jnp.float32)
    new_right[0] = 0.9 * right[0] + jnp.where(holds, scale * gram, 0.0)


def statistics(rows_of, named, parts, factor_left, factor_right):
    capacity, block_size = factor_left.shape[0], factor_left.shape[1]
    at_row = lambda t, rows_of, named: (rows_of[t], 0, 0, 0)
    square = pl.BlockSpec((1, block_size, block_size), lambda t, rows_of, named: (t, 0, 0))
    return pl.pallas_call(
        functools.partial(gram_kernel, len(parts)),
        grid_spec=pltpu.PrefetchScalarGridSpec(
            num_scalar_prefetch=2,
            grid=(capacity,),
            in_specs=[pl.BlockSpec((1,) + part.shape[1:], at_row) for part in parts]
            + [square, square],
            out_specs=[square, square],
        ),
        out_shape=[jax.ShapeDtypeStruct(factor_left.shape, jnp.float32)] * 2,
        compiler_params=params(),
        cost_estimate=pl.CostEstimate(
            flops=4 * capacity * block_size**3,
            bytes_accessed=18 * capacity * block_size**2,
            transcendentals=0,
        ),
        name="statistics",
    )(rows_of, named, *parts, factor_left, factor_right)


def pick_kernel(block_size, count, owners, slots, out, sems):
    copies = []
    for at in range(count):
        columns = pl.ds(at * block_size, block_size)
        copy = pltpu.make_async_copy(slots.at[owners[at]], out.at[:, columns], sems.at[at])
        copy.start()
        copies.append(copy)
    for copy in copies:
        copy.wait()


def from_slots(owners, slots):
    count = owners.shape[0]
    _, rows, block_size = slots.shape
    return pl.pallas_call(
        functools.partial(pick_kernel, block_size, count),
        out_shape=jax.ShapeDtypeStruct((rows, count * block_size), jnp.bfloat16),
        in_specs=[pl.BlockSpec(memory_space=pltpu.SMEM), any_spec()],
        out_specs=any_spec(),
        scratch_shapes=[pltpu.SemaphoreType.DMA((count,))],
        compiler_params=params(),
        cost_estimate=pl.CostEstimate(
            flops=0, bytes_accessed=4 * rows * count * block_size, transcendentals=0
        ),
        name="from_slots",
    )(owners, slots)


def place_kernel(start, groups, own, left, right, far_left, far_right, *rest):
    out, sems = rest[-2:]
    rows, width = own.shape
    half = far_left.shape[1]
    copies = []
    for at, (piece, group, shift) in enumerate(
        ((own, 0, 0), (left, 1, 0), (right, 2, 0), (far_left, 3, 0), (far_right, 3, half))
    ):
        first = pl.multiple_of(groups[group] * width + shift, 128)
        copy = pltpu.make_async_copy(
            piece, out.at[pl.ds(start, rows), pl.ds(first, piece.shape[1])], sems.at[at]
        )
        copy.start()
        copies.append(copy)
    for copy in copies:
        copy.wait()


def place(groups, pieces, start, shape, held):
    given = () if held is None else (held,)
    return pl.pallas_call(
        functools.partial(place_kernel, start),
        out_shape=jax.ShapeDtypeStruct(shape, jnp.bfloat16),
        in_specs=[pl.BlockSpec(memory_space=pltpu.SMEM)] + [any_spec()] * (5 + len(given)),
        out_specs=any_spec(),
        scratch_shapes=[pltpu.SemaphoreType.DMA((5,))],
        input_output_aliases={} if held is None else {6: 0},
        compiler_params=params(),
        cost_estimate=pl.CostEstimate(
            flops=0, bytes_accessed=4 * pieces[0].shape[0] * shape[1], transcendentals=0
        ),
        name="place",
    )(groups, *pieces, *given)


def body(grads, owner_map, factor_left, factor_right, left_inverse_roots, right_inverse_roots):
    num_replicas = lax.axis_size("replica")
    num_shards = lax.axis_size("shard")
    replica_at = lax.axis_index("replica")
    shard_at = lax.axis_index("shard")
    strip_rows, columns = grads.shape[1], grads.shape[2]
    capacity, block_size = factor_left.shape[1], factor_left.shape[2]
    block_rows, block_cols = owner_map.shape
    per_group = block_cols // num_replicas
    width = per_group * block_size
    strips = block_size // strip_rows
    onward = [(at, (at + 1) % num_replicas) for at in range(num_replicas)]
    back = [(at, (at - 1) % num_replicas) for at in range(num_replicas)]
    to_right = lambda a: lax.ppermute(a, "replica", onward)
    to_left = lambda a: lax.ppermute(a, "replica", back)
    right_at = (replica_at + 1) % num_replicas
    left_at = (replica_at + num_replicas - 1) % num_replicas
    far_at = (replica_at + 2) % num_replicas

    group_entries = lax.dynamic_slice_in_dim(owner_map, replica_at * per_group, per_group, 1)
    row_entries = lax.dynamic_index_in_dim(group_entries, shard_at // strips, 0, keepdims=False)
    owners = row_entries // capacity
    targets = shard_at * capacity + jnp.arange(capacity, dtype=jnp.int32)
    match = jnp.any(group_entries[None] == targets[:, None, None], axis=2)
    named = jnp.any(match, axis=1)
    unused = jnp.logical_not(jnp.any(match, axis=0))
    rank_slot = jnp.cumsum(jnp.logical_not(named).astype(jnp.int32))
    rank_row = jnp.cumsum(unused.astype(jnp.int32))
    spare = jnp.logical_and(
        jnp.logical_and(jnp.logical_not(named)[:, None], unused[None]),
        rank_slot[:, None] == rank_row[None],
    )
    chosen = jnp.logical_or(match, spare)
    rows_of = jnp.sum(
        jnp.where(chosen, jnp.arange(block_rows, dtype=jnp.int32)[None], 0), axis=1
    ).astype(jnp.int32)
    named = named.astype(jnp.int32)

    tile = 8
    view = grads[0].reshape(strip_rows // tile, tile, num_replicas, width).transpose(0, 2, 1, 3)

    def piece(group, start, rows):
        part = lax.dynamic_slice(
            view, (start // tile, group, 0, 0), (rows // tile, 1, tile, width)
        )
        return part.reshape(rows, width)

    arrived = []
    for start, rows in zip(offsets(FORWARD), FORWARD, strict=True):
        half = rows // 2
        passed_right = to_right(piece(far_at, start, half))
        passed_left = to_left(piece(far_at, start + half, half))
        ahead = piece(right_at, start, rows)
        behind = piece(left_at, start, rows)
        add = lambda a, b: (a.astype(jnp.float32) + b.astype(jnp.float32)).astype(jnp.bfloat16)
        from_left = to_right(jnp.concatenate([add(ahead[:half], passed_right), ahead[half:]]))
        from_right = to_left(jnp.concatenate([behind[:half], add(behind[half:], passed_left)]))
        slots = to_slots(
            owners, piece(replica_at, start, rows), from_left, from_right, num_shards, block_size
        )
        came = lax.all_to_all(slots, "shard", split_axis=0, concat_axis=0, tiled=True)
        arrived.append(came.reshape(block_rows, strips, rows, block_size))

    outs = updates(rows_of, arrived, left_inverse_roots[0], right_inverse_roots[0], BACKWARD)
    new_left, new_right = statistics(rows_of, named, arrived, factor_left[0], factor_right[0])

    update = None
    groups = jnp.stack([replica_at, left_at, right_at, far_at]).astype(jnp.int32)
    for start, out in zip(offsets(BACKWARD), outs, strict=True):
        rows = out.shape[2]
        came = lax.all_to_all(
            out.reshape(num_shards, rows, block_size),
            "shard",
            split_axis=0,
            concat_axis=0,
            tiled=True,
        )
        own = from_slots(owners, came)
        from_left, from_right = to_right(own), to_left(own)
        far_left = to_right(from_left[:, : width // 2])
        far_right = to_left(from_right[:, width // 2 :])
        update = place(
            groups,
            (own, from_left, from_right, far_left, far_right),
            start,
            (strip_rows, columns),
            update,
        )
    return (new_left[None], new_right[None], update)


def solution(mesh):
    in_specs = (
        P("replica", "shard", None),
        P(),
        P(("replica", "shard"), None, None, None),
        P(("replica", "shard"), None, None, None),
        P(("replica", "shard"), None, None, None),
        P(("replica", "shard"), None, None, None),
    )
    out_specs = (
        P(("replica", "shard"), None, None, None),
        P(("replica", "shard"), None, None, None),
        P("shard", None),
    )
    return jax.shard_map(body, mesh=mesh, in_specs=in_specs, out_specs=out_specs, check_vma=False)
```

time: 285 us -> 165 us (0.58)
  waiting for transfers between devices: 186 us -> 82.8 us
  matrix products: 43.5 us -> 0 us
  blocking collectives: 0 us -> 31.3 us
  local copies, waits for them, and re-layouts: 24.9 us -> 8.4 us
  Pallas kernels: 0 us -> 16.2 us
  other arithmetic: 7.08 us -> 2.5 us
    all_to_all x2 -> x1, waiting for transfers between devices: 186 us -> 28 us  [body(): lax.all_to_all(slots, 'shard', split_axis=0, concat_axis=0, tiled=True)]
    ppermute x0 -> x8, waiting for transfers between devices: none -> 54.8 us  [the longest x4 32 us: body(): to_right = lambda a: lax.ppermute(a, 'replica', onward)]
    dot_general x7 -> x0, matrix products: 43.5 us -> none  [the longest x1 13.1 us: body(): jnp.einsum('dk,dab->kab', destination, returned, preferred_element_type=j...]
    all_to_all x0 -> x1, blocking collectives: none -> 31.3 us  [body(): lax.all_to_all(out.reshape(num_shards, rows, block_size), 'shard', split_...]
    pallas_call x0 -> x5, Pallas kernels: none -> 16.2 us  [the longest x1 6.61 us: statistics(): pl.pallas_call(functools.partial(gram_kernel, len(parts)), grid_spec=pltp...]
    ppermute x0 -> x8, starting transfers between devices: none -> 14.6 us  [the longest x4 11.2 us: body(): to_left = lambda a: lax.ppermute(a, 'replica', back)]
    all_to_all x2 -> x1, starting transfers between devices: 21.5 us -> 7.32 us  [body(): lax.all_to_all(slots, 'shard', split_axis=0, concat_axis=0, tiled=True)]
    convert_element_type x2 -> x0, local copies, waits for them, and re-layouts: 11.7 us -> none  [the longest x1 11.3 us: body(): outgoing = jnp.einsum('dk,kab->dab', destination, pieces, preferred_eleme...]
  transfers between devices with their start and end apart: 2 -> 9, of which waited for: 2 -> 6; matrix products, arithmetic and copies ran while one was open for 3% -> 1% of each run, Pallas kernels for 0% -> 4%
where the time goes in v1:
time: 165 us; the launch traced here: 164 us
  waiting for transfers between devices  82.8 us (50%)
  blocking collectives  31.3 us (19%)
  starting transfers between devices  22 us (13%)
  Pallas kernels  16.2 us (10%)
  local copies, waits for them, and re-layouts  8.4 us (5%)
  other arithmetic  2.5 us (2%)
    ppermute x4, waiting for transfers between devices, body(): to_right = lambda a: lax.ppermute(a, 'replica', onward)  32 us
    all_to_all x1, blocking collectives, body(): lax.all_to_all(out.reshape(num_shards, rows, block_size), 'shard', split_...  31.3 us
    all_to_all x1, waiting for transfers between devices, body(): lax.all_to_all(slots, 'shard', split_axis=0, concat_axis=0, tiled=True)  28 us
    ppermute x4, waiting for transfers between devices, body(): to_left = lambda a: lax.ppermute(a, 'replica', back)  22.8 us
    ppermute x4, starting transfers between devices, body(): to_left = lambda a: lax.ppermute(a, 'replica', back)  11.2 us
    all_to_all x1, starting transfers between devices, body(): lax.all_to_all(slots, 'shard', split_axis=0, concat_axis=0, tiled=True)  7.32 us
    pallas_call x1, Pallas kernels, statistics(): pl.pallas_call(functools.partial(gram_kernel, len(parts)), grid_spec=pltp...  6.61 us
    unnamed x14, local copies, waits for them, and re-layouts  5.46 us
  transfers between devices with their start and end apart: 9, of which 6 were waited for; matrix products, arithmetic and copies ran while one was open for 1% of the time, Pallas kernels for 4%

profile of v1, /device:TPU:0, one launch (start us, length us, event | category | flops | bytes accessed | tf_op | source)
XLA Modules:
  0.0 164.0 jit_solution(15248680165161367811)
XLA Ops:
  0.7 1.6 dynamic-slice_bitcast_fusion.2
  2.2 2.1 %collective-permute-start = (bf16[32,7168]{1,0:T(8,128)(2,1)S(1)}, bf16[32,7168]{1,0:T(8,128)(2,1)S(1)}, u32[]{:S(2)}, u32[]{:S(2)}) collective-permute-start(bf16[32,7168]{1,0:T(8,128)(2,1)S(1)} %get-tuple-element.11), channel_id=1, source_target_pairs={{0,32},{32,64},{64,96},{96,0},{1,33},{33,65},{65,97},{97,1},{2,34}... | collective-permute-start | bytes 1376264 | tf_op jit(solution)/shard_map/ppermute | solution.py:226
  4.3 2.2 %collective-permute-start.2 = (bf16[32,7168]{1,0:T(8,128)(2,1)S(1)}, bf16[32,7168]{1,0:T(8,128)(2,1)S(1)}, u32[]{:S(2)}, u32[]{:S(2)}) collective-permute-start(bf16[32,7168]{1,0:T(8,128)(2,1)S(1)} %get-tuple-element.13), channel_id=1, source_target_pairs={{0,96},{32,0},{64,32},{96,64},{1,97},{33,1},{65,33},{97,65},{2,98}... | collective-permute-start | bytes 1376264 | tf_op jit(solution)/shard_map/ppermute | solution.py:227
  6.5 10.4 %collective-permute-done = bf16[32,7168]{1,0:T(8,128)(2,1)S(1)} collective-permute-done((bf16[32,7168]{1,0:T(8,128)(2,1)S(1)}, bf16[32,7168]{1,0:T(8,128)(2,1)S(1)}, u32[]{:S(2)}, u32[]{:S(2)}) %collective-permute-start) | collective-permute-done | bytes 458784 | tf_op jit(solution)/shard_map/ppermute | solution.py:226
  17.0 1.4 fusion
  18.4 1.3 collective-permute-start.1
  19.8 2.1 %collective-permute-start.3 = (bf16[64,7168]{1,0:T(8,128)(2,1)S(1)}, bf16[64,7168]{1,0:T(8,128)(2,1)S(1)}, u32[]{:S(2)}, u32[]{:S(2)}) collective-permute-start(bf16[64,7168]{1,0:T(8,128)(2,1)S(1)} %pad_maximum_fusion.1), channel_id=1, source_target_pairs={{0,96},{32,0},{64,32},{96,64},{1,97},{33,1},{65,33},{97,65},{2,98}... | collective-permute-start | bytes 2752520 | tf_op jit(solution)/shard_map/ppermute | solution.py:227
  21.9 0.1 bitcast_select_fusion.owners
  21.9 1.2 dynamic-slice_bitcast_fusion.own
  23.2 18.1 %collective-permute-done.1.left = bf16[64,7168]{1,0:T(8,128)(2,1)S(1)} collective-permute-done((bf16[64,7168]{1,0:T(8,128)(2,1)S(1)}, bf16[64,7168]{1,0:T(8,128)(2,1)S(1)}, u32[]{:S(2)}, u32[]{:S(2)}) %collective-permute-start.1) | collective-permute-done | bytes 917536 | tf_op jit(solution)/shard_map/ppermute | solution.py:226
  41.2 2.2 %to_slots.1 = bf16[32,64,512]{2,1,0:T(8,128)(2,1)S(1)} custom-call(s32[14]{0:T(128)S(1)} %bitcast_select_fusion.owners, bf16[64,7168]{1,0:T(8,128)(2,1)S(1)} %dynamic-slice_bitcast_fusion.own, bf16[64,7168]{1,0:T(8,128)(2,1)S(1)} %collective-permute-done.1.left, bf16[64,7168]{1,0:T(8,128)(2,1)S(1)} %collective-permute-done.3.right), custom_call_target="tpu_custom_call" | custom-call | flops 1376256 | bytes 3670016 | tf_op jit(solution)/shard_map/to_slots/pallas_call | solution.py:51
  43.5 1.3 copy-done.2
  44.8 7.3 %all-to-all-start = ((bf16[32,64,512]{2,1,0:T(8,128)(2,1)}), bf16[32,64,512]{2,1,0:T(8,128)(2,1)S(1)}, u32[]{:S(2)}, u32[]{:S(2)}) async-start(bf16[32,64,512]{2,1,0:T(8,128)(2,1)} %copy-done.2), calls=%async_computation | async-start | bytes 4194304 | tf_op jit(solution)/shard_map/all_to_all | solution.py:273
  52.2 0.3 compare_reduce_fusion.1
  52.5 0.2 reduce-window.16
  52.7 0.2 reduce-window.17
  52.9 0.2 select_reduce_fusion.rows_of
  53.1 28.0 %all-to-all-done = bf16[32,64,512]{2,1,0:T(8,128)(2,1)S(1)} async-done(((bf16[32,64,512]{2,1,0:T(8,128)(2,1)}), bf16[32,64,512]{2,1,0:T(8,128)(2,1)S(1)}, u32[]{:S(2)}, u32[]{:S(2)}) %all-to-all-start) | async-done | bytes 2097184 | tf_op jit(solution)/shard_map/all_to_all | solution.py:273
  81.0 1.3 copy-done
  82.4 1.4 copy-done.4
  83.8 1.4 copy-done.5
  85.2 4.1 %updates.1 = bf16[4,8,64,512]{3,2,1,0:T(8,128)(2,1)S(1)} custom-call(s32[3]{0:T(128)S(1)} %select_reduce_fusion.rows_of, bf16[4,8,64,512]{3,2,1,0:T(8,128)(2,1)} %bitcast.59, bf16[3,512,512]{2,1,0:T(8,128)(2,1)S(1)} %bitcast.63, bf16[3,512,512]{2,1,0:T(8,128)(2,1)S(1)} %bitcast.64), custom_call_target="tpu_custom_call" | custom-call | flops 1610612736 | bytes 6291456 | tf_op jit(solution)/shard_map/updates/pallas_call | solution.py:91
  89.3 31.3 %all_to_all.10.slots = bf16[32,64,512]{2,1,0:T(8,128)(2,1)S(1)} all-to-all(bf16[32,64,512]{2,1,0:T(8,128)(2,1)S(1)} %bitcast.61), channel_id=1, replica_groups=mesh['replica'=4,'shard'=32] {'shard'}, dimensions={0} | all-to-all | bytes 4194304 | tf_op jit(solution)/shard_map/all_to_all | solution.py:283
  120.6 0.9 from_slots.1.own
  121.5 3.2 %collective-permute-start.5 = (bf16[64,7168]{1,0:T(8,128)(2,1)S(1)}, bf16[64,7168]{1,0:T(8,128)(2,1)S(1)}, u32[]{:S(2)}, u32[]{:S(2)}) collective-permute-start(bf16[64,7168]{1,0:T(8,128)(2,1)S(1)} %from_slots.1.own), channel_id=1, source_target_pairs={{0,96},{32,0},{64,32},{96,64},{1,97},{33,1},{65,33},{97,65},{2,98}... | collective-permute-start | bytes 2752520 | tf_op jit(solution)/shard_map/ppermute | solution.py:227
  124.7 20.1 %collective-permute-done.5.right = bf16[64,7168]{1,0:T(8,128)(2,1)S(1)} collective-permute-done((bf16[64,7168]{1,0:T(8,128)(2,1)S(1)}, bf16[64,7168]{1,0:T(8,128)(2,1)S(1)}, u32[]{:S(2)}, u32[]{:S(2)}) %collective-permute-start.5) | collective-permute-done | bytes 917536 | tf_op jit(solution)/shard_map/ppermute | solution.py:227
  144.8 3.8 %collective-permute-start.7 = (bf16[64,3584]{1,0:T(8,128)(2,1)S(1)}, bf16[64,3584]{1,0:T(8,128)(2,1)S(1)}, u32[]{:S(2)}, u32[]{:S(2)}) collective-permute-start(bf16[64,3584]{1,0:T(8,128)(2,1)S(1)} %slice.39), channel_id=1, source_target_pairs={{0,96},{32,0},{64,32},{96,64},{1,97},{33,1},{65,33},{97,65},{2,98}... | collective-permute-start | bytes 1376264 | tf_op jit(solution)/shard_map/ppermute | solution.py:227
  148.7 0.1 pad_add_fusion.groups
  148.8 6.6 %statistics.1 = (f32[3,512,512]{2,1,0:T(8,128)}, f32[3,512,512]{2,1,0:T(8,128)}) custom-call(s32[3]{0:T(128)S(1)} %select_reduce_fusion.rows_of, s32[3]{0:T(128)S(1)} %get-tuple-element.16.named, bf16[4,8,64,512]{3,2,1,0:T(8,128)(2,1)S(1)} %bitcast.60, f32[3,512,512]{2,1,0:T(8,128)S(1)} %bitcast.62, f32[3,512,512]{2,1,0:T(8,128)} %bitcast.68), custom_call_target="tpu_custom_call" | custom-call | flops 1610612736 | bytes 14155776 | tf_op jit(solution)/shard_map/statistics/pallas_call | solution.py:130
  155.4 2.7 %collective-permute-done.7.far_right = bf16[64,3584]{1,0:T(8,128)(2,1)S(1)} collective-permute-done((bf16[64,3584]{1,0:T(8,128)(2,1)S(1)}, bf16[64,3584]{1,0:T(8,128)(2,1)S(1)}, u32[]{:S(2)}, u32[]{:S(2)}) %collective-permute-start.7) | collective-permute-done | bytes 458784 | tf_op jit(solution)/shard_map/ppermute | solution.py:227
  158.1 3.5 %collective-permute-done.6.far_left = bf16[64,3584]{1,0:T(8,128)(2,1)S(1)} collective-permute-done((bf16[64,3584]{1,0:T(8,128)(2,1)S(1)}, bf16[64,3584]{1,0:T(8,128)(2,1)S(1)}, u32[]{:S(2)}, u32[]{:S(2)}) %collective-permute-start.6) | collective-permute-done | bytes 458784 | tf_op jit(solution)/shard_map/ppermute | solution.py:226
  161.6 2.4 %place.1 = bf16[64,28672]{1,0:T(8,128)(2,1)} custom-call(s32[4]{0:T(128)S(1)} %pad_add_fusion.groups, bf16[64,7168]{1,0:T(8,128)(2,1)S(1)} %from_slots.1.own, bf16[64,7168]{1,0:T(8,128)(2,1)S(1)} %collective-permute-done.4.left, bf16[64,7168]{1,0:T(8,128)(2,1)S(1)} %collective-permute-done.5.right, bf16[64,3584]{1,0:T(8,128)(2,1)S(1)} %collective-permute-done.6.far_left, ...), custom_call_target="tpu_custom_call" | custom-call | bytes 7340032 | tf_op jit(solution)/shard_map/place/pallas_call | solution.py:198
  (23 shorter events, 0.4 us)
Async XLA Ops:
  2.2 14.7 %collective-permute-start = (bf16[32,7168]{1,0:T(8,128)(2,1)S(1)}, bf16[32,7168]{1,0:T(8,128)(2,1)S(1)}, u32[]{:S(2)}, u32[]{:S(2)}) collective-permute-start(bf16[32,7168]{1,0:T(8,128)(2,1)S(1)} %get-tuple-element.11), channel_id=1, source_target_pairs={{0,32},{32,64},{64,96},{96,0},{1,33},{33,65},{65,97},{97,1},{2,34}... | collective-permute-start | bytes 1376264 | tf_op jit(solution)/shard_map/ppermute | solution.py:226
  4.3 12.6 %collective-permute-start.2 = (bf16[32,7168]{1,0:T(8,128)(2,1)S(1)}, bf16[32,7168]{1,0:T(8,128)(2,1)S(1)}, u32[]{:S(2)}, u32[]{:S(2)}) collective-permute-start(bf16[32,7168]{1,0:T(8,128)(2,1)S(1)} %get-tuple-element.13), channel_id=1, source_target_pairs={{0,96},{32,0},{64,32},{96,64},{1,97},{33,1},{65,33},{97,65},{2,98}... | collective-permute-start | bytes 1376264 | tf_op jit(solution)/shard_map/ppermute | solution.py:227
  18.3 3.5 %copy-start.6 = (s32[4,56]{1,0:T(4,128)S(1)}, s32[4,56]{1,0:T(4,128)}, u32[]{:S(2)}) copy-start(s32[4,56]{1,0:T(4,128)} %param.7) | copy-start | bytes 2692
  18.4 22.8 %collective-permute-start.1 = (bf16[64,7168]{1,0:T(8,128)(2,1)S(1)}, bf16[64,7168]{1,0:T(8,128)(2,1)S(1)}, u32[]{:S(2)}, u32[]{:S(2)}) collective-permute-start(bf16[64,7168]{1,0:T(8,128)(2,1)S(1)} %pad_maximum_fusion), channel_id=1, source_target_pairs={{0,32},{32,64},{64,96},{96,0},{1,33},{33,65},{65,97},{97,1},{2,34}... | collective-permute-start | bytes 2752520 | tf_op jit(solution)/shard_map/ppermute | solution.py:226
  19.8 21.4 %collective-permute-start.3 = (bf16[64,7168]{1,0:T(8,128)(2,1)S(1)}, bf16[64,7168]{1,0:T(8,128)(2,1)S(1)}, u32[]{:S(2)}, u32[]{:S(2)}) collective-permute-start(bf16[64,7168]{1,0:T(8,128)(2,1)S(1)} %pad_maximum_fusion.1), channel_id=1, source_target_pairs={{0,96},{32,0},{64,32},{96,64},{1,97},{33,1},{65,33},{97,65},{2,98}... | collective-permute-start | bytes 2752520 | tf_op jit(solution)/shard_map/ppermute | solution.py:227
  43.5 1.3 copy-start.2
  44.8 36.3 %all-to-all-start = ((bf16[32,64,512]{2,1,0:T(8,128)(2,1)}), bf16[32,64,512]{2,1,0:T(8,128)(2,1)S(1)}, u32[]{:S(2)}, u32[]{:S(2)}) async-start(bf16[32,64,512]{2,1,0:T(8,128)(2,1)} %copy-done.2), calls=%async_computation | async-start | bytes 4194304 | tf_op jit(solution)/shard_map/all_to_all | solution.py:273
  81.0 1.3 copy-start
  82.4 1.4 copy-start.4
  83.8 1.4 copy-start.5
  89.3 59.5 %copy-start.3 = (f32[1,3,512,512]{3,2,1,0:T(8,128)S(1)}, f32[1,3,512,512]{3,2,1,0:T(8,128)}, u32[]{:S(2)}) copy-start(f32[1,3,512,512]{3,2,1,0:T(8,128)} %param.8) | copy-start | bytes 9437188
  120.6 28.2 %copy-start.1 = (bf16[32,64,512]{2,1,0:T(8,128)(2,1)S(1)}, bf16[32,64,512]{2,1,0:T(8,128)(2,1)}, u32[]{:S(2)}) copy-start(bf16[32,64,512]{2,1,0:T(8,128)(2,1)} %copy-done) | copy-start | bytes 6291460
  121.5 23.3 %collective-permute-start.5 = (bf16[64,7168]{1,0:T(8,128)(2,1)S(1)}, bf16[64,7168]{1,0:T(8,128)(2,1)S(1)}, u32[]{:S(2)}, u32[]{:S(2)}) collective-permute-start(bf16[64,7168]{1,0:T(8,128)(2,1)S(1)} %from_slots.1.own), channel_id=1, source_target_pairs={{0,96},{32,0},{64,32},{96,64},{1,97},{33,1},{65,33},{97,65},{2,98}... | collective-permute-start | bytes 2752520 | tf_op jit(solution)/shard_map/ppermute | solution.py:227
  124.7 23.9 %collective-permute-start.4 = (bf16[64,7168]{1,0:T(8,128)(2,1)S(1)}, bf16[64,7168]{1,0:T(8,128)(2,1)S(1)}, u32[]{:S(2)}, u32[]{:S(2)}) collective-permute-start(bf16[64,7168]{1,0:T(8,128)(2,1)S(1)} %from_slots.1.own), channel_id=1, source_target_pairs={{0,32},{32,64},{64,96},{96,0},{1,33},{33,65},{65,97},{97,1},{2,34}... | collective-permute-start | bytes 2752520 | tf_op jit(solution)/shard_map/ppermute | solution.py:226
  144.8 13.3 %collective-permute-start.7 = (bf16[64,3584]{1,0:T(8,128)(2,1)S(1)}, bf16[64,3584]{1,0:T(8,128)(2,1)S(1)}, u32[]{:S(2)}, u32[]{:S(2)}) collective-permute-start(bf16[64,3584]{1,0:T(8,128)(2,1)S(1)} %slice.39), channel_id=1, source_target_pairs={{0,96},{32,0},{64,32},{96,64},{1,97},{33,1},{65,33},{97,65},{2,98}... | collective-permute-start | bytes 1376264 | tf_op jit(solution)/shard_map/ppermute | solution.py:227
  148.6 13.0 %collective-permute-start.6 = (bf16[64,3584]{1,0:T(8,128)(2,1)S(1)}, bf16[64,3584]{1,0:T(8,128)(2,1)S(1)}, u32[]{:S(2)}, u32[]{:S(2)}) collective-permute-start(bf16[64,3584]{1,0:T(8,128)(2,1)S(1)} %slice.38), channel_id=1, source_target_pairs={{0,32},{32,64},{64,96},{96,0},{1,33},{33,65},{65,97},{97,1},{2,34}... | collective-permute-start | bytes 1376264 | tf_op jit(solution)/shard_map/ppermute | solution.py:226

commit v2 on v1

--- a/solution.py
+++ b/solution.py
@@ -7,7 +7,7 @@
 from jax.experimental.pallas import tpu as pltpu
 from jax.sharding import PartitionSpec as P
 
-FORWARD = (64,)
+RELAY_FLOPS = 30_000_000_000
 BACKWARD = (64,)
 
 
@@ -23,21 +23,45 @@
     return pl.BlockSpec(memory_space=pltpu.VMEM)
 
 
-def params():
-    return pltpu.CompilerParams(vmem_limit_bytes=48 * 1024 * 1024)
-
-
-def slot_kernel(block_size, owners, own, left, right, out, held, sems):
-    count = held.shape[0]
+def params(mib=48):
+    return pltpu.CompilerParams(vmem_limit_bytes=mib * 1024 * 1024)
+
+
+def relay_kernel(ahead, passed_right, behind, passed_left, out_right, out_left):
+    for mine, passed, out in ((ahead, passed_right, out_right), (behind, passed_left, out_left)):
+        out[...] = (mine[...].astype(jnp.float32) + passed[...].astype(jnp.float32)).astype(
+            jnp.bfloat16
+        )
+
+
+def relays(ahead, passed_right, behind, passed_left):
+    rows, columns = ahead.shape
+    return pl.pallas_call(
+        relay_kernel,
+        out_shape=[jax.ShapeDtypeStruct((rows, columns), jnp.bfloat16)] * 2,
+        in_specs=[vmem_spec()] * 4,
+        out_specs=[vmem_spec()] * 2,
+        compiler_params=params(),
+        cost_estimate=pl.CostEstimate(
+            flops=RELAY_FLOPS, bytes_accessed=12 * rows * columns, transcendentals=0
+        ),
+        name="relays",
+    )(ahead, passed_right, behind, passed_left)
+
+
+def slot_kernel(block_size, owners, own, low_a, low_b, high_a, high_b, out, held, sems):
+    count, rows = held.shape[:2]
+    half = rows // 2
     copies = []
     for at in range(count):
         columns = slice(at * block_size, (at + 1) * block_size)
-        total = (
-            own[:, columns].astype(jnp.float32)
-            + left[:, columns].astype(jnp.float32)
-            + right[:, columns].astype(jnp.float32)
-        )
-        held[at] = total.astype(jnp.bfloat16)
+        for first, one, other in ((0, low_a, low_b), (half, high_a, high_b)):
+            total = (
+                own[first : first + half, columns].astype(jnp.float32)
+                + one[:, columns].astype(jnp.float32)
+                + other[:, columns].astype(jnp.float32)
+            )
+            held[at, first : first + half] = total.astype(jnp.bfloat16)
         copy = pltpu.make_async_copy(held.at[at], out.at[owners[at]], sems.at[at])
         copy.start()
         copies.append(copy)
@@ -45,13 +69,13 @@
         copy.wait()
 
 
-def to_slots(owners, own, left, right, num_shards, block_size):
+def to_slots(owners, own, lower, upper, num_shards, block_size):
     rows, columns = own.shape
     count = columns // block_size
     return pl.pallas_call(
         functools.partial(slot_kernel, block_size),
         out_shape=jax.ShapeDtypeStruct((num_shards, rows, block_size), jnp.bfloat16),
-        in_specs=[pl.BlockSpec(memory_space=pltpu.SMEM)] + [vmem_spec()] * 3,
+        in_specs=[pl.BlockSpec(memory_space=pltpu.SMEM)] + [vmem_spec()] * 5,
         out_specs=any_spec(),
         scratch_shapes=[
             pltpu.VMEM((count, rows, block_size), jnp.bfloat16),
@@ -62,7 +86,7 @@
             flops=3 * rows * columns, bytes_accessed=8 * rows * columns, transcendentals=0
         ),
         name="to_slots",
-    )(owners, own, left, right)
+    )(owners, own, *lower, *upper)
 
 
 def whole_block(parts):
@@ -147,10 +171,11 @@
     )(rows_of, named, *parts, factor_left, factor_right)
 
 
-def pick_kernel(block_size, count, owners, slots, out, sems):
+def pick_kernel(block_size, count, owners, slots, low, high, sems):
     copies = []
-    for at in range(count):
-        columns = pl.ds(at * block_size, block_size)
+    for at in range(2 * count):
+        out, first = (low, at) if at < count else (high, at - count)
+        columns = pl.ds(first * block_size, block_size)
         copy = pltpu.make_async_copy(slots.at[owners[at]], out.at[:, columns], sems.at[at])
         copy.start()
         copies.append(copy)
@@ -159,55 +184,48 @@
 
 
 def from_slots(owners, slots):
-    count = owners.shape[0]
+    count = owners.shape[0] // 2
     _, rows, block_size = slots.shape
     return pl.pallas_call(
         functools.partial(pick_kernel, block_size, count),
-        out_shape=jax.ShapeDtypeStruct((rows, count * block_size), jnp.bfloat16),
+        out_shape=[jax.ShapeDtypeStruct((rows, count * block_size), jnp.bfloat16)] * 2,
         in_specs=[pl.BlockSpec(memory_space=pltpu.SMEM), any_spec()],
-        out_specs=any_spec(),
-        scratch_shapes=[pltpu.SemaphoreType.DMA((count,))],
-        compiler_params=params(),
-        cost_estimate=pl.CostEstimate(
-            flops=0, bytes_accessed=4 * rows * count * block_size, transcendentals=0
+        out_specs=[vmem_spec()] * 2,
+        scratch_shapes=[pltpu.SemaphoreType.DMA((2 * count,))],
+        compiler_params=params(),
+        cost_estimate=pl.CostEstimate(
+            flops=0, bytes_accessed=8 * rows * count * block_size, transcendentals=0
         ),
         name="from_slots",
     )(owners, slots)
 
 
-def place_kernel(start, groups, own, left, right, far_left, far_right, *rest):
-    out, sems = rest[-2:]
-    rows, width = own.shape
-    half = far_left.shape[1]
+def place_kernel(groups, *refs):
+    pieces, out, sems = refs[:-2], refs[-2], refs[-1]
+    half = pieces[0].shape[1]
     copies = []
-    for at, (piece, group, shift) in enumerate(
-        ((own, 0, 0), (left, 1, 0), (right, 2, 0), (far_left, 3, 0), (far_right, 3, half))
-    ):
-        first = pl.multiple_of(groups[group] * width + shift, 128)
-        copy = pltpu.make_async_copy(
-            piece, out.at[pl.ds(start, rows), pl.ds(first, piece.shape[1])], sems.at[at]
-        )
+    for at, piece in enumerate(pieces):
+        first = pl.multiple_of(groups[at // 2] * (2 * half) + at % 2 * half, 128)
+        copy = pltpu.make_async_copy(piece, out.at[:, pl.ds(first, half)], sems.at[at])
         copy.start()
         copies.append(copy)
     for copy in copies:
         copy.wait()
 
 
-def place(groups, pieces, start, shape, held):
-    given = () if held is None else (held,)
-    return pl.pallas_call(
-        functools.partial(place_kernel, start),
+def place(groups, pieces, shape):
+    return pl.pallas_call(
+        place_kernel,
         out_shape=jax.ShapeDtypeStruct(shape, jnp.bfloat16),
-        in_specs=[pl.BlockSpec(memory_space=pltpu.SMEM)] + [any_spec()] * (5 + len(given)),
+        in_specs=[pl.BlockSpec(memory_space=pltpu.SMEM)] + [vmem_spec()] * len(pieces),
         out_specs=any_spec(),
-        scratch_shapes=[pltpu.SemaphoreType.DMA((5,))],
-        input_output_aliases={} if held is None else {6: 0},
-        compiler_params=params(),
-        cost_estimate=pl.CostEstimate(
-            flops=0, bytes_accessed=4 * pieces[0].shape[0] * shape[1], transcendentals=0
+        scratch_shapes=[pltpu.SemaphoreType.DMA((len(pieces),))],
+        compiler_params=params(),
+        cost_estimate=pl.CostEstimate(
+            flops=0, bytes_accessed=4 * shape[0] * shape[1], transcendentals=0
         ),
         name="place",
-    )(groups, *pieces, *given)
+    )(groups, *pieces)
 
 
 def body(grads, owner_map, factor_left, factor_right, left_inverse_roots, right_inverse_roots):
@@ -257,47 +275,46 @@
         )
         return part.reshape(rows, width)
 
-    arrived = []
-    for start, rows in zip(offsets(FORWARD), FORWARD, strict=True):
-        half = rows // 2
-        passed_right = to_right(piece(far_at, start, half))
-        passed_left = to_left(piece(far_at, start + half, half))
-        ahead = piece(right_at, start, rows)
-        behind = piece(left_at, start, rows)
-        add = lambda a, b: (a.astype(jnp.float32) + b.astype(jnp.float32)).astype(jnp.bfloat16)
-        from_left = to_right(jnp.concatenate([add(ahead[:half], passed_right), ahead[half:]]))
-        from_right = to_left(jnp.concatenate([behind[:half], add(behind[half:], passed_left)]))
-        slots = to_slots(
-            owners, piece(replica_at, start, rows), from_left, from_right, num_shards, block_size
-        )
-        came = lax.all_to_all(slots, "shard", split_axis=0, concat_axis=0, tiled=True)
-        arrived.append(came.reshape(block_rows, strips, rows, block_size))
+    half = strip_rows // 2
+    far = (piece(far_at, 0, half), piece(far_at, half, half))
+    (ahead_at, behind_at), far = lax.optimization_barrier(((right_at, left_at), far))
+    passed_right, passed_left = to_right(far[0]), to_left(far[1])
+    plain_right = to_right(piece(ahead_at, half, half))
+    plain_left = to_left(piece(behind_at, 0, half))
+    ahead, behind = relays(
+        piece(right_at, 0, half), passed_right, piece(left_at, half, half), passed_left
+    )
+    added_right, added_left = to_right(ahead), to_left(behind)
+    lower = (plain_left, added_right)
+    upper = (added_left, plain_right)
+    groups = jnp.stack([replica_at, left_at, right_at, far_at]).astype(jnp.int32)
+    upper, rows_of, named, groups = lax.optimization_barrier((upper, rows_of, named, groups))
+    own = piece(replica_at, 0, strip_rows)
+    slots = to_slots(owners, own, lower, upper, num_shards, block_size)
+    came = lax.all_to_all(slots, "shard", split_axis=0, concat_axis=0, tiled=True)
+    arrived = [came.reshape(block_rows, strips, strip_rows, block_size)]
 
     outs = updates(rows_of, arrived, left_inverse_roots[0], right_inverse_roots[0], BACKWARD)
     new_left, new_right = statistics(rows_of, named, arrived, factor_left[0], factor_right[0])
 
-    update = None
-    groups = jnp.stack([replica_at, left_at, right_at, far_at]).astype(jnp.int32)
-    for start, out in zip(offsets(BACKWARD), outs, strict=True):
-        rows = out.shape[2]
-        came = lax.all_to_all(
-            out.reshape(num_shards, rows, block_size),
-            "shard",
-            split_axis=0,
-            concat_axis=0,
-            tiled=True,
-        )
-        own = from_slots(owners, came)
-        from_left, from_right = to_right(own), to_left(own)
-        far_left = to_right(from_left[:, : width // 2])
-        far_right = to_left(from_right[:, width // 2 :])
-        update = place(
-            groups,
-            (own, from_left, from_right, far_left, far_right),
-            start,
-            (strip_rows, columns),
-            update,
-        )
+    returned = lax.all_to_all(
+        outs[0].reshape(num_shards, strip_rows, block_size),
+        "shard",
+        split_axis=0,
+        concat_axis=0,
+        tiled=True,
+    )
+    low, high = from_slots(owners, returned)
+    later, (low, high) = lax.optimization_barrier((owners, (low, high)))
+    left_low, right_high = to_right(low), to_left(high)
+    own_low, own_high = from_slots(later, returned)
+    left_high, right_low = to_right(own_high), to_left(own_low)
+    far_low, far_high = to_right(left_low), to_left(right_high)
+    update = place(
+        groups,
+        (own_low, own_high, left_low, left_high, right_low, right_high, far_low, far_high),
+        (strip_rows, columns),
+    )
     return (new_left[None], new_right[None], update)
 
 

time: 165 us -> 149 us (0.903)
  waiting for transfers between devices: 82.8 us -> 35.8 us
  blocking collectives: 31.3 us -> 67.7 us
  starting transfers between devices: 22 us -> 18.1 us
  Pallas kernels: 16.2 us -> 19.1 us
  local copies, waits for them, and re-layouts: 8.4 us -> 5.97 us
    all_to_all x1 -> x2, blocking collectives: 31.3 us -> 67.7 us  [the longest x1 35.5 us: body(): lax.all_to_all(slots, 'shard', split_axis=0, concat_axis=0, tiled=True)]
    all_to_all x1 -> x0, waiting for transfers between devices: 28 us -> none  [body(): lax.all_to_all(slots, 'shard', split_axis=0, concat_axis=0, tiled=True)]
    ppermute x4 -> x6, waiting for transfers between devices: 22.8 us -> 8.73 us  [body(): to_left = lambda a: lax.ppermute(a, 'replica', back)]
    all_to_all x1 -> x0, starting transfers between devices: 7.32 us -> none  [body(): lax.all_to_all(slots, 'shard', split_axis=0, concat_axis=0, tiled=True)]
    unnamed x14 -> x10, local copies, waits for them, and re-layouts: 5.46 us -> 0.03 us
    ppermute x4 -> x6, waiting for transfers between devices: 32 us -> 27.1 us  [body(): to_right = lambda a: lax.ppermute(a, 'replica', onward)]
    reshape x1 -> x3, local copies, waits for them, and re-layouts: 1.24 us -> 5.87 us  [piece(): return part.reshape(rows, width)]
    ppermute x4 -> x6, starting transfers between devices: 11.2 us -> 14.4 us  [body(): to_left = lambda a: lax.ppermute(a, 'replica', back)]
  transfers between devices with their start and end apart: 9 -> 12, of which waited for: 6 -> 8; matrix products, arithmetic and copies ran while one was open for 1% -> 3% of each run, Pallas kernels for 4% -> 6%
where the time goes in v2:
time: 149 us; the launch traced here: 148 us
  blocking collectives  67.7 us (45%)
  waiting for transfers between devices  35.8 us (24%)
  Pallas kernels  19.1 us (13%)
  starting transfers between devices  18.1 us (12%)
  local copies, waits for them, and re-layouts  5.97 us (4%)
    all_to_all x1, blocking collectives, body(): lax.all_to_all(slots, 'shard', split_axis=0, concat_axis=0, tiled=True)  35.5 us
    all_to_all x1, blocking collectives, body(): lax.all_to_all(outs[0].reshape(num_shards, strip_rows, block_size), 'shar...  32.2 us
    ppermute x6, waiting for transfers between devices, body(): to_right = lambda a: lax.ppermute(a, 'replica', onward)  27.1 us
    ppermute x6, starting transfers between devices, body(): to_left = lambda a: lax.ppermute(a, 'replica', back)  14.4 us
    ppermute x6, waiting for transfers between devices, body(): to_left = lambda a: lax.ppermute(a, 'replica', back)  8.73 us
    pallas_call x1, Pallas kernels, statistics(): pl.pallas_call(functools.partial(gram_kernel, len(parts)), grid_spec=pltp...  6.55 us
    reshape x3, local copies, waits for them, and re-layouts, piece(): return part.reshape(rows, width)  5.87 us
    pallas_call x1, Pallas kernels, updates(): pl.pallas_call(functools.partial(update_kernel, len(parts), bounds), grid...  4.08 us
  transfers between devices with their start and end apart: 12, of which 8 were waited for; matrix products, arithmetic and copies ran while one was open for 3% of the time, Pallas kernels for 6%

profile of v2, /device:TPU:0, one launch (start us, length us, event | category | flops | bytes accessed | tf_op | source)
XLA Modules:
  0.0 148.5 jit_solution(6440086617635817498)
XLA Ops:
  0.7 2.1 %dynamic-slice_bitcast_fusion.4 = (bf16[32,7168]{1,0:T(8,128)(2,1)}, bf16[32,7168]{1,0:T(8,128)(2,1)}) fusion(bf16[8,8,4,7168]{3,1,2,0:T(8,128)(2,1)} %bitcast.57, s32[]{:T(128)S(6)} %select_n.62), kind=kLoop, calls=%fused_computation.4 | loop fusion | bytes 1835012 | tf_op jit(solution)/shard_map/reshape | solution.py:276
  2.8 2.0 %collective-permute-start = (bf16[32,7168]{1,0:T(8,128)(2,1)}, bf16[32,7168]{1,0:T(8,128)(2,1)S(1)}, u32[]{:S(2)}, u32[]{:S(2)}) collective-permute-start(bf16[32,7168]{1,0:T(8,128)(2,1)} %get-tuple-element.23), channel_id=1, source_target_pairs={{0,32},{32,64},{64,96},{96,0},{1,33},{33,65},{65,97},{97,1},{2,34}... | collective-permute-start | bytes 1376264 | tf_op jit(solution)/shard_map/ppermute | solution.py:244
  4.8 2.1 %collective-permute-start.1 = (bf16[32,7168]{1,0:T(8,128)(2,1)}, bf16[32,7168]{1,0:T(8,128)(2,1)}, u32[]{:S(2)}, u32[]{:S(2)}) collective-permute-start(bf16[32,7168]{1,0:T(8,128)(2,1)} %get-tuple-element.24), channel_id=1, source_target_pairs={{0,96},{32,0},{64,32},{96,64},{1,97},{33,1},{65,33},{97,65},{2,98}... | collective-permute-start | bytes 1376264 | tf_op jit(solution)/shard_map/ppermute | solution.py:245
  6.9 2.5 %dynamic-slice_bitcast_fusion.1 = (bf16[32,7168]{1,0:T(8,128)(2,1)}, bf16[32,7168]{1,0:T(8,128)(2,1)}, bf16[32,7168]{1,0:T(8,128)(2,1)S(1)}, bf16[32,7168]{1,0:T(8,128)(2,1)S(1)}) fusion(bf16[8,8,4,7168]{3,1,2,0:T(8,128)(2,1)} %bitcast.58, s32[]{:T(128)S(6)} %select_n.73, s32[]{:T(128)S(6)} %select_n.64, s32[]{:T(128)S(6)} %select_n.63, s32[]{:T(128)S(6)} %select_n.59), kind=kLoop, calls=%fused_computation.1 | loop fusion | bytes 3670032 | tf_op jit(solution)/shard_map/reshape | solution.py:276
  9.4 2.0 %collective-permute-start.4 = (bf16[32,7168]{1,0:T(8,128)(2,1)}, bf16[32,7168]{1,0:T(8,128)(2,1)S(1)}, u32[]{:S(2)}, u32[]{:S(2)}) collective-permute-start(bf16[32,7168]{1,0:T(8,128)(2,1)} %get-tuple-element.46), channel_id=1, source_target_pairs={{0,96},{32,0},{64,32},{96,64},{1,97},{33,1},{65,33},{97,65},{2,98}... | collective-permute-start | bytes 1376264 | tf_op jit(solution)/shard_map/ppermute | solution.py:245
  11.5 0.3 compare_reduce_fusion.1
  11.8 0.2 reduce-window.16
  12.0 1.2 dynamic-slice_bitcast_fusion.own
  13.3 5.2 %collective-permute-done.passed_right = bf16[32,7168]{1,0:T(8,128)(2,1)S(1)} collective-permute-done((bf16[32,7168]{1,0:T(8,128)(2,1)}, bf16[32,7168]{1,0:T(8,128)(2,1)S(1)}, u32[]{:S(2)}, u32[]{:S(2)}) %collective-permute-start) | collective-permute-done | bytes 458784 | tf_op jit(solution)/shard_map/ppermute | solution.py:244
  18.6 2.0 %relays.1 = (bf16[32,7168]{1,0:T(8,128)(2,1)}, bf16[32,7168]{1,0:T(8,128)(2,1)}) custom-call(bf16[32,7168]{1,0:T(8,128)(2,1)S(1)} %get-tuple-element.49.ahead, bf16[32,7168]{1,0:T(8,128)(2,1)S(1)} %collective-permute-done.passed_right, bf16[32,7168]{1,0:T(8,128)(2,1)S(1)} %get-tuple-element.48.behind, bf16[32,7168]{1,0:T(8,128)(2,1)} %collective-permute-done.1.passed_left), custom_call_target="tpu_custom_call" | custom-call | flops 30000001024 | bytes 2752512 | tf_op jit(solution)/shard_map/relays/pallas_call | solution.py:39
  20.6 3.3 %collective-permute-start.2 = (bf16[32,7168]{1,0:T(8,128)(2,1)}, bf16[32,7168]{1,0:T(8,128)(2,1)S(1)}, u32[]{:S(2)}, u32[]{:S(2)}) collective-permute-start(bf16[32,7168]{1,0:T(8,128)(2,1)} %get-tuple-element.25), channel_id=1, source_target_pairs={{0,96},{32,0},{64,32},{96,64},{1,97},{33,1},{65,33},{97,65},{2,98}... | collective-permute-start | bytes 1376264 | tf_op jit(solution)/shard_map/ppermute | solution.py:245
  23.9 0.2 reduce-window.17
  24.3 0.2 select_reduce_fusion.rows_of
  24.5 3.9 %collective-permute-done.3.high_b = bf16[32,7168]{1,0:T(8,128)(2,1)S(1)} collective-permute-done((bf16[32,7168]{1,0:T(8,128)(2,1)}, bf16[32,7168]{1,0:T(8,128)(2,1)S(1)}, u32[]{:S(2)}, u32[]{:S(2)}) %collective-permute-start.3) | collective-permute-done | bytes 458784 | tf_op jit(solution)/shard_map/ppermute | solution.py:244
  28.3 8.5 %collective-permute-done.2.high_a = bf16[32,7168]{1,0:T(8,128)(2,1)S(1)} collective-permute-done((bf16[32,7168]{1,0:T(8,128)(2,1)}, bf16[32,7168]{1,0:T(8,128)(2,1)S(1)}, u32[]{:S(2)}, u32[]{:S(2)}) %collective-permute-start.2) | collective-permute-done | bytes 458784 | tf_op jit(solution)/shard_map/ppermute | solution.py:245
  36.9 0.5 collective-permute-done.5.low_b
  37.3 2.2 %to_slots.1 = bf16[32,64,512]{2,1,0:T(8,128)(2,1)S(1)} custom-call(s32[14]{0:T(128)S(1)} %bitcast_select_fusion.owners, bf16[64,7168]{1,0:T(8,128)(2,1)S(1)} %dynamic-slice_bitcast_fusion.own, bf16[32,7168]{1,0:T(8,128)(2,1)S(1)} %collective-permute-done.4.low_a, bf16[32,7168]{1,0:T(8,128)(2,1)S(1)} %collective-permute-done.5.low_b, ...), custom_call_target="tpu_custom_call" | custom-call | flops 1376256 | bytes 3670016 | tf_op jit(solution)/shard_map/to_slots/pallas_call | solution.py:75
  39.6 35.5 %all_to_all.10 = bf16[32,64,512]{2,1,0:T(8,128)(2,1)} all-to-all(bf16[32,64,512]{2,1,0:T(8,128)(2,1)S(1)} %to_slots.1), channel_id=1, replica_groups=mesh['replica'=4,'shard'=32] {'shard'}, dimensions={0} | all-to-all | bytes 4194304 | tf_op jit(solution)/shard_map/all_to_all | solution.py:294
  75.1 4.1 %updates.1 = bf16[4,8,64,512]{3,2,1,0:T(8,128)(2,1)S(1)} custom-call(s32[3]{0:T(128)S(1)} %select_reduce_fusion.rows_of, bf16[4,8,64,512]{3,2,1,0:T(8,128)(2,1)} %bitcast.51, bf16[3,512,512]{2,1,0:T(8,128)(2,1)S(1)} %bitcast.55, bf16[3,512,512]{2,1,0:T(8,128)(2,1)S(1)} %bitcast.56), custom_call_target="tpu_custom_call" | custom-call | flops 1610612736 | bytes 6291456 | tf_op jit(solution)/shard_map/updates/pallas_call | solution.py:115
  79.2 32.2 %all_to_all.11.slots = bf16[32,64,512]{2,1,0:T(8,128)(2,1)S(1)} all-to-all(bf16[32,64,512]{2,1,0:T(8,128)(2,1)S(1)} %bitcast.53), channel_id=1, replica_groups=mesh['replica'=4,'shard'=32] {'shard'}, dimensions={0} | all-to-all | bytes 4194304 | tf_op jit(solution)/shard_map/all_to_all | solution.py:300
  111.4 0.9 from_slots.2
  112.3 1.4 collective-permute-start.6
  113.6 2.0 %collective-permute-start.9 = (bf16[64,3584]{1,0:T(8,128)(2,1)S(1)}, bf16[64,3584]{1,0:T(8,128)(2,1)S(1)}, u32[]{:S(2)}, u32[]{:S(2)}) collective-permute-start(bf16[64,3584]{1,0:T(8,128)(2,1)S(1)} %get-tuple-element.42), channel_id=1, source_target_pairs={{0,96},{32,0},{64,32},{96,64},{1,97},{33,1},{65,33},{97,65},{2,98}... | collective-permute-start | bytes 1376264 | tf_op jit(solution)/shard_map/ppermute | solution.py:245
  115.6 0.9 from_slots.3
  116.5 1.8 %collective-permute-start.8 = (bf16[64,3584]{1,0:T(8,128)(2,1)S(1)}, bf16[64,3584]{1,0:T(8,128)(2,1)S(1)}, u32[]{:S(2)}, u32[]{:S(2)}) collective-permute-start(bf16[64,3584]{1,0:T(8,128)(2,1)S(1)} %get-tuple-element.39.refs_0_), channel_id=1, source_target_pairs={{0,96},{32,0},{64,32},{96,64},{1,97},{33,1},{65,33},{97,65},{2,98}... | collective-permute-start | bytes 1376264 | tf_op jit(solution)/shard_map/ppermute | solution.py:245
  118.3 0.3 collective-permute-start.7
  118.6 8.3 %collective-permute-done.6.refs_2_ = bf16[64,3584]{1,0:T(8,128)(2,1)S(1)} collective-permute-done((bf16[64,3584]{1,0:T(8,128)(2,1)S(1)}, bf16[64,3584]{1,0:T(8,128)(2,1)S(1)}, u32[]{:S(2)}, u32[]{:S(2)}) %collective-permute-start.6) | collective-permute-done | bytes 458784 | tf_op jit(solution)/shard_map/ppermute | solution.py:244
  127.0 3.2 %collective-permute-start.11 = (bf16[64,3584]{1,0:T(8,128)(2,1)S(1)}, bf16[64,3584]{1,0:T(8,128)(2,1)S(1)}, u32[]{:S(2)}, u32[]{:S(2)}) collective-permute-start(bf16[64,3584]{1,0:T(8,128)(2,1)S(1)} %collective-permute-done.9.refs_5_), channel_id=1, source_target_pairs={{0,96},{32,0},{64,32},{96,64},{1,97},{33,1},{65,33},{97,65},{2,98}... | collective-permute-start | bytes 1376264 | tf_op jit(solution)/shard_map/ppermute | solution.py:245
  130.2 6.6 %statistics.1 = (f32[3,512,512]{2,1,0:T(8,128)}, f32[3,512,512]{2,1,0:T(8,128)}) custom-call(s32[3]{0:T(128)S(1)} %select_reduce_fusion.rows_of, s32[3]{0:T(128)S(1)} %get-tuple-element.28.named, bf16[4,8,64,512]{3,2,1,0:T(8,128)(2,1)S(1)} %bitcast.52, f32[3,512,512]{2,1,0:T(8,128)S(1)} %bitcast.54, f32[3,512,512]{2,1,0:T(8,128)} %bitcast.60), custom_call_target="tpu_custom_call" | custom-call | flops 1610612736 | bytes 14155776 | tf_op jit(solution)/shard_map/statistics/pallas_call | solution.py:154
  136.7 0.1 collective-permute-done.8.refs_4_
  136.9 9.2 %collective-permute-done.10.refs_6_ = bf16[64,3584]{1,0:T(8,128)(2,1)S(1)} collective-permute-done((bf16[64,3584]{1,0:T(8,128)(2,1)S(1)}, bf16[64,3584]{1,0:T(8,128)(2,1)S(1)}, u32[]{:S(2)}, u32[]{:S(2)}) %collective-permute-start.10) | collective-permute-done | bytes 458784 | tf_op jit(solution)/shard_map/ppermute | solution.py:244
  146.1 2.4 %place.1 = bf16[64,28672]{1,0:T(8,128)(2,1)} custom-call(s32[4]{0:T(128)S(1)} %pad_add_fusion.groups, bf16[64,3584]{1,0:T(8,128)(2,1)S(1)} %get-tuple-element.39.refs_0_, bf16[64,3584]{1,0:T(8,128)(2,1)S(1)} %get-tuple-element.40.refs_1_, bf16[64,3584]{1,0:T(8,128)(2,1)S(1)} %collective-permute-done.6.refs_2_, ...), custom_call_target="tpu_custom_call" | custom-call | bytes 7340032 | tf_op jit(solution)/shard_map/place/pallas_call | solution.py:217
  (24 shorter events, 0.5 us)
Async XLA Ops:
  0.6 10.8 %copy-start.4 = (s32[4,56]{1,0:T(4,128)S(1)}, s32[4,56]{1,0:T(4,128)}, u32[]{:S(2)}) copy-start(s32[4,56]{1,0:T(4,128)} %param.7) | copy-start | bytes 2692
  2.8 15.7 %collective-permute-start = (bf16[32,7168]{1,0:T(8,128)(2,1)}, bf16[32,7168]{1,0:T(8,128)(2,1)S(1)}, u32[]{:S(2)}, u32[]{:S(2)}) collective-permute-start(bf16[32,7168]{1,0:T(8,128)(2,1)} %get-tuple-element.23), channel_id=1, source_target_pairs={{0,32},{32,64},{64,96},{96,0},{1,33},{33,65},{65,97},{97,1},{2,34}... | collective-permute-start | bytes 1376264 | tf_op jit(solution)/shard_map/ppermute | solution.py:244
  4.8 13.7 %collective-permute-start.1 = (bf16[32,7168]{1,0:T(8,128)(2,1)}, bf16[32,7168]{1,0:T(8,128)(2,1)}, u32[]{:S(2)}, u32[]{:S(2)}) collective-permute-start(bf16[32,7168]{1,0:T(8,128)(2,1)} %get-tuple-element.24), channel_id=1, source_target_pairs={{0,96},{32,0},{64,32},{96,64},{1,97},{33,1},{65,33},{97,65},{2,98}... | collective-permute-start | bytes 1376264 | tf_op jit(solution)/shard_map/ppermute | solution.py:245
  9.4 27.4 %collective-permute-start.4 = (bf16[32,7168]{1,0:T(8,128)(2,1)}, bf16[32,7168]{1,0:T(8,128)(2,1)S(1)}, u32[]{:S(2)}, u32[]{:S(2)}) collective-permute-start(bf16[32,7168]{1,0:T(8,128)(2,1)} %get-tuple-element.46), channel_id=1, source_target_pairs={{0,96},{32,0},{64,32},{96,64},{1,97},{33,1},{65,33},{97,65},{2,98}... | collective-permute-start | bytes 1376264 | tf_op jit(solution)/shard_map/ppermute | solution.py:245
  11.5 16.9 %collective-permute-start.3 = (bf16[32,7168]{1,0:T(8,128)(2,1)}, bf16[32,7168]{1,0:T(8,128)(2,1)S(1)}, u32[]{:S(2)}, u32[]{:S(2)}) collective-permute-start(bf16[32,7168]{1,0:T(8,128)(2,1)} %get-tuple-element.47), channel_id=1, source_target_pairs={{0,32},{32,64},{64,96},{96,0},{1,33},{33,65},{65,97},{97,1},{2,34}... | collective-permute-start | bytes 1376264 | tf_op jit(solution)/shard_map/ppermute | solution.py:244
  20.6 16.2 %collective-permute-start.2 = (bf16[32,7168]{1,0:T(8,128)(2,1)}, bf16[32,7168]{1,0:T(8,128)(2,1)S(1)}, u32[]{:S(2)}, u32[]{:S(2)}) collective-permute-start(bf16[32,7168]{1,0:T(8,128)(2,1)} %get-tuple-element.25), channel_id=1, source_target_pairs={{0,96},{32,0},{64,32},{96,64},{1,97},{33,1},{65,33},{97,65},{2,98}... | collective-permute-start | bytes 1376264 | tf_op jit(solution)/shard_map/ppermute | solution.py:245
  23.9 13.4 %collective-permute-start.5 = (bf16[32,7168]{1,0:T(8,128)(2,1)}, bf16[32,7168]{1,0:T(8,128)(2,1)S(1)}, u32[]{:S(2)}, u32[]{:S(2)}) collective-permute-start(bf16[32,7168]{1,0:T(8,128)(2,1)} %get-tuple-element.30), channel_id=1, source_target_pairs={{0,32},{32,64},{64,96},{96,0},{1,33},{33,65},{65,97},{97,1},{2,34}... | collective-permute-start | bytes 1376264 | tf_op jit(solution)/shard_map/ppermute | solution.py:244
  39.6 35.6 %copy-start.2 = (bf16[1,3,512,512]{3,2,1,0:T(8,128)(2,1)S(1)}, bf16[1,3,512,512]{3,2,1,0:T(8,128)(2,1)}, u32[]{:S(2)}) copy-start(bf16[1,3,512,512]{3,2,1,0:T(8,128)(2,1)} %param.10) | copy-start | bytes 4718596
  39.6 35.6 %copy-start.3 = (bf16[1,3,512,512]{3,2,1,0:T(8,128)(2,1)S(1)}, bf16[1,3,512,512]{3,2,1,0:T(8,128)(2,1)}, u32[]{:S(2)}) copy-start(bf16[1,3,512,512]{3,2,1,0:T(8,128)(2,1)} %param.11) | copy-start | bytes 4718596
  79.2 51.0 %copy-start.1 = (f32[1,3,512,512]{3,2,1,0:T(8,128)S(1)}, f32[1,3,512,512]{3,2,1,0:T(8,128)}, u32[]{:S(2)}) copy-start(f32[1,3,512,512]{3,2,1,0:T(8,128)} %param.8) | copy-start | bytes 9437188
  111.4 18.8 %copy-start = (bf16[32,64,512]{2,1,0:T(8,128)(2,1)S(1)}, bf16[32,64,512]{2,1,0:T(8,128)(2,1)}, u32[]{:S(2)}) copy-start(bf16[32,64,512]{2,1,0:T(8,128)(2,1)} %all_to_all.10) | copy-start | bytes 6291460
  112.3 14.6 %collective-permute-start.6 = (bf16[64,3584]{1,0:T(8,128)(2,1)S(1)}, bf16[64,3584]{1,0:T(8,128)(2,1)S(1)}, u32[]{:S(2)}, u32[]{:S(2)}) collective-permute-start(bf16[64,3584]{1,0:T(8,128)(2,1)S(1)} %get-tuple-element.41), channel_id=1, source_target_pairs={{0,32},{32,64},{64,96},{96,0},{1,33},{33,65},{65,97},{97,1},{2,34}... | collective-permute-start | bytes 1376264 | tf_op jit(solution)/shard_map/ppermute | solution.py:244
  113.6 13.4 %collective-permute-start.9 = (bf16[64,3584]{1,0:T(8,128)(2,1)S(1)}, bf16[64,3584]{1,0:T(8,128)(2,1)S(1)}, u32[]{:S(2)}, u32[]{:S(2)}) collective-permute-start(bf16[64,3584]{1,0:T(8,128)(2,1)S(1)} %get-tuple-element.42), channel_id=1, source_target_pairs={{0,96},{32,0},{64,32},{96,64},{1,97},{33,1},{65,33},{97,65},{2,98}... | collective-permute-start | bytes 1376264 | tf_op jit(solution)/shard_map/ppermute | solution.py:245
  116.5 20.3 %collective-permute-start.8 = (bf16[64,3584]{1,0:T(8,128)(2,1)S(1)}, bf16[64,3584]{1,0:T(8,128)(2,1)S(1)}, u32[]{:S(2)}, u32[]{:S(2)}) collective-permute-start(bf16[64,3584]{1,0:T(8,128)(2,1)S(1)} %get-tuple-element.39.refs_0_), channel_id=1, source_target_pairs={{0,96},{32,0},{64,32},{96,64},{1,97},{33,1},{65,33},{97,65},{2,98}... | collective-permute-start | bytes 1376264 | tf_op jit(solution)/shard_map/ppermute | solution.py:245
  118.3 18.5 %collective-permute-start.7 = (bf16[64,3584]{1,0:T(8,128)(2,1)S(1)}, bf16[64,3584]{1,0:T(8,128)(2,1)S(1)}, u32[]{:S(2)}, u32[]{:S(2)}) collective-permute-start(bf16[64,3584]{1,0:T(8,128)(2,1)S(1)} %get-tuple-element.40.refs_1_), channel_id=1, source_target_pairs={{0,32},{32,64},{64,96},{96,0},{1,33},{33,65},{65,97},{97,1},{2,34}... | collective-permute-start | bytes 1376264 | tf_op jit(solution)/shard_map/ppermute | solution.py:244
  126.9 19.1 %collective-permute-start.10 = (bf16[64,3584]{1,0:T(8,128)(2,1)S(1)}, bf16[64,3584]{1,0:T(8,128)(2,1)S(1)}, u32[]{:S(2)}, u32[]{:S(2)}) collective-permute-start(bf16[64,3584]{1,0:T(8,128)(2,1)S(1)} %collective-permute-done.6.refs_2_), channel_id=1, source_target_pairs={{0,32},{32,64},{64,96},{96,0},{1,33},{33,65},{65,97},{97,1},{2,34}... | collective-permute-start | bytes 1376264 | tf_op jit(solution)/shard_map/ppermute | solution.py:244
  127.0 19.0 %collective-permute-start.11 = (bf16[64,3584]{1,0:T(8,128)(2,1)S(1)}, bf16[64,3584]{1,0:T(8,128)(2,1)S(1)}, u32[]{:S(2)}, u32[]{:S(2)}) collective-permute-start(bf16[64,3584]{1,0:T(8,128)(2,1)S(1)} %collective-permute-done.9.refs_5_), channel_id=1, source_target_pairs={{0,96},{32,0},{64,32},{96,64},{1,97},{33,1},{65,33},{97,65},{2,98}... | collective-permute-start | bytes 1376264 | tf_op jit(solution)/shard_map/ppermute | solution.py:245

commit v3 on v2

--- a/solution.py
+++ b/solution.py
@@ -8,11 +8,6 @@
 from jax.sharding import PartitionSpec as P
 
 RELAY_FLOPS = 30_000_000_000
-BACKWARD = (64,)
-
-
-def offsets(parts):
-    return [sum(parts[:at]) for at in range(len(parts))]
 
 
 def any_spec():
@@ -49,11 +44,9 @@
     )(ahead, passed_right, behind, passed_left)
 
 
-def slot_kernel(block_size, owners, own, low_a, low_b, high_a, high_b, out, held, sems):
-    count, rows = held.shape[:2]
-    half = rows // 2
-    copies = []
-    for at in range(count):
+def slot_kernel(block_size, owners, own, low_a, low_b, high_a, high_b, out):
+    half = own.shape[0] // 2
+    for at in range(own.shape[1] // block_size):
         columns = slice(at * block_size, (at + 1) * block_size)
         for first, one, other in ((0, low_a, low_b), (half, high_a, high_b)):
             total = (
@@ -61,26 +54,16 @@
                 + one[:, columns].astype(jnp.float32)
                 + other[:, columns].astype(jnp.float32)
             )
-            held[at, first : first + half] = total.astype(jnp.bfloat16)
-        copy = pltpu.make_async_copy(held.at[at], out.at[owners[at]], sems.at[at])
-        copy.start()
-        copies.append(copy)
-    for copy in copies:
-        copy.wait()
+            out[owners[at], first : first + half] = total.astype(jnp.bfloat16)
 
 
 def to_slots(owners, own, lower, upper, num_shards, block_size):
     rows, columns = own.shape
-    count = columns // block_size
     return pl.pallas_call(
         functools.partial(slot_kernel, block_size),
         out_shape=jax.ShapeDtypeStruct((num_shards, rows, block_size), jnp.bfloat16),
         in_specs=[pl.BlockSpec(memory_space=pltpu.SMEM)] + [vmem_spec()] * 5,
-        out_specs=any_spec(),
-        scratch_shapes=[
-            pltpu.VMEM((count, rows, block_size), jnp.bfloat16),
-            pltpu.SemaphoreType.DMA((count,)),
-        ],
+        out_specs=vmem_spec(),
         compiler_params=params(),
         cost_estimate=pl.CostEstimate(
             flops=3 * rows * columns, bytes_accessed=8 * rows * columns, transcendentals=0
@@ -89,41 +72,23 @@
     )(owners, own, *lower, *upper)
 
 
-def whole_block(parts):
-    joined = jnp.concatenate([part[0] for part in parts], axis=1)
-    return joined.reshape(joined.shape[0] * joined.shape[1], joined.shape[2])
-
-
-def update_kernel(num_parts, bounds, rows_of, *refs):
-    parts = refs[:num_parts]
-    left_root, right_root = refs[num_parts], refs[num_parts + 1]
-    outs = refs[num_parts + 2 :]
-    block = whole_block(parts)
-    applied = jnp.dot(left_root[0], block, preferred_element_type=jnp.float32).astype(jnp.bfloat16)
-    product = jnp.dot(applied, right_root[0], preferred_element_type=jnp.float32).astype(jnp.bfloat16)
-    product = product.reshape(parts[0].shape[1], -1, product.shape[1])
-    for out, (start, rows) in zip(outs, bounds, strict=True):
-        out[0] = product[:, start : start + rows]
-
-
-def updates(rows_of, parts, left_roots, right_roots, back):
+def update_kernel(rows_of, blocks, left_roots, right_roots, out):
+    for slot in range(left_roots.shape[0]):
+        block = blocks[rows_of[slot]]
+        applied = jnp.dot(left_roots[slot], block, preferred_element_type=jnp.float32)
+        product = jnp.dot(
+            applied.astype(jnp.bfloat16), right_roots[slot], preferred_element_type=jnp.float32
+        )
+        out[rows_of[slot]] = product.astype(jnp.bfloat16)
+
+
+def updates(rows_of, blocks, left_roots, right_roots):
     capacity, block_size = left_roots.shape[0], left_roots.shape[1]
-    block_rows, strips = parts[0].shape[:2]
-    bounds = list(zip(offsets(back), back, strict=True))
-    at_row = lambda t, rows_of: (rows_of[t], 0, 0, 0)
-    root = pl.BlockSpec((1, block_size, block_size), lambda t, rows_of: (t, 0, 0))
-    return pl.pallas_call(
-        functools.partial(update_kernel, len(parts), bounds),
-        grid_spec=pltpu.PrefetchScalarGridSpec(
-            num_scalar_prefetch=1,
-            grid=(capacity,),
-            in_specs=[pl.BlockSpec((1,) + part.shape[1:], at_row) for part in parts] + [root, root],
-            out_specs=[pl.BlockSpec((1, strips, rows, block_size), at_row) for rows in back],
-        ),
-        out_shape=[
-            jax.ShapeDtypeStruct((block_rows, strips, rows, block_size), jnp.bfloat16)
-            for rows in back
-        ],
+    return pl.pallas_call(
+        update_kernel,
+        out_shape=jax.ShapeDtypeStruct(blocks.shape, jnp.bfloat16),
+        in_specs=[pl.BlockSpec(memory_space=pltpu.SMEM)] + [vmem_spec()] * 3,
+        out_specs=vmem_spec(),
         compiler_params=params(),
         cost_estimate=pl.CostEstimate(
             flops=4 * capacity * block_size**3,
@@ -131,33 +96,29 @@
             transcendentals=0,
         ),
         name="updates",
-    )(rows_of, *parts, left_roots, right_roots)
-
-
-def gram_kernel(num_parts, rows_of, named, *refs):
-    parts = refs[:num_parts]
-    left, right, new_left, new_right = refs[num_parts:]
-    block = whole_block(parts)
-    size = block.shape[0]
+    )(rows_of, blocks, left_roots, right_roots)
+
+
+def gram_kernel(rows_of, named, blocks, left, right, new_left, new_right):
+    block = blocks[0]
     holds = named[pl.program_id(0)] > 0
-    scale = 0.1 / size
+    scale = 0.1 / block.shape[0]
     gram = lax.dot_general(block, block, (((1,), (1,)), ((), ())), preferred_element_type=jnp.float32)
     new_left[0] = 0.9 * left[0] + jnp.where(holds, scale * gram, 0.0)
     gram = lax.dot_general(block, block, (((0,), (0,)), ((), ())), preferred_element_type=jnp.float32)
     new_right[0] = 0.9 * right[0] + jnp.where(holds, scale * gram, 0.0)
 
 
-def statistics(rows_of, named, parts, factor_left, factor_right):
+def statistics(rows_of, named, blocks, factor_left, factor_right):
     capacity, block_size = factor_left.shape[0], factor_left.shape[1]
-    at_row = lambda t, rows_of, named: (rows_of[t], 0, 0, 0)
+    at_row = lambda t, rows_of, named: (rows_of[t], 0, 0)
     square = pl.BlockSpec((1, block_size, block_size), lambda t, rows_of, named: (t, 0, 0))
     return pl.pallas_call(
-        functools.partial(gram_kernel, len(parts)),
+        gram_kernel,
         grid_spec=pltpu.PrefetchScalarGridSpec(
             num_scalar_prefetch=2,
             grid=(capacity,),
-            in_specs=[pl.BlockSpec((1,) + part.shape[1:], at_row) for part in parts]
-            + [square, square],
+            in_specs=[pl.BlockSpec((1, block_size, block_size), at_row), square, square],
             out_specs=[square, square],
         ),
         out_shape=[jax.ShapeDtypeStruct(factor_left.shape, jnp.float32)] * 2,
@@ -168,30 +129,24 @@
             transcendentals=0,
         ),
         name="statistics",
-    )(rows_of, named, *parts, factor_left, factor_right)
-
-
-def pick_kernel(block_size, count, owners, slots, low, high, sems):
-    copies = []
+    )(rows_of, named, blocks, factor_left, factor_right)
+
+
+def pick_kernel(block_size, owners, slots, low, high):
+    count = low.shape[1] // block_size
     for at in range(2 * count):
         out, first = (low, at) if at < count else (high, at - count)
-        columns = pl.ds(first * block_size, block_size)
-        copy = pltpu.make_async_copy(slots.at[owners[at]], out.at[:, columns], sems.at[at])
-        copy.start()
-        copies.append(copy)
-    for copy in copies:
-        copy.wait()
+        out[:, first * block_size : (first + 1) * block_size] = slots[owners[at]]
 
 
 def from_slots(owners, slots):
     count = owners.shape[0] // 2
     _, rows, block_size = slots.shape
     return pl.pallas_call(
-        functools.partial(pick_kernel, block_size, count),
+        functools.partial(pick_kernel, block_size),
         out_shape=[jax.ShapeDtypeStruct((rows, count * block_size), jnp.bfloat16)] * 2,
-        in_specs=[pl.BlockSpec(memory_space=pltpu.SMEM), any_spec()],
+        in_specs=[pl.BlockSpec(memory_space=pltpu.SMEM), vmem_spec()],
         out_specs=[vmem_spec()] * 2,
-        scratch_shapes=[pltpu.SemaphoreType.DMA((2 * count,))],
         compiler_params=params(),
         cost_estimate=pl.CostEstimate(
             flops=0, bytes_accessed=8 * rows * count * block_size, transcendentals=0
@@ -201,7 +156,7 @@
 
 
 def place_kernel(groups, *refs):
-    pieces, out, sems = refs[:-2], refs[-2], refs[-1]
+    pieces, out, sems = refs[: 2 * groups.shape[0]], refs[-2], refs[-1]
     half = pieces[0].shape[1]
     copies = []
     for at, piece in enumerate(pieces):
@@ -213,19 +168,24 @@
         copy.wait()
 
 
-def place(groups, pieces, shape):
+def place(groups, pieces, shape, held=()):
     return pl.pallas_call(
         place_kernel,
         out_shape=jax.ShapeDtypeStruct(shape, jnp.bfloat16),
-        in_specs=[pl.BlockSpec(memory_space=pltpu.SMEM)] + [vmem_spec()] * len(pieces),
+        in_specs=[pl.BlockSpec(memory_space=pltpu.SMEM)]
+        + [vmem_spec()] * len(pieces)
+        + [any_spec()] * len(held),
         out_specs=any_spec(),
         scratch_shapes=[pltpu.SemaphoreType.DMA((len(pieces),))],
-        compiler_params=params(),
-        cost_estimate=pl.CostEstimate(
-            flops=0, bytes_accessed=4 * shape[0] * shape[1], transcendentals=0
+        input_output_aliases={1 + len(pieces): 0} if held else {},
+        compiler_params=params(),
+        cost_estimate=pl.CostEstimate(
+            flops=0,
+            bytes_accessed=4 * len(pieces) * pieces[0].shape[0] * pieces[0].shape[1],
+            transcendentals=0,
         ),
         name="place",
-    )(groups, *pieces)
+    )(groups, *pieces, *held)
 
 
 def body(grads, owner_map, factor_left, factor_right, left_inverse_roots, right_inverse_roots):
@@ -292,13 +252,12 @@
     own = piece(replica_at, 0, strip_rows)
     slots = to_slots(owners, own, lower, upper, num_shards, block_size)
     came = lax.all_to_all(slots, "shard", split_axis=0, concat_axis=0, tiled=True)
-    arrived = [came.reshape(block_rows, strips, strip_rows, block_size)]
-
-    outs = updates(rows_of, arrived, left_inverse_roots[0], right_inverse_roots[0], BACKWARD)
-    new_left, new_right = statistics(rows_of, named, arrived, factor_left[0], factor_right[0])
+    blocks = came.reshape(block_rows, block_size, block_size)
+    outs = updates(rows_of, blocks, left_inverse_roots[0], right_inverse_roots[0])
+    new_left, new_right = statistics(rows_of, named, blocks, factor_left[0], factor_right[0])
 
     returned = lax.all_to_all(
-        outs[0].reshape(num_shards, strip_rows, block_size),
+        outs.reshape(num_shards, strip_rows, block_size),
         "shard",
         split_axis=0,
         concat_axis=0,
@@ -310,11 +269,9 @@
     own_low, own_high = from_slots(later, returned)
     left_high, right_low = to_right(own_high), to_left(own_low)
     far_low, far_high = to_right(left_low), to_left(right_high)
-    update = place(
-        groups,
-        (own_low, own_high, left_low, left_high, right_low, right_high, far_low, far_high),
-        (strip_rows, columns),
-    )
+    near = (own_low, own_high, left_low, left_high, right_low, right_high)
+    update = place(groups[:3], near, (strip_rows, columns))
+    update = place(groups[3:], (far_low, far_high), (strip_rows, columns), (update,))
     return (new_left[None], new_right[None], update)
 
 

time: 149 us -> 146 us (0.980)
  waiting for transfers between devices: 35.8 us -> 33.3 us
    ppermute x6, waiting for transfers between devices: 27.1 us -> 24.7 us  [body(): to_right = lambda a: lax.ppermute(a, 'replica', onward)]
    pallas_call x1 -> x2, Pallas kernels: 2.44 us -> 3.69 us  [place(): pl.pallas_call(place_kernel, out_shape=jax.ShapeDtypeStruct(shape, jnp.bf...]
  transfers between devices with their start and end apart: 12 -> 12, of which waited for: 8 -> 7; matrix products, arithmetic and copies ran while one was open for 3% -> 4% of each run, Pallas kernels for 6% -> 8%
where the time goes in v3:
time: 146 us; the launch traced here: 145 us
  blocking collectives  67.7 us (46%)
  waiting for transfers between devices  33.3 us (23%)
  starting transfers between devices  18.1 us (12%)
  Pallas kernels  17.8 us (12%)
  local copies, waits for them, and re-layouts  6.61 us (5%)
    all_to_all x1, blocking collectives, body(): lax.all_to_all(slots, 'shard', split_axis=0, concat_axis=0, tiled=True)  35.5 us
    all_to_all x1, blocking collectives, body(): lax.all_to_all(outs.reshape(num_shards, strip_rows, block_size), 'shard',...  32.2 us
    ppermute x6, waiting for transfers between devices, body(): to_right = lambda a: lax.ppermute(a, 'replica', onward)  24.7 us
    ppermute x6, starting transfers between devices, body(): to_left = lambda a: lax.ppermute(a, 'replica', back)  14.4 us
    ppermute x6, waiting for transfers between devices, body(): to_left = lambda a: lax.ppermute(a, 'replica', back)  8.63 us
    pallas_call x1, Pallas kernels, statistics(): pl.pallas_call(gram_kernel, grid_spec=pltpu.PrefetchScalarGridSpec(num_sc...  6.55 us
    reshape x3, local copies, waits for them, and re-layouts, piece(): return part.reshape(rows, width)  5.87 us
    ppermute x6, starting transfers between devices, body(): to_right = lambda a: lax.ppermute(a, 'replica', onward)  3.7 us
  transfers between devices with their start and end apart: 12, of which 7 were waited for; matrix products, arithmetic and copies ran while one was open for 4% of the time, Pallas kernels for 8%

profile of v3, /device:TPU:0, one launch (start us, length us, event | category | flops | bytes accessed | tf_op | source)
XLA Modules:
  0.0 145.3 jit_solution(5038399936085632904)
XLA Ops:
  0.7 2.1 %dynamic-slice_bitcast_fusion.4 = (bf16[32,7168]{1,0:T(8,128)(2,1)}, bf16[32,7168]{1,0:T(8,128)(2,1)}) fusion(bf16[8,8,4,7168]{3,1,2,0:T(8,128)(2,1)} %bitcast.59, s32[]{:T(128)S(6)} %select_n.62), kind=kLoop, calls=%fused_computation.4 | loop fusion | bytes 1835012 | tf_op jit(solution)/shard_map/reshape | solution.py:236
  2.8 2.0 %collective-permute-start = (bf16[32,7168]{1,0:T(8,128)(2,1)}, bf16[32,7168]{1,0:T(8,128)(2,1)S(1)}, u32[]{:S(2)}, u32[]{:S(2)}) collective-permute-start(bf16[32,7168]{1,0:T(8,128)(2,1)} %get-tuple-element.23), channel_id=1, source_target_pairs={{0,32},{32,64},{64,96},{96,0},{1,33},{33,65},{65,97},{97,1},{2,34}... | collective-permute-start | bytes 1376264 | tf_op jit(solution)/shard_map/ppermute | solution.py:204
  4.8 2.1 %collective-permute-start.1 = (bf16[32,7168]{1,0:T(8,128)(2,1)}, bf16[32,7168]{1,0:T(8,128)(2,1)}, u32[]{:S(2)}, u32[]{:S(2)}) collective-permute-start(bf16[32,7168]{1,0:T(8,128)(2,1)} %get-tuple-element.24), channel_id=1, source_target_pairs={{0,96},{32,0},{64,32},{96,64},{1,97},{33,1},{65,33},{97,65},{2,98}... | collective-permute-start | bytes 1376264 | tf_op jit(solution)/shard_map/ppermute | solution.py:205
  6.9 2.5 %dynamic-slice_bitcast_fusion.1 = (bf16[32,7168]{1,0:T(8,128)(2,1)}, bf16[32,7168]{1,0:T(8,128)(2,1)}, bf16[32,7168]{1,0:T(8,128)(2,1)S(1)}, bf16[32,7168]{1,0:T(8,128)(2,1)S(1)}) fusion(bf16[8,8,4,7168]{3,1,2,0:T(8,128)(2,1)} %bitcast.60, s32[]{:T(128)S(6)} %select_n.73, s32[]{:T(128)S(6)} %select_n.64, s32[]{:T(128)S(6)} %select_n.63, s32[]{:T(128)S(6)} %select_n.59), kind=kLoop, calls=%fused_computation.1 | loop fusion | bytes 3670032 | tf_op jit(solution)/shard_map/reshape | solution.py:236
  9.4 2.0 %collective-permute-start.4 = (bf16[32,7168]{1,0:T(8,128)(2,1)}, bf16[32,7168]{1,0:T(8,128)(2,1)S(1)}, u32[]{:S(2)}, u32[]{:S(2)}) collective-permute-start(bf16[32,7168]{1,0:T(8,128)(2,1)} %get-tuple-element.46), channel_id=1, source_target_pairs={{0,96},{32,0},{64,32},{96,64},{1,97},{33,1},{65,33},{97,65},{2,98}... | collective-permute-start | bytes 1376264 | tf_op jit(solution)/shard_map/ppermute | solution.py:205
  11.5 0.3 compare_reduce_fusion.1
  12.0 1.2 dynamic-slice_bitcast_fusion.own
  13.3 5.2 %collective-permute-done.passed_right = bf16[32,7168]{1,0:T(8,128)(2,1)S(1)} collective-permute-done((bf16[32,7168]{1,0:T(8,128)(2,1)}, bf16[32,7168]{1,0:T(8,128)(2,1)S(1)}, u32[]{:S(2)}, u32[]{:S(2)}) %collective-permute-start) | collective-permute-done | bytes 458784 | tf_op jit(solution)/shard_map/ppermute | solution.py:204
  18.6 2.0 %relays.1 = (bf16[32,7168]{1,0:T(8,128)(2,1)}, bf16[32,7168]{1,0:T(8,128)(2,1)}) custom-call(bf16[32,7168]{1,0:T(8,128)(2,1)S(1)} %get-tuple-element.49.ahead, bf16[32,7168]{1,0:T(8,128)(2,1)S(1)} %collective-permute-done.passed_right, bf16[32,7168]{1,0:T(8,128)(2,1)S(1)} %get-tuple-element.48.behind, bf16[32,7168]{1,0:T(8,128)(2,1)} %collective-permute-done.1.passed_left), custom_call_target="tpu_custom_call" | custom-call | flops 30000001024 | bytes 2752512 | tf_op jit(solution)/shard_map/relays/pallas_call | solution.py:34
  20.6 3.3 %collective-permute-start.2 = (bf16[32,7168]{1,0:T(8,128)(2,1)}, bf16[32,7168]{1,0:T(8,128)(2,1)S(1)}, u32[]{:S(2)}, u32[]{:S(2)}) collective-permute-start(bf16[32,7168]{1,0:T(8,128)(2,1)} %get-tuple-element.25), channel_id=1, source_target_pairs={{0,96},{32,0},{64,32},{96,64},{1,97},{33,1},{65,33},{97,65},{2,98}... | collective-permute-start | bytes 1376264 | tf_op jit(solution)/shard_map/ppermute | solution.py:205
  23.9 0.2 reduce-window.17
  24.3 0.2 select_reduce_fusion.rows_of
  24.5 3.9 %collective-permute-done.3.high_b = bf16[32,7168]{1,0:T(8,128)(2,1)S(1)} collective-permute-done((bf16[32,7168]{1,0:T(8,128)(2,1)}, bf16[32,7168]{1,0:T(8,128)(2,1)S(1)}, u32[]{:S(2)}, u32[]{:S(2)}) %collective-permute-start.3) | collective-permute-done | bytes 458784 | tf_op jit(solution)/shard_map/ppermute | solution.py:204
  28.3 8.5 %collective-permute-done.2.high_a = bf16[32,7168]{1,0:T(8,128)(2,1)S(1)} collective-permute-done((bf16[32,7168]{1,0:T(8,128)(2,1)}, bf16[32,7168]{1,0:T(8,128)(2,1)S(1)}, u32[]{:S(2)}, u32[]{:S(2)}) %collective-permute-start.2) | collective-permute-done | bytes 458784 | tf_op jit(solution)/shard_map/ppermute | solution.py:205
  36.9 0.5 collective-permute-done.5.low_b
  37.3 0.9 to_slots.1
  38.2 35.5 %all_to_all.10 = bf16[32,64,512]{2,1,0:T(8,128)(2,1)} all-to-all(bf16[32,64,512]{2,1,0:T(8,128)(2,1)S(1)} %to_slots.1), channel_id=1, replica_groups=mesh['replica'=4,'shard'=32] {'shard'}, dimensions={0} | all-to-all | bytes 4194304 | tf_op jit(solution)/shard_map/all_to_all | solution.py:254
  73.8 3.4 %updates.1 = bf16[4,512,512]{2,1,0:T(8,128)(2,1)S(1)} custom-call(s32[3]{0:T(128)S(1)} %select_reduce_fusion.rows_of, bf16[4,512,512]{2,1,0:T(8,128)(2,1)} %bitcast.52, bf16[3,512,512]{2,1,0:T(8,128)(2,1)S(1)} %bitcast.56, bf16[3,512,512]{2,1,0:T(8,128)(2,1)S(1)} %bitcast.57), custom_call_target="tpu_custom_call" | custom-call | flops 1610612736 | bytes 6291456 | tf_op jit(solution)/shard_map/updates/pallas_call | solution.py:87
  77.2 32.2 %all_to_all.11.slots = bf16[32,64,512]{2,1,0:T(8,128)(2,1)S(1)} all-to-all(bf16[32,64,512]{2,1,0:T(8,128)(2,1)S(1)} %bitcast.54), channel_id=1, replica_groups=mesh['replica'=4,'shard'=32] {'shard'}, dimensions={0} | all-to-all | bytes 4194304 | tf_op jit(solution)/shard_map/all_to_all | solution.py:259
  109.4 0.6 from_slots.2
  110.0 1.4 collective-permute-start.6
  111.3 2.0 %collective-permute-start.8 = (bf16[64,3584]{1,0:T(8,128)(2,1)S(1)}, bf16[64,3584]{1,0:T(8,128)(2,1)S(1)}, u32[]{:S(2)}, u32[]{:S(2)}) collective-permute-start(bf16[64,3584]{1,0:T(8,128)(2,1)S(1)} %get-tuple-element.39), channel_id=1, source_target_pairs={{0,96},{32,0},{64,32},{96,64},{1,97},{33,1},{65,33},{97,65},{2,98}... | collective-permute-start | bytes 1376264 | tf_op jit(solution)/shard_map/ppermute | solution.py:205
  113.3 0.6 from_slots.3
  113.9 1.8 %collective-permute-start.11 = (bf16[64,3584]{1,0:T(8,128)(2,1)S(1)}, bf16[64,3584]{1,0:T(8,128)(2,1)S(1)}, u32[]{:S(2)}, u32[]{:S(2)}) collective-permute-start(bf16[64,3584]{1,0:T(8,128)(2,1)S(1)} %get-tuple-element.41.refs_0_), channel_id=1, source_target_pairs={{0,96},{32,0},{64,32},{96,64},{1,97},{33,1},{65,33},{97,65},{2,98}... | collective-permute-start | bytes 1376264 | tf_op jit(solution)/shard_map/ppermute | solution.py:205
  115.7 0.3 collective-permute-start.10
  116.0 8.6 %collective-permute-done.6.refs_2_ = bf16[64,3584]{1,0:T(8,128)(2,1)S(1)} collective-permute-done((bf16[64,3584]{1,0:T(8,128)(2,1)S(1)}, bf16[64,3584]{1,0:T(8,128)(2,1)S(1)}, u32[]{:S(2)}, u32[]{:S(2)}) %collective-permute-start.6) | collective-permute-done | bytes 458784 | tf_op jit(solution)/shard_map/ppermute | solution.py:204
  124.7 3.2 %collective-permute-start.9 = (bf16[64,3584]{1,0:T(8,128)(2,1)S(1)}, bf16[64,3584]{1,0:T(8,128)(2,1)S(1)}, u32[]{:S(2)}, u32[]{:S(2)}) collective-permute-start(bf16[64,3584]{1,0:T(8,128)(2,1)S(1)} %collective-permute-done.8.refs_5_), channel_id=1, source_target_pairs={{0,96},{32,0},{64,32},{96,64},{1,97},{33,1},{65,33},{97,65},{2,98}... | collective-permute-start | bytes 1376264 | tf_op jit(solution)/shard_map/ppermute | solution.py:205
  127.9 0.6 slice.6.groups
  128.5 6.5 %statistics.1 = (f32[3,512,512]{2,1,0:T(8,128)}, f32[3,512,512]{2,1,0:T(8,128)}) custom-call(s32[3]{0:T(128)S(1)} %select_reduce_fusion.rows_of, s32[3]{0:T(128)S(1)} %get-tuple-element.28.named, bf16[4,512,512]{2,1,0:T(8,128)(2,1)S(1)} %bitcast.53, f32[3,512,512]{2,1,0:T(8,128)S(1)} %bitcast.55, f32[3,512,512]{2,1,0:T(8,128)} %bitcast.62), custom_call_target="tpu_custom_call" | custom-call | flops 1610612736 | bytes 14155776 | tf_op jit(solution)/shard_map/statistics/pallas_call | solution.py:116
  135.1 2.1 %place.2.refs_2_ = bf16[64,28672]{1,0:T(8,128)(2,1)} custom-call(s32[3]{0:T(128)S(1)} %bitcast.58, bf16[64,3584]{1,0:T(8,128)(2,1)S(1)} %get-tuple-element.41.refs_0_, bf16[64,3584]{1,0:T(8,128)(2,1)S(1)} %get-tuple-element.42.refs_1_, bf16[64,3584]{1,0:T(8,128)(2,1)S(1)} %collective-permute-done.6.refs_2_, ...), custom_call_target="tpu_custom_call" | custom-call | bytes 5505024 | tf_op jit(solution)/shard_map/place/pallas_call | solution.py:172
  137.2 6.5 %collective-permute-done.7.refs_0_ = bf16[64,3584]{1,0:T(8,128)(2,1)S(1)} collective-permute-done((bf16[64,3584]{1,0:T(8,128)(2,1)S(1)}, bf16[64,3584]{1,0:T(8,128)(2,1)S(1)}, u32[]{:S(2)}, u32[]{:S(2)}) %collective-permute-start.7) | collective-permute-done | bytes 458784 | tf_op jit(solution)/shard_map/ppermute | solution.py:204
  143.7 1.6 %place.3 = bf16[64,28672]{1,0:T(8,128)(2,1)} custom-call(s32[1]{0:T(128)} %slice.6.groups, bf16[64,3584]{1,0:T(8,128)(2,1)S(1)} %collective-permute-done.7.refs_0_, bf16[64,3584]{1,0:T(8,128)(2,1)S(1)} %collective-permute-done.9.refs_1_, bf16[64,28672]{1,0:T(8,128)(2,1)} %place.2.refs_2_), custom_call_target="tpu_custom_call", output_to_operand_aliasing={{}: (3, {})} | custom-call | bytes 1835008 | tf_op jit(solution)/shard_map/place/pallas_call | solution.py:172
  (26 shorter events, 0.6 us)
Async XLA Ops:
  0.6 10.8 %copy-start.4 = (s32[4,56]{1,0:T(4,128)S(1)}, s32[4,56]{1,0:T(4,128)}, u32[]{:S(2)}) copy-start(s32[4,56]{1,0:T(4,128)} %param.7) | copy-start | bytes 2692
  2.8 15.7 %collective-permute-start = (bf16[32,7168]{1,0:T(8,128)(2,1)}, bf16[32,7168]{1,0:T(8,128)(2,1)S(1)}, u32[]{:S(2)}, u32[]{:S(2)}) collective-permute-start(bf16[32,7168]{1,0:T(8,128)(2,1)} %get-tuple-element.23), channel_id=1, source_target_pairs={{0,32},{32,64},{64,96},{96,0},{1,33},{33,65},{65,97},{97,1},{2,34}... | collective-permute-start | bytes 1376264 | tf_op jit(solution)/shard_map/ppermute | solution.py:204
  4.8 13.7 %collective-permute-start.1 = (bf16[32,7168]{1,0:T(8,128)(2,1)}, bf16[32,7168]{1,0:T(8,128)(2,1)}, u32[]{:S(2)}, u32[]{:S(2)}) collective-permute-start(bf16[32,7168]{1,0:T(8,128)(2,1)} %get-tuple-element.24), channel_id=1, source_target_pairs={{0,96},{32,0},{64,32},{96,64},{1,97},{33,1},{65,33},{97,65},{2,98}... | collective-permute-start | bytes 1376264 | tf_op jit(solution)/shard_map/ppermute | solution.py:205
  9.4 27.4 %collective-permute-start.4 = (bf16[32,7168]{1,0:T(8,128)(2,1)}, bf16[32,7168]{1,0:T(8,128)(2,1)S(1)}, u32[]{:S(2)}, u32[]{:S(2)}) collective-permute-start(bf16[32,7168]{1,0:T(8,128)(2,1)} %get-tuple-element.46), channel_id=1, source_target_pairs={{0,96},{32,0},{64,32},{96,64},{1,97},{33,1},{65,33},{97,65},{2,98}... | collective-permute-start | bytes 1376264 | tf_op jit(solution)/shard_map/ppermute | solution.py:205
  11.5 16.9 %collective-permute-start.3 = (bf16[32,7168]{1,0:T(8,128)(2,1)}, bf16[32,7168]{1,0:T(8,128)(2,1)S(1)}, u32[]{:S(2)}, u32[]{:S(2)}) collective-permute-start(bf16[32,7168]{1,0:T(8,128)(2,1)} %get-tuple-element.47), channel_id=1, source_target_pairs={{0,32},{32,64},{64,96},{96,0},{1,33},{33,65},{65,97},{97,1},{2,34}... | collective-permute-start | bytes 1376264 | tf_op jit(solution)/shard_map/ppermute | solution.py:204
  20.6 16.2 %collective-permute-start.2 = (bf16[32,7168]{1,0:T(8,128)(2,1)}, bf16[32,7168]{1,0:T(8,128)(2,1)S(1)}, u32[]{:S(2)}, u32[]{:S(2)}) collective-permute-start(bf16[32,7168]{1,0:T(8,128)(2,1)} %get-tuple-element.25), channel_id=1, source_target_pairs={{0,96},{32,0},{64,32},{96,64},{1,97},{33,1},{65,33},{97,65},{2,98}... | collective-permute-start | bytes 1376264 | tf_op jit(solution)/shard_map/ppermute | solution.py:205
  23.9 13.4 %collective-permute-start.5 = (bf16[32,7168]{1,0:T(8,128)(2,1)}, bf16[32,7168]{1,0:T(8,128)(2,1)S(1)}, u32[]{:S(2)}, u32[]{:S(2)}) collective-permute-start(bf16[32,7168]{1,0:T(8,128)(2,1)} %get-tuple-element.30), channel_id=1, source_target_pairs={{0,32},{32,64},{64,96},{96,0},{1,33},{33,65},{65,97},{97,1},{2,34}... | collective-permute-start | bytes 1376264 | tf_op jit(solution)/shard_map/ppermute | solution.py:204
  38.2 35.6 %copy-start.2 = (bf16[1,3,512,512]{3,2,1,0:T(8,128)(2,1)S(1)}, bf16[1,3,512,512]{3,2,1,0:T(8,128)(2,1)}, u32[]{:S(2)}) copy-start(bf16[1,3,512,512]{3,2,1,0:T(8,128)(2,1)} %param.10) | copy-start | bytes 4718596
  38.2 35.6 %copy-start.3 = (bf16[1,3,512,512]{3,2,1,0:T(8,128)(2,1)S(1)}, bf16[1,3,512,512]{3,2,1,0:T(8,128)(2,1)}, u32[]{:S(2)}) copy-start(bf16[1,3,512,512]{3,2,1,0:T(8,128)(2,1)} %param.11) | copy-start | bytes 4718596
  77.2 51.3 %copy-start.1 = (f32[1,3,512,512]{3,2,1,0:T(8,128)S(1)}, f32[1,3,512,512]{3,2,1,0:T(8,128)}, u32[]{:S(2)}) copy-start(f32[1,3,512,512]{3,2,1,0:T(8,128)} %param.8) | copy-start | bytes 9437188
  109.4 19.2 %copy-start = (bf16[32,64,512]{2,1,0:T(8,128)(2,1)S(1)}, bf16[32,64,512]{2,1,0:T(8,128)(2,1)}, u32[]{:S(2)}) copy-start(bf16[32,64,512]{2,1,0:T(8,128)(2,1)} %all_to_all.10) | copy-start | bytes 6291460
  110.0 14.6 %collective-permute-start.6 = (bf16[64,3584]{1,0:T(8,128)(2,1)S(1)}, bf16[64,3584]{1,0:T(8,128)(2,1)S(1)}, u32[]{:S(2)}, u32[]{:S(2)}) collective-permute-start(bf16[64,3584]{1,0:T(8,128)(2,1)S(1)} %get-tuple-element.38), channel_id=1, source_target_pairs={{0,32},{32,64},{64,96},{96,0},{1,33},{33,65},{65,97},{97,1},{2,34}... | collective-permute-start | bytes 1376264 | tf_op jit(solution)/shard_map/ppermute | solution.py:204
  111.3 13.4 %collective-permute-start.8 = (bf16[64,3584]{1,0:T(8,128)(2,1)S(1)}, bf16[64,3584]{1,0:T(8,128)(2,1)S(1)}, u32[]{:S(2)}, u32[]{:S(2)}) collective-permute-start(bf16[64,3584]{1,0:T(8,128)(2,1)S(1)} %get-tuple-element.39), channel_id=1, source_target_pairs={{0,96},{32,0},{64,32},{96,64},{1,97},{33,1},{65,33},{97,65},{2,98}... | collective-permute-start | bytes 1376264 | tf_op jit(solution)/shard_map/ppermute | solution.py:205
  113.9 21.2 %collective-permute-start.11 = (bf16[64,3584]{1,0:T(8,128)(2,1)S(1)}, bf16[64,3584]{1,0:T(8,128)(2,1)S(1)}, u32[]{:S(2)}, u32[]{:S(2)}) collective-permute-start(bf16[64,3584]{1,0:T(8,128)(2,1)S(1)} %get-tuple-element.41.refs_0_), channel_id=1, source_target_pairs={{0,96},{32,0},{64,32},{96,64},{1,97},{33,1},{65,33},{97,65},{2,98}... | collective-permute-start | bytes 1376264 | tf_op jit(solution)/shard_map/ppermute | solution.py:205
  115.7 19.3 %collective-permute-start.10 = (bf16[64,3584]{1,0:T(8,128)(2,1)S(1)}, bf16[64,3584]{1,0:T(8,128)(2,1)S(1)}, u32[]{:S(2)}, u32[]{:S(2)}) collective-permute-start(bf16[64,3584]{1,0:T(8,128)(2,1)S(1)} %get-tuple-element.42.refs_1_), channel_id=1, source_target_pairs={{0,32},{32,64},{64,96},{96,0},{1,33},{33,65},{65,97},{97,1},{2,34}... | collective-permute-start | bytes 1376264 | tf_op jit(solution)/shard_map/ppermute | solution.py:204
  124.6 19.1 %collective-permute-start.7 = (bf16[64,3584]{1,0:T(8,128)(2,1)S(1)}, bf16[64,3584]{1,0:T(8,128)(2,1)S(1)}, u32[]{:S(2)}, u32[]{:S(2)}) collective-permute-start(bf16[64,3584]{1,0:T(8,128)(2,1)S(1)} %collective-permute-done.6.refs_2_), channel_id=1, source_target_pairs={{0,32},{32,64},{64,96},{96,0},{1,33},{33,65},{65,97},{97,1},{2,34}... | collective-permute-start | bytes 1376264 | tf_op jit(solution)/shard_map/ppermute | solution.py:204
  124.7 19.0 %collective-permute-start.9 = (bf16[64,3584]{1,0:T(8,128)(2,1)S(1)}, bf16[64,3584]{1,0:T(8,128)(2,1)S(1)}, u32[]{:S(2)}, u32[]{:S(2)}) collective-permute-start(bf16[64,3584]{1,0:T(8,128)(2,1)S(1)} %collective-permute-done.8.refs_5_), channel_id=1, source_target_pairs={{0,96},{32,0},{64,32},{96,64},{1,97},{33,1},{65,33},{97,65},{2,98}... | collective-permute-start | bytes 1376264 | tf_op jit(solution)/shard_map/ppermute | solution.py:205

commit v4 on v3

--- a/solution.py
+++ b/solution.py
@@ -18,7 +18,7 @@
     return pl.BlockSpec(memory_space=pltpu.VMEM)
 
 
-def params(mib=48):
+def params(mib=16):
     return pltpu.CompilerParams(vmem_limit_bytes=mib * 1024 * 1024)
 
 

time: 146 us -> 145 us (level)
  Pallas kernels: 17.8 us -> 14.5 us
  waiting for transfers between devices: 33.3 us -> 35.6 us
    pallas_call x1, Pallas kernels: 6.55 us -> 4.33 us  [statistics(): pl.pallas_call(gram_kernel, grid_spec=pltpu.PrefetchScalarGridSpec(num_sc...]
    ppermute x6, waiting for transfers between devices: 8.63 us -> 10.3 us  [body(): to_left = lambda a: lax.ppermute(a, 'replica', back)]
  transfers between devices with their start and end apart: 12 -> 12, of which waited for: 7 -> 8; matrix products, arithmetic and copies ran while one was open for 4% -> 4% of each run, Pallas kernels for 8% -> 6%
where the time goes in v4:
time: 145 us; the launch traced here: 144 us
  blocking collectives  67.6 us (47%)
  waiting for transfers between devices  35.6 us (25%)
  starting transfers between devices  18.1 us (12%)
  Pallas kernels  14.5 us (10%)
  local copies, waits for them, and re-layouts  6.62 us (5%)
    all_to_all x1, blocking collectives, body(): lax.all_to_all(slots, 'shard', split_axis=0, concat_axis=0, tiled=True)  35.4 us
    all_to_all x1, blocking collectives, body(): lax.all_to_all(outs.reshape(num_shards, strip_rows, block_size), 'shard',...  32.2 us
    ppermute x6, waiting for transfers between devices, body(): to_right = lambda a: lax.ppermute(a, 'replica', onward)  25.2 us
    ppermute x6, starting transfers between devices, body(): to_left = lambda a: lax.ppermute(a, 'replica', back)  14.4 us
    ppermute x6, waiting for transfers between devices, body(): to_left = lambda a: lax.ppermute(a, 'replica', back)  10.3 us
    reshape x3, local copies, waits for them, and re-layouts, piece(): return part.reshape(rows, width)  5.87 us
    pallas_call x1, Pallas kernels, statistics(): pl.pallas_call(gram_kernel, grid_spec=pltpu.PrefetchScalarGridSpec(num_sc...  4.33 us
    pallas_call x2, Pallas kernels, place(): pl.pallas_call(place_kernel, out_shape=jax.ShapeDtypeStruct(shape, jnp.bf...  3.74 us
  transfers between devices with their start and end apart: 12, of which 8 were waited for; matrix products, arithmetic and copies ran while one was open for 4% of the time, Pallas kernels for 6%

profile of v4, /device:TPU:0, one launch (start us, length us, event | category | flops | bytes accessed | tf_op | source)
XLA Modules:
  0.0 144.2 jit_solution(7088607727793740581)
XLA Ops:
  0.7 2.1 %dynamic-slice_bitcast_fusion.4 = (bf16[32,7168]{1,0:T(8,128)(2,1)}, bf16[32,7168]{1,0:T(8,128)(2,1)}) fusion(bf16[8,8,4,7168]{3,1,2,0:T(8,128)(2,1)} %bitcast.60, s32[]{:T(128)S(6)} %select_n.62), kind=kLoop, calls=%fused_computation.4 | loop fusion | bytes 1835012 | tf_op jit(solution)/shard_map/reshape | solution.py:236
  2.8 2.0 %collective-permute-start = (bf16[32,7168]{1,0:T(8,128)(2,1)}, bf16[32,7168]{1,0:T(8,128)(2,1)S(1)}, u32[]{:S(2)}, u32[]{:S(2)}) collective-permute-start(bf16[32,7168]{1,0:T(8,128)(2,1)} %get-tuple-element.23), channel_id=1, source_target_pairs={{0,32},{32,64},{64,96},{96,0},{1,33},{33,65},{65,97},{97,1},{2,34}... | collective-permute-start | bytes 1376264 | tf_op jit(solution)/shard_map/ppermute | solution.py:204
  4.8 2.1 %collective-permute-start.1 = (bf16[32,7168]{1,0:T(8,128)(2,1)}, bf16[32,7168]{1,0:T(8,128)(2,1)}, u32[]{:S(2)}, u32[]{:S(2)}) collective-permute-start(bf16[32,7168]{1,0:T(8,128)(2,1)} %get-tuple-element.24), channel_id=1, source_target_pairs={{0,96},{32,0},{64,32},{96,64},{1,97},{33,1},{65,33},{97,65},{2,98}... | collective-permute-start | bytes 1376264 | tf_op jit(solution)/shard_map/ppermute | solution.py:205
  6.9 2.5 %dynamic-slice_bitcast_fusion.1 = (bf16[32,7168]{1,0:T(8,128)(2,1)}, bf16[32,7168]{1,0:T(8,128)(2,1)}, bf16[32,7168]{1,0:T(8,128)(2,1)S(1)}, bf16[32,7168]{1,0:T(8,128)(2,1)S(1)}) fusion(bf16[8,8,4,7168]{3,1,2,0:T(8,128)(2,1)} %bitcast.61, s32[]{:T(128)S(6)} %select_n.73, s32[]{:T(128)S(6)} %select_n.64, s32[]{:T(128)S(6)} %select_n.63, s32[]{:T(128)S(6)} %select_n.59), kind=kLoop, calls=%fused_computation.1 | loop fusion | bytes 3670032 | tf_op jit(solution)/shard_map/reshape | solution.py:236
  9.4 2.0 %collective-permute-start.4 = (bf16[32,7168]{1,0:T(8,128)(2,1)}, bf16[32,7168]{1,0:T(8,128)(2,1)S(1)}, u32[]{:S(2)}, u32[]{:S(2)}) collective-permute-start(bf16[32,7168]{1,0:T(8,128)(2,1)} %get-tuple-element.46), channel_id=1, source_target_pairs={{0,96},{32,0},{64,32},{96,64},{1,97},{33,1},{65,33},{97,65},{2,98}... | collective-permute-start | bytes 1376264 | tf_op jit(solution)/shard_map/ppermute | solution.py:205
  11.5 0.3 compare_reduce_fusion.1
  12.0 1.2 dynamic-slice_bitcast_fusion.own
  13.3 5.2 %collective-permute-done.passed_right = bf16[32,7168]{1,0:T(8,128)(2,1)S(1)} collective-permute-done((bf16[32,7168]{1,0:T(8,128)(2,1)}, bf16[32,7168]{1,0:T(8,128)(2,1)S(1)}, u32[]{:S(2)}, u32[]{:S(2)}) %collective-permute-start) | collective-permute-done | bytes 458784 | tf_op jit(solution)/shard_map/ppermute | solution.py:204
  18.6 2.0 %relays.1 = (bf16[32,7168]{1,0:T(8,128)(2,1)}, bf16[32,7168]{1,0:T(8,128)(2,1)}) custom-call(bf16[32,7168]{1,0:T(8,128)(2,1)S(1)} %get-tuple-element.49.ahead, bf16[32,7168]{1,0:T(8,128)(2,1)S(1)} %collective-permute-done.passed_right, bf16[32,7168]{1,0:T(8,128)(2,1)S(1)} %get-tuple-element.48.behind, bf16[32,7168]{1,0:T(8,128)(2,1)} %collective-permute-done.1.passed_left), custom_call_target="tpu_custom_call" | custom-call | flops 30000001024 | bytes 2752512 | tf_op jit(solution)/shard_map/relays/pallas_call | solution.py:34
  20.6 3.3 %collective-permute-start.2 = (bf16[32,7168]{1,0:T(8,128)(2,1)}, bf16[32,7168]{1,0:T(8,128)(2,1)S(1)}, u32[]{:S(2)}, u32[]{:S(2)}) collective-permute-start(bf16[32,7168]{1,0:T(8,128)(2,1)} %get-tuple-element.25), channel_id=1, source_target_pairs={{0,96},{32,0},{64,32},{96,64},{1,97},{33,1},{65,33},{97,65},{2,98}... | collective-permute-start | bytes 1376264 | tf_op jit(solution)/shard_map/ppermute | solution.py:205
  24.3 0.2 select_reduce_fusion.rows_of
  24.5 3.9 %collective-permute-done.3.high_b = bf16[32,7168]{1,0:T(8,128)(2,1)S(1)} collective-permute-done((bf16[32,7168]{1,0:T(8,128)(2,1)}, bf16[32,7168]{1,0:T(8,128)(2,1)S(1)}, u32[]{:S(2)}, u32[]{:S(2)}) %collective-permute-start.3) | collective-permute-done | bytes 458784 | tf_op jit(solution)/shard_map/ppermute | solution.py:204
  28.3 8.5 %collective-permute-done.2.high_a = bf16[32,7168]{1,0:T(8,128)(2,1)S(1)} collective-permute-done((bf16[32,7168]{1,0:T(8,128)(2,1)}, bf16[32,7168]{1,0:T(8,128)(2,1)S(1)}, u32[]{:S(2)}, u32[]{:S(2)}) %collective-permute-start.2) | collective-permute-done | bytes 458784 | tf_op jit(solution)/shard_map/ppermute | solution.py:205
  36.9 0.5 collective-permute-done.5.low_b
  37.3 0.9 to_slots.1
  38.2 35.4 %all_to_all.10 = bf16[32,64,512]{2,1,0:T(8,128)(2,1)S(1)} all-to-all(bf16[32,64,512]{2,1,0:T(8,128)(2,1)S(1)} %to_slots.1), channel_id=1, replica_groups=mesh['replica'=4,'shard'=32] {'shard'}, dimensions={0} | all-to-all | bytes 4194304 | tf_op jit(solution)/shard_map/all_to_all | solution.py:254
  73.7 2.3 %updates.1 = bf16[4,512,512]{2,1,0:T(8,128)(2,1)S(1)} custom-call(s32[3]{0:T(128)S(1)} %select_reduce_fusion.rows_of, bf16[4,512,512]{2,1,0:T(8,128)(2,1)S(1)} %bitcast.52, bf16[3,512,512]{2,1,0:T(8,128)(2,1)S(1)} %bitcast.57, bf16[3,512,512]{2,1,0:T(8,128)(2,1)S(1)} %bitcast.58), custom_call_target="tpu_custom_call" | custom-call | flops 1610612736 | bytes 6291456 | tf_op jit(solution)/shard_map/updates/pallas_call | solution.py:87
  76.0 32.2 %all_to_all.11.slots = bf16[32,64,512]{2,1,0:T(8,128)(2,1)S(1)} all-to-all(bf16[32,64,512]{2,1,0:T(8,128)(2,1)S(1)} %bitcast.54), channel_id=1, replica_groups=mesh['replica'=4,'shard'=32] {'shard'}, dimensions={0} | all-to-all | bytes 4194304 | tf_op jit(solution)/shard_map/all_to_all | solution.py:259
  108.2 0.6 from_slots.2
  108.8 1.4 collective-permute-start.6
  110.2 2.0 %collective-permute-start.8 = (bf16[64,3584]{1,0:T(8,128)(2,1)S(1)}, bf16[64,3584]{1,0:T(8,128)(2,1)S(1)}, u32[]{:S(2)}, u32[]{:S(2)}) collective-permute-start(bf16[64,3584]{1,0:T(8,128)(2,1)S(1)} %get-tuple-element.39), channel_id=1, source_target_pairs={{0,96},{32,0},{64,32},{96,64},{1,97},{33,1},{65,33},{97,65},{2,98}... | collective-permute-start | bytes 1376264 | tf_op jit(solution)/shard_map/ppermute | solution.py:205
  112.1 0.6 from_slots.3
  112.7 1.8 %collective-permute-start.11 = (bf16[64,3584]{1,0:T(8,128)(2,1)S(1)}, bf16[64,3584]{1,0:T(8,128)(2,1)S(1)}, u32[]{:S(2)}, u32[]{:S(2)}) collective-permute-start(bf16[64,3584]{1,0:T(8,128)(2,1)S(1)} %get-tuple-element.41.refs_0_), channel_id=1, source_target_pairs={{0,96},{32,0},{64,32},{96,64},{1,97},{33,1},{65,33},{97,65},{2,98}... | collective-permute-start | bytes 1376264 | tf_op jit(solution)/shard_map/ppermute | solution.py:205
  114.6 0.3 collective-permute-start.10
  114.8 8.6 %collective-permute-done.6.refs_2_ = bf16[64,3584]{1,0:T(8,128)(2,1)S(1)} collective-permute-done((bf16[64,3584]{1,0:T(8,128)(2,1)S(1)}, bf16[64,3584]{1,0:T(8,128)(2,1)S(1)}, u32[]{:S(2)}, u32[]{:S(2)}) %collective-permute-start.6) | collective-permute-done | bytes 458784 | tf_op jit(solution)/shard_map/ppermute | solution.py:204
  123.5 3.2 %collective-permute-start.9 = (bf16[64,3584]{1,0:T(8,128)(2,1)S(1)}, bf16[64,3584]{1,0:T(8,128)(2,1)S(1)}, u32[]{:S(2)}, u32[]{:S(2)}) collective-permute-start(bf16[64,3584]{1,0:T(8,128)(2,1)S(1)} %collective-permute-done.8.refs_5_), channel_id=1, source_target_pairs={{0,96},{32,0},{64,32},{96,64},{1,97},{33,1},{65,33},{97,65},{2,98}... | collective-permute-start | bytes 1376264 | tf_op jit(solution)/shard_map/ppermute | solution.py:205
  126.7 0.6 slice.6.groups
  127.3 4.3 %statistics.1 = (f32[3,512,512]{2,1,0:T(8,128)}, f32[3,512,512]{2,1,0:T(8,128)}) custom-call(s32[3]{0:T(128)S(1)} %select_reduce_fusion.rows_of, s32[3]{0:T(128)S(1)} %get-tuple-element.28.named, bf16[4,512,512]{2,1,0:T(8,128)(2,1)S(1)} %bitcast.53, f32[3,512,512]{2,1,0:T(8,128)S(1)} %bitcast.55, f32[3,512,512]{2,1,0:T(8,128)S(1)} %bitcast.56), custom_call_target="tpu_custom_call" | custom-call | flops 1610612736 | bytes 14155776 | tf_op jit(solution)/shard_map/statistics/pallas_call | solution.py:116
  131.7 1.7 %collective-permute-done.11.refs_4_ = bf16[64,3584]{1,0:T(8,128)(2,1)S(1)} collective-permute-done((bf16[64,3584]{1,0:T(8,128)(2,1)S(1)}, bf16[64,3584]{1,0:T(8,128)(2,1)S(1)}, u32[]{:S(2)}, u32[]{:S(2)}) %collective-permute-start.11) | collective-permute-done | bytes 458784 | tf_op jit(solution)/shard_map/ppermute | solution.py:205
  133.4 2.1 %place.2.refs_2_ = bf16[64,28672]{1,0:T(8,128)(2,1)} custom-call(s32[3]{0:T(128)S(1)} %bitcast.59, bf16[64,3584]{1,0:T(8,128)(2,1)S(1)} %get-tuple-element.41.refs_0_, bf16[64,3584]{1,0:T(8,128)(2,1)S(1)} %get-tuple-element.42.refs_1_, bf16[64,3584]{1,0:T(8,128)(2,1)S(1)} %collective-permute-done.6.refs_2_, ...), custom_call_target="tpu_custom_call" | custom-call | bytes 5505024 | tf_op jit(solution)/shard_map/place/pallas_call | solution.py:172
  135.5 7.1 %collective-permute-done.7.refs_0_ = bf16[64,3584]{1,0:T(8,128)(2,1)S(1)} collective-permute-done((bf16[64,3584]{1,0:T(8,128)(2,1)S(1)}, bf16[64,3584]{1,0:T(8,128)(2,1)S(1)}, u32[]{:S(2)}, u32[]{:S(2)}) %collective-permute-start.7) | collective-permute-done | bytes 458784 | tf_op jit(solution)/shard_map/ppermute | solution.py:204
  142.6 1.6 %place.3 = bf16[64,28672]{1,0:T(8,128)(2,1)} custom-call(s32[1]{0:T(128)} %slice.6.groups, bf16[64,3584]{1,0:T(8,128)(2,1)S(1)} %collective-permute-done.7.refs_0_, bf16[64,3584]{1,0:T(8,128)(2,1)S(1)} %collective-permute-done.9.refs_1_, bf16[64,28672]{1,0:T(8,128)(2,1)} %place.2.refs_2_), custom_call_target="tpu_custom_call", output_to_operand_aliasing={{}: (3, {})} | custom-call | bytes 1835008 | tf_op jit(solution)/shard_map/place/pallas_call | solution.py:172
  (26 shorter events, 0.8 us)
Async XLA Ops:
  0.6 10.8 %copy-start.4 = (s32[4,56]{1,0:T(4,128)S(1)}, s32[4,56]{1,0:T(4,128)}, u32[]{:S(2)}) copy-start(s32[4,56]{1,0:T(4,128)} %param.7) | copy-start | bytes 2692
  2.8 15.7 %collective-permute-start = (bf16[32,7168]{1,0:T(8,128)(2,1)}, bf16[32,7168]{1,0:T(8,128)(2,1)S(1)}, u32[]{:S(2)}, u32[]{:S(2)}) collective-permute-start(bf16[32,7168]{1,0:T(8,128)(2,1)} %get-tuple-element.23), channel_id=1, source_target_pairs={{0,32},{32,64},{64,96},{96,0},{1,33},{33,65},{65,97},{97,1},{2,34}... | collective-permute-start | bytes 1376264 | tf_op jit(solution)/shard_map/ppermute | solution.py:204
  4.8 13.7 %collective-permute-start.1 = (bf16[32,7168]{1,0:T(8,128)(2,1)}, bf16[32,7168]{1,0:T(8,128)(2,1)}, u32[]{:S(2)}, u32[]{:S(2)}) collective-permute-start(bf16[32,7168]{1,0:T(8,128)(2,1)} %get-tuple-element.24), channel_id=1, source_target_pairs={{0,96},{32,0},{64,32},{96,64},{1,97},{33,1},{65,33},{97,65},{2,98}... | collective-permute-start | bytes 1376264 | tf_op jit(solution)/shard_map/ppermute | solution.py:205
  9.4 27.4 %collective-permute-start.4 = (bf16[32,7168]{1,0:T(8,128)(2,1)}, bf16[32,7168]{1,0:T(8,128)(2,1)S(1)}, u32[]{:S(2)}, u32[]{:S(2)}) collective-permute-start(bf16[32,7168]{1,0:T(8,128)(2,1)} %get-tuple-element.46), channel_id=1, source_target_pairs={{0,96},{32,0},{64,32},{96,64},{1,97},{33,1},{65,33},{97,65},{2,98}... | collective-permute-start | bytes 1376264 | tf_op jit(solution)/shard_map/ppermute | solution.py:205
  11.5 16.9 %collective-permute-start.3 = (bf16[32,7168]{1,0:T(8,128)(2,1)}, bf16[32,7168]{1,0:T(8,128)(2,1)S(1)}, u32[]{:S(2)}, u32[]{:S(2)}) collective-permute-start(bf16[32,7168]{1,0:T(8,128)(2,1)} %get-tuple-element.47), channel_id=1, source_target_pairs={{0,32},{32,64},{64,96},{96,0},{1,33},{33,65},{65,97},{97,1},{2,34}... | collective-permute-start | bytes 1376264 | tf_op jit(solution)/shard_map/ppermute | solution.py:204
  20.6 16.2 %collective-permute-start.2 = (bf16[32,7168]{1,0:T(8,128)(2,1)}, bf16[32,7168]{1,0:T(8,128)(2,1)S(1)}, u32[]{:S(2)}, u32[]{:S(2)}) collective-permute-start(bf16[32,7168]{1,0:T(8,128)(2,1)} %get-tuple-element.25), channel_id=1, source_target_pairs={{0,96},{32,0},{64,32},{96,64},{1,97},{33,1},{65,33},{97,65},{2,98}... | collective-permute-start | bytes 1376264 | tf_op jit(solution)/shard_map/ppermute | solution.py:205
  23.9 13.4 %collective-permute-start.5 = (bf16[32,7168]{1,0:T(8,128)(2,1)}, bf16[32,7168]{1,0:T(8,128)(2,1)S(1)}, u32[]{:S(2)}, u32[]{:S(2)}) collective-permute-start(bf16[32,7168]{1,0:T(8,128)(2,1)} %get-tuple-element.30), channel_id=1, source_target_pairs={{0,32},{32,64},{64,96},{96,0},{1,33},{33,65},{65,97},{97,1},{2,34}... | collective-permute-start | bytes 1376264 | tf_op jit(solution)/shard_map/ppermute | solution.py:204
  38.2 35.5 %copy-start.2 = (bf16[1,3,512,512]{3,2,1,0:T(8,128)(2,1)S(1)}, bf16[1,3,512,512]{3,2,1,0:T(8,128)(2,1)}, u32[]{:S(2)}) copy-start(bf16[1,3,512,512]{3,2,1,0:T(8,128)(2,1)} %param.10) | copy-start | bytes 4718596
  38.2 35.4 %copy-start.3 = (bf16[1,3,512,512]{3,2,1,0:T(8,128)(2,1)S(1)}, bf16[1,3,512,512]{3,2,1,0:T(8,128)(2,1)}, u32[]{:S(2)}) copy-start(bf16[1,3,512,512]{3,2,1,0:T(8,128)(2,1)} %param.11) | copy-start | bytes 4718596
  76.0 51.3 %copy-start.1 = (f32[1,3,512,512]{3,2,1,0:T(8,128)S(1)}, f32[1,3,512,512]{3,2,1,0:T(8,128)}, u32[]{:S(2)}) copy-start(f32[1,3,512,512]{3,2,1,0:T(8,128)} %param.9) | copy-start | bytes 9437188
  108.2 19.2 %copy-start = (f32[1,3,512,512]{3,2,1,0:T(8,128)S(1)}, f32[1,3,512,512]{3,2,1,0:T(8,128)}, u32[]{:S(2)}) copy-start(f32[1,3,512,512]{3,2,1,0:T(8,128)} %param.8) | copy-start | bytes 9437188
  108.8 14.6 %collective-permute-start.6 = (bf16[64,3584]{1,0:T(8,128)(2,1)S(1)}, bf16[64,3584]{1,0:T(8,128)(2,1)S(1)}, u32[]{:S(2)}, u32[]{:S(2)}) collective-permute-start(bf16[64,3584]{1,0:T(8,128)(2,1)S(1)} %get-tuple-element.38), channel_id=1, source_target_pairs={{0,32},{32,64},{64,96},{96,0},{1,33},{33,65},{65,97},{97,1},{2,34}... | collective-permute-start | bytes 1376264 | tf_op jit(solution)/shard_map/ppermute | solution.py:204
  110.2 13.4 %collective-permute-start.8 = (bf16[64,3584]{1,0:T(8,128)(2,1)S(1)}, bf16[64,3584]{1,0:T(8,128)(2,1)S(1)}, u32[]{:S(2)}, u32[]{:S(2)}) collective-permute-start(bf16[64,3584]{1,0:T(8,128)(2,1)S(1)} %get-tuple-element.39), channel_id=1, source_target_pairs={{0,96},{32,0},{64,32},{96,64},{1,97},{33,1},{65,33},{97,65},{2,98}... | collective-permute-start | bytes 1376264 | tf_op jit(solution)/shard_map/ppermute | solution.py:205
  112.7 20.6 %collective-permute-start.11 = (bf16[64,3584]{1,0:T(8,128)(2,1)S(1)}, bf16[64,3584]{1,0:T(8,128)(2,1)S(1)}, u32[]{:S(2)}, u32[]{:S(2)}) collective-permute-start(bf16[64,3584]{1,0:T(8,128)(2,1)S(1)} %get-tuple-element.41.refs_0_), channel_id=1, source_target_pairs={{0,96},{32,0},{64,32},{96,64},{1,97},{33,1},{65,33},{97,65},{2,98}... | collective-permute-start | bytes 1376264 | tf_op jit(solution)/shard_map/ppermute | solution.py:205
  114.6 18.8 %collective-permute-start.10 = (bf16[64,3584]{1,0:T(8,128)(2,1)S(1)}, bf16[64,3584]{1,0:T(8,128)(2,1)S(1)}, u32[]{:S(2)}, u32[]{:S(2)}) collective-permute-start(bf16[64,3584]{1,0:T(8,128)(2,1)S(1)} %get-tuple-element.42.refs_1_), channel_id=1, source_target_pairs={{0,32},{32,64},{64,96},{96,0},{1,33},{33,65},{65,97},{97,1},{2,34}... | collective-permute-start | bytes 1376264 | tf_op jit(solution)/shard_map/ppermute | solution.py:204
  123.4 19.1 %collective-permute-start.7 = (bf16[64,3584]{1,0:T(8,128)(2,1)S(1)}, bf16[64,3584]{1,0:T(8,128)(2,1)S(1)}, u32[]{:S(2)}, u32[]{:S(2)}) collective-permute-start(bf16[64,3584]{1,0:T(8,128)(2,1)S(1)} %collective-permute-done.6.refs_2_), channel_id=1, source_target_pairs={{0,32},{32,64},{64,96},{96,0},{1,33},{33,65},{65,97},{97,1},{2,34}... | collective-permute-start | bytes 1376264 | tf_op jit(solution)/shard_map/ppermute | solution.py:204
  123.5 19.0 %collective-permute-start.9 = (bf16[64,3584]{1,0:T(8,128)(2,1)S(1)}, bf16[64,3584]{1,0:T(8,128)(2,1)S(1)}, u32[]{:S(2)}, u32[]{:S(2)}) collective-permute-start(bf16[64,3584]{1,0:T(8,128)(2,1)S(1)} %collective-permute-done.8.refs_5_), channel_id=1, source_target_pairs={{0,96},{32,0},{64,32},{96,64},{1,97},{33,1},{65,33},{97,65},{2,98}... | collective-permute-start | bytes 1376264 | tf_op jit(solution)/shard_map/ppermute | solution.py:205

commit v5 on v4

--- a/solution.py
+++ b/solution.py
@@ -7,7 +7,8 @@
 from jax.experimental.pallas import tpu as pltpu
 from jax.sharding import PartitionSpec as P
 
-RELAY_FLOPS = 30_000_000_000
+AHEAD = 30_000_000_000
+BACKWARD = (48, 16)
 
 
 def any_spec():
@@ -20,6 +21,35 @@
 
 def params(mib=16):
     return pltpu.CompilerParams(vmem_limit_bytes=mib * 1024 * 1024)
+
+
+def cut_kernel(cuts, groups, grads, *refs):
+    outs, sems = refs[-1 - len(cuts) : -1], refs[-1]
+    width = outs[0].shape[1]
+    copies = []
+    for at, (out, (group, start)) in enumerate(zip(outs, cuts, strict=True)):
+        first = pl.multiple_of(groups[group] * width, 128)
+        part = grads.at[0, pl.ds(start, out.shape[0]), pl.ds(first, width)]
+        copy = pltpu.make_async_copy(part, out, sems.at[at])
+        copy.start()
+        copies.append(copy)
+    for copy in copies:
+        copy.wait()
+
+
+def cut(groups, grads, cuts, width, after=()):
+    total = sum(rows for _, _, rows in cuts) * width
+    return pl.pallas_call(
+        functools.partial(cut_kernel, [(group, start) for group, start, _ in cuts]),
+        out_shape=[jax.ShapeDtypeStruct((rows, width), jnp.bfloat16) for _, _, rows in cuts],
+        in_specs=[pl.BlockSpec(memory_space=pltpu.SMEM), pl.BlockSpec(memory_space=pltpu.HBM)]
+        + [any_spec()] * len(after),
+        out_specs=[vmem_spec()] * len(cuts),
+        scratch_shapes=[pltpu.SemaphoreType.DMA((len(cuts),))],
+        compiler_params=params(),
+        cost_estimate=pl.CostEstimate(flops=0, bytes_accessed=4 * total, transcendentals=0),
+        name="cut",
+    )(groups, pltpu.with_memory_space_constraint(grads, pltpu.HBM), *after)
 
 
 def relay_kernel(ahead, passed_right, behind, passed_left, out_right, out_left):
@@ -38,7 +68,7 @@
         out_specs=[vmem_spec()] * 2,
         compiler_params=params(),
         cost_estimate=pl.CostEstimate(
-            flops=RELAY_FLOPS, bytes_accessed=12 * rows * columns, transcendentals=0
+            flops=AHEAD, bytes_accessed=12 * rows * columns, transcendentals=0
         ),
         name="relays",
     )(ahead, passed_right, behind, passed_left)
@@ -72,23 +102,30 @@
     )(owners, own, *lower, *upper)
 
 
-def update_kernel(rows_of, blocks, left_roots, right_roots, out):
+def update_kernel(rows_of, blocks, left_roots, right_roots, *outs):
     for slot in range(left_roots.shape[0]):
         block = blocks[rows_of[slot]]
         applied = jnp.dot(left_roots[slot], block, preferred_element_type=jnp.float32)
         product = jnp.dot(
             applied.astype(jnp.bfloat16), right_roots[slot], preferred_element_type=jnp.float32
-        )
-        out[rows_of[slot]] = product.astype(jnp.bfloat16)
-
-
-def updates(rows_of, blocks, left_roots, right_roots):
+        ).astype(jnp.bfloat16)
+        product = product.reshape(outs[0].shape[1], -1, product.shape[1])
+        start = 0
+        for out in outs:
+            out[rows_of[slot]] = product[:, start : start + out.shape[2]]
+            start += out.shape[2]
+
+
+def updates(rows_of, blocks, left_roots, right_roots, strips):
     capacity, block_size = left_roots.shape[0], left_roots.shape[1]
     return pl.pallas_call(
         update_kernel,
-        out_shape=jax.ShapeDtypeStruct(blocks.shape, jnp.bfloat16),
+        out_shape=[
+            jax.ShapeDtypeStruct((blocks.shape[0], strips, rows, block_size), jnp.bfloat16)
+            for rows in BACKWARD
+        ],
         in_specs=[pl.BlockSpec(memory_space=pltpu.SMEM)] + [vmem_spec()] * 3,
-        out_specs=vmem_spec(),
+        out_specs=[vmem_spec()] * len(BACKWARD),
         compiler_params=params(),
         cost_estimate=pl.CostEstimate(
             flops=4 * capacity * block_size**3,
@@ -124,53 +161,62 @@
         out_shape=[jax.ShapeDtypeStruct(factor_left.shape, jnp.float32)] * 2,
         compiler_params=params(),
         cost_estimate=pl.CostEstimate(
-            flops=4 * capacity * block_size**3,
+            flops=AHEAD,
             bytes_accessed=18 * capacity * block_size**2,
             transcendentals=0,
         ),
         name="statistics",
-    )(rows_of, named, blocks, factor_left, factor_right)
-
-
-def pick_kernel(block_size, owners, slots, low, high):
+    )(
+        rows_of,
+        named,
+        blocks,
+        pltpu.with_memory_space_constraint(factor_left, pltpu.HBM),
+        pltpu.with_memory_space_constraint(factor_right, pltpu.HBM),
+    )
+
+
+def pick_kernel(block_size, owners, slots, *refs):
+    low, high = refs[-2:]
     count = low.shape[1] // block_size
     for at in range(2 * count):
         out, first = (low, at) if at < count else (high, at - count)
         out[:, first * block_size : (first + 1) * block_size] = slots[owners[at]]
 
 
-def from_slots(owners, slots):
+def from_slots(owners, slots, after=(), flops=0):
     count = owners.shape[0] // 2
     _, rows, block_size = slots.shape
     return pl.pallas_call(
         functools.partial(pick_kernel, block_size),
         out_shape=[jax.ShapeDtypeStruct((rows, count * block_size), jnp.bfloat16)] * 2,
-        in_specs=[pl.BlockSpec(memory_space=pltpu.SMEM), vmem_spec()],
+        in_specs=[pl.BlockSpec(memory_space=pltpu.SMEM), vmem_spec()]
+        + [pl.BlockSpec(memory_space=pltpu.HBM)] * len(after),
         out_specs=[vmem_spec()] * 2,
         compiler_params=params(),
         cost_estimate=pl.CostEstimate(
-            flops=0, bytes_accessed=8 * rows * count * block_size, transcendentals=0
+            flops=flops, bytes_accessed=8 * rows * count * block_size, transcendentals=0
         ),
         name="from_slots",
-    )(owners, slots)
-
-
-def place_kernel(groups, *refs):
+    )(owners, slots, *(pltpu.with_memory_space_constraint(a, pltpu.HBM) for a in after))
+
+
+def place_kernel(start, groups, *refs):
     pieces, out, sems = refs[: 2 * groups.shape[0]], refs[-2], refs[-1]
-    half = pieces[0].shape[1]
+    rows, half = pieces[0].shape
     copies = []
     for at, piece in enumerate(pieces):
         first = pl.multiple_of(groups[at // 2] * (2 * half) + at % 2 * half, 128)
-        copy = pltpu.make_async_copy(piece, out.at[:, pl.ds(first, half)], sems.at[at])
+        where = out.at[pl.ds(start, rows), pl.ds(first, half)]
+        copy = pltpu.make_async_copy(piece, where, sems.at[at])
         copy.start()
         copies.append(copy)
     for copy in copies:
         copy.wait()
 
 
-def place(groups, pieces, shape, held=()):
-    return pl.pallas_call(
-        place_kernel,
+def place(groups, pieces, start, shape, held):
+    return pl.pallas_call(
+        functools.partial(place_kernel, start),
         out_shape=jax.ShapeDtypeStruct(shape, jnp.bfloat16),
         in_specs=[pl.BlockSpec(memory_space=pltpu.SMEM)]
         + [vmem_spec()] * len(pieces)
@@ -226,6 +272,11 @@
     ).astype(jnp.int32)
     named = named.astype(jnp.int32)
 
+    groups = jnp.stack([replica_at, left_at, right_at, far_at]).astype(jnp.int32)
+    half = strip_rows // 2
+    far = cut(groups, grads, ((3, 0, half), (3, half, half)), width)
+    passed_right, passed_left = to_right(far[0]), to_left(far[1])
+    after, before = cut(groups, grads, ((2, half, half), (1, 0, half)), width, far)
     tile = 8
     view = grads[0].reshape(strip_rows // tile, tile, num_replicas, width).transpose(0, 2, 1, 3)
 
@@ -235,43 +286,42 @@
         )
         return part.reshape(rows, width)
 
-    half = strip_rows // 2
-    far = (piece(far_at, 0, half), piece(far_at, half, half))
-    (ahead_at, behind_at), far = lax.optimization_barrier(((right_at, left_at), far))
-    passed_right, passed_left = to_right(far[0]), to_left(far[1])
-    plain_right = to_right(piece(ahead_at, half, half))
-    plain_left = to_left(piece(behind_at, 0, half))
-    ahead, behind = relays(
-        piece(right_at, 0, half), passed_right, piece(left_at, half, half), passed_left
-    )
+    ahead, behind = piece(right_at, 0, half), piece(left_at, half, half)
+    own = piece(replica_at, 0, strip_rows)
+    plain_right, plain_left = to_right(after), to_left(before)
+    ahead, behind = relays(ahead, passed_right, behind, passed_left)
     added_right, added_left = to_right(ahead), to_left(behind)
     lower = (plain_left, added_right)
     upper = (added_left, plain_right)
-    groups = jnp.stack([replica_at, left_at, right_at, far_at]).astype(jnp.int32)
     upper, rows_of, named, groups = lax.optimization_barrier((upper, rows_of, named, groups))
-    own = piece(replica_at, 0, strip_rows)
     slots = to_slots(owners, own, lower, upper, num_shards, block_size)
     came = lax.all_to_all(slots, "shard", split_axis=0, concat_axis=0, tiled=True)
     blocks = came.reshape(block_rows, block_size, block_size)
-    outs = updates(rows_of, blocks, left_inverse_roots[0], right_inverse_roots[0])
+    outs = updates(rows_of, blocks, left_inverse_roots[0], right_inverse_roots[0], strips)
     new_left, new_right = statistics(rows_of, named, blocks, factor_left[0], factor_right[0])
 
-    returned = lax.all_to_all(
-        outs.reshape(num_shards, strip_rows, block_size),
-        "shard",
-        split_axis=0,
-        concat_axis=0,
-        tiled=True,
-    )
-    low, high = from_slots(owners, returned)
-    later, (low, high) = lax.optimization_barrier((owners, (low, high)))
-    left_low, right_high = to_right(low), to_left(high)
-    own_low, own_high = from_slots(later, returned)
-    left_high, right_low = to_right(own_high), to_left(own_low)
-    far_low, far_high = to_right(left_low), to_left(right_high)
-    near = (own_low, own_high, left_low, left_high, right_low, right_high)
-    update = place(groups[:3], near, (strip_rows, columns))
-    update = place(groups[3:], (far_low, far_high), (strip_rows, columns), (update,))
+    held, start, before = (), 0, None
+    for out in outs:
+        rows = out.shape[2]
+        if before is not None:
+            out, before = lax.optimization_barrier((out, before))
+        returned = lax.all_to_all(
+            out.reshape(num_shards, rows, block_size),
+            "shard",
+            split_axis=0,
+            concat_axis=0,
+            tiled=True,
+        )
+        low, high = from_slots(owners, returned, () if before is None else (new_left,))
+        later, (low, high) = lax.optimization_barrier((owners, (low, high)))
+        left_low, right_high = to_right(low), to_left(high)
+        own_low, own_high = before = from_slots(later, returned)
+        left_high, right_low = to_right(own_high), to_left(own_low)
+        far_low, far_high = to_right(left_low), to_left(right_high)
+        near = (own_low, own_high, left_low, left_high, right_low, right_high)
+        held = (place(groups, near + (far_low, far_high), start, (strip_rows, columns), held),)
+        start += rows
+    (update,) = held
     return (new_left[None], new_right[None], update)
 
 

time: 145 us -> 143 us (0.986)
  waiting for transfers between devices: 35.6 us -> 16.7 us
  starting transfers between devices: 18.1 us -> 31.2 us
  Pallas kernels: 14.5 us -> 26.8 us
  blocking collectives: 67.6 us -> 61.7 us
  local copies, waits for them, and re-layouts: 6.62 us -> 4.34 us
    ppermute x6 -> x9, waiting for transfers between devices: 25.2 us -> 7.66 us  [body(): to_right = lambda a: lax.ppermute(a, 'replica', onward)]
    ppermute x6 -> x9, starting transfers between devices: 14.4 us -> 22.5 us  [body(): to_left = lambda a: lax.ppermute(a, 'replica', back)]
    pallas_call x3 -> x5, Pallas kernels: 6.08 us -> 12.1 us  [the longest x2 4.63 us: place(): pl.pallas_call(functools.partial(place_kernel, start), out_shape=jax.Shap...]
    all_to_all x1, blocking collectives: 32.2 us -> 26.2 us  [body(): lax.all_to_all(out.reshape(num_shards, rows, block_size), 'shard', split_...]
    all_to_all x0 -> x1, starting transfers between devices: none -> 4.1 us  [body(): lax.all_to_all(out.reshape(num_shards, rows, block_size), 'shard', split_...]
    pallas_call x1, Pallas kernels: 4.33 us -> 7.63 us  [statistics(): pl.pallas_call(gram_kernel, grid_spec=pltpu.PrefetchScalarGridSpec(num_sc...]
    pallas_call x2 -> x4, Pallas kernels: 1.21 us -> 4.01 us  [from_slots(): pl.pallas_call(functools.partial(pick_kernel, block_size), out_shape=[jax...]
    reshape x3 -> x2, local copies, waits for them, and re-layouts: 5.87 us -> 3.23 us  [piece(): return part.reshape(rows, width)]
  transfers between devices with their start and end apart: 12 -> 19, of which waited for: 8 -> 7; matrix products, arithmetic and copies ran while one was open for 4% -> 3% of each run, Pallas kernels for 6% -> 13%
where the time goes in v5:
time: 143 us
  blocking collectives  61.7 us (43%)
  starting transfers between devices  31.2 us (22%)
  Pallas kernels  26.8 us (19%)
  waiting for transfers between devices  16.7 us (12%)
  local copies, waits for them, and re-layouts  4.34 us (3%)
    all_to_all x1, blocking collectives, body(): lax.all_to_all(slots, 'shard', split_axis=0, concat_axis=0, tiled=True)  35.4 us
    all_to_all x1, blocking collectives, body(): lax.all_to_all(out.reshape(num_shards, rows, block_size), 'shard', split_...  26.2 us
    ppermute x9, starting transfers between devices, body(): to_left = lambda a: lax.ppermute(a, 'replica', back)  22.5 us
    ppermute x9, waiting for transfers between devices, body(): to_left = lambda a: lax.ppermute(a, 'replica', back)  9.05 us
    ppermute x9, waiting for transfers between devices, body(): to_right = lambda a: lax.ppermute(a, 'replica', onward)  7.66 us
    pallas_call x1, Pallas kernels, statistics(): pl.pallas_call(gram_kernel, grid_spec=pltpu.PrefetchScalarGridSpec(num_sc...  7.63 us
    pallas_call x2, Pallas kernels, place(): pl.pallas_call(functools.partial(place_kernel, start), out_shape=jax.Shap...  4.63 us
    ppermute x9, starting transfers between devices, body(): to_right = lambda a: lax.ppermute(a, 'replica', onward)  4.61 us
  transfers between devices with their start and end apart: 19, of which 7 were waited for; matrix products, arithmetic and copies ran while one was open for 3% of the time, Pallas kernels for 13%

profile of v5, /device:TPU:0, one launch (start us, length us, event | category | flops | bytes accessed | tf_op | source)
XLA Modules:
  0.0 142.6 jit_solution(17738725479554084240)
XLA Ops:
  0.7 1.7 %cut.2 = (bf16[32,7168]{1,0:T(8,128)(2,1)S(1)}, bf16[32,7168]{1,0:T(8,128)(2,1)S(1)}) custom-call(s32[4]{0:T(128)S(1)} %pad_add_fusion.groups, bf16[1,64,28672]{2,1,0:T(8,128)(2,1)} %grads.3), custom_call_target="tpu_custom_call" | custom-call | bytes 1835008 | tf_op jit(solution)/shard_map/cut/pallas_call | solution.py:42
  2.5 2.1 %collective-permute-start = (bf16[32,7168]{1,0:T(8,128)(2,1)S(1)}, bf16[32,7168]{1,0:T(8,128)(2,1)}, u32[]{:S(2)}, u32[]{:S(2)}) collective-permute-start(bf16[32,7168]{1,0:T(8,128)(2,1)S(1)} %get-tuple-element.33.refs_0_), channel_id=1, source_target_pairs={{0,32},{32,64},{64,96},{96,0},{1,33},{33,65},{65,97},{97,1},{2,34}... | collective-permute-start | bytes 1376264 | tf_op jit(solution)/shard_map/ppermute | solution.py:250
  4.5 2.2 %collective-permute-start.1 = (bf16[32,7168]{1,0:T(8,128)(2,1)S(1)}, bf16[32,7168]{1,0:T(8,128)(2,1)}, u32[]{:S(2)}, u32[]{:S(2)}) collective-permute-start(bf16[32,7168]{1,0:T(8,128)(2,1)S(1)} %get-tuple-element.34.refs_1_), channel_id=1, source_target_pairs={{0,96},{32,0},{64,32},{96,64},{1,97},{33,1},{65,33},{97,65},{2,98}... | collective-permute-start | bytes 1376264 | tf_op jit(solution)/shard_map/ppermute | solution.py:251
  6.8 2.6 %cut.3 = (bf16[32,7168]{1,0:T(8,128)(2,1)}, bf16[32,7168]{1,0:T(8,128)(2,1)}) custom-call(s32[4]{0:T(128)S(1)} %pad_add_fusion.groups, bf16[1,64,28672]{2,1,0:T(8,128)(2,1)} %grads.3, bf16[32,7168]{1,0:T(8,128)(2,1)S(1)} %get-tuple-element.33.refs_0_, bf16[32,7168]{1,0:T(8,128)(2,1)S(1)} %get-tuple-element.34.refs_1_), custom_call_target="tpu_custom_call" | custom-call | bytes 1835008 | tf_op jit(solution)/shard_map/cut/pallas_call | solution.py:42
  9.5 3.2 %collective-permute-start.4 = (bf16[32,7168]{1,0:T(8,128)(2,1)}, bf16[32,7168]{1,0:T(8,128)(2,1)S(1)}, u32[]{:S(2)}, u32[]{:S(2)}) collective-permute-start(bf16[32,7168]{1,0:T(8,128)(2,1)} %get-tuple-element.39), channel_id=1, source_target_pairs={{0,96},{32,0},{64,32},{96,64},{1,97},{33,1},{65,33},{97,65},{2,98}... | collective-permute-start | bytes 1376264 | tf_op jit(solution)/shard_map/ppermute | solution.py:251
  12.7 1.2 dynamic-slice_bitcast_fusion.own
  13.9 2.0 %dynamic-slice_bitcast_fusion.1 = (bf16[32,7168]{1,0:T(8,128)(2,1)S(1)}, bf16[32,7168]{1,0:T(8,128)(2,1)}) fusion(bf16[8,8,4,7168]{3,1,2,0:T(8,128)(2,1)} %bitcast.42, s32[]{:T(128)S(6)} %select_n.52, s32[]{:T(128)S(6)} %select_n.49), kind=kLoop, calls=%fused_computation.1 | loop fusion | bytes 1835016 | tf_op jit(solution)/shard_map/reshape | solution.py:287
  16.3 1.8 %collective-permute-done.passed_right = bf16[32,7168]{1,0:T(8,128)(2,1)} collective-permute-done((bf16[32,7168]{1,0:T(8,128)(2,1)S(1)}, bf16[32,7168]{1,0:T(8,128)(2,1)}, u32[]{:S(2)}, u32[]{:S(2)}) %collective-permute-start) | collective-permute-done | bytes 458784 | tf_op jit(solution)/shard_map/ppermute | solution.py:250
  18.1 1.0 copy-done
  19.1 2.2 %relays.1 = (bf16[32,7168]{1,0:T(8,128)(2,1)}, bf16[32,7168]{1,0:T(8,128)(2,1)}) custom-call(bf16[32,7168]{1,0:T(8,128)(2,1)S(1)} %copy-done, bf16[32,7168]{1,0:T(8,128)(2,1)} %collective-permute-done.passed_right, bf16[32,7168]{1,0:T(8,128)(2,1)S(1)} %get-tuple-element.66.behind, bf16[32,7168]{1,0:T(8,128)(2,1)} %collective-permute-done.1.passed_left), custom_call_target="tpu_custom_call" | custom-call | flops 30000001024 | bytes 2752512 | tf_op jit(solution)/shard_map/relays/pallas_call | solution.py:64
  21.3 3.4 %collective-permute-start.2 = (bf16[32,7168]{1,0:T(8,128)(2,1)}, bf16[32,7168]{1,0:T(8,128)(2,1)S(1)}, u32[]{:S(2)}, u32[]{:S(2)}) collective-permute-start(bf16[32,7168]{1,0:T(8,128)(2,1)} %get-tuple-element.35), channel_id=1, source_target_pairs={{0,96},{32,0},{64,32},{96,64},{1,97},{33,1},{65,33},{97,65},{2,98}... | collective-permute-start | bytes 1376264 | tf_op jit(solution)/shard_map/ppermute | solution.py:251
  25.4 2.3 %collective-permute-done.3.high_b = bf16[32,7168]{1,0:T(8,128)(2,1)S(1)} collective-permute-done((bf16[32,7168]{1,0:T(8,128)(2,1)}, bf16[32,7168]{1,0:T(8,128)(2,1)S(1)}, u32[]{:S(2)}, u32[]{:S(2)}) %collective-permute-start.3) | collective-permute-done | bytes 458784 | tf_op jit(solution)/shard_map/ppermute | solution.py:250
  27.7 8.7 %collective-permute-done.2.high_a = bf16[32,7168]{1,0:T(8,128)(2,1)S(1)} collective-permute-done((bf16[32,7168]{1,0:T(8,128)(2,1)}, bf16[32,7168]{1,0:T(8,128)(2,1)S(1)}, u32[]{:S(2)}, u32[]{:S(2)}) %collective-permute-start.2) | collective-permute-done | bytes 458784 | tf_op jit(solution)/shard_map/ppermute | solution.py:251
  36.8 0.9 to_slots.1
  37.7 35.4 %all_to_all.15 = bf16[32,64,512]{2,1,0:T(8,128)(2,1)S(1)} all-to-all(bf16[32,64,512]{2,1,0:T(8,128)(2,1)S(1)} %to_slots.1), channel_id=1, replica_groups=mesh['replica'=4,'shard'=32] {'shard'}, dimensions={0} | all-to-all | bytes 4194304 | tf_op jit(solution)/shard_map/all_to_all | solution.py:298
  73.2 3.1 %updates.1 = (bf16[4,8,48,512]{3,2,1,0:T(8,128)(2,1)S(1)}, bf16[4,8,16,512]{3,2,1,0:T(8,128)(2,1)}) custom-call(s32[3]{0:T(128)S(1)} %select_reduce_fusion.rows_of, bf16[4,512,512]{2,1,0:T(8,128)(2,1)S(1)} %bitcast.36, bf16[3,512,512]{2,1,0:T(8,128)(2,1)S(1)} %bitcast.39, bf16[3,512,512]{2,1,0:T(8,128)(2,1)S(1)} %bitcast.40), custom_call_target="tpu_custom_call" | custom-call | flops 1610612736 | bytes 6291456 | tf_op jit(solution)/shard_map/updates/pallas_call | solution.py:121
  76.3 26.2 %all_to_all.16.slots = bf16[32,48,512]{2,1,0:T(8,128)(2,1)S(1)} all-to-all(bf16[32,48,512]{2,1,0:T(8,128)(2,1)S(1)} %bitcast.38), channel_id=1, replica_groups=mesh['replica'=4,'shard'=32] {'shard'}, dimensions={0} | all-to-all | bytes 3145728 | tf_op jit(solution)/shard_map/all_to_all | solution.py:308
  102.5 1.4 %from_slots.4 = (bf16[48,3584]{1,0:T(8,128)(2,1)}, bf16[48,3584]{1,0:T(8,128)(2,1)}) custom-call(s32[14]{0:T(128)S(1)} %bitcast_select_fusion.owners, bf16[32,48,512]{2,1,0:T(8,128)(2,1)S(1)} %all_to_all.16.slots), custom_call_target="tpu_custom_call" | custom-call | bytes 1376256 | tf_op jit(solution)/shard_map/from_slots/pallas_call | solution.py:189
  104.0 1.3 collective-permute-start.12
  105.2 2.0 %collective-permute-start.15 = (bf16[48,3584]{1,0:T(8,128)(2,1)}, bf16[48,3584]{1,0:T(8,128)(2,1)S(1)}, u32[]{:S(2)}, u32[]{:S(2)}) collective-permute-start(bf16[48,3584]{1,0:T(8,128)(2,1)} %get-tuple-element.62), channel_id=1, source_target_pairs={{0,96},{32,0},{64,32},{96,64},{1,97},{33,1},{65,33},{97,65},{2,98}... | collective-permute-start | bytes 1032200 | tf_op jit(solution)/shard_map/ppermute | solution.py:251
  107.2 1.5 %from_slots.5 = (bf16[48,3584]{1,0:T(8,128)(2,1)}, bf16[48,3584]{1,0:T(8,128)(2,1)}) custom-call(s32[14]{0:T(128)S(1)} %bitcast_select_fusion.owners, bf16[32,48,512]{2,1,0:T(8,128)(2,1)S(1)} %all_to_all.16.slots), custom_call_target="tpu_custom_call" | custom-call | bytes 1376256 | tf_op jit(solution)/shard_map/from_slots/pallas_call | solution.py:189
  108.7 1.8 %collective-permute-start.14 = (bf16[48,3584]{1,0:T(8,128)(2,1)}, bf16[48,3584]{1,0:T(8,128)(2,1)}, u32[]{:S(2)}, u32[]{:S(2)}) collective-permute-start(bf16[48,3584]{1,0:T(8,128)(2,1)} %get-tuple-element.51.refs_0_), channel_id=1, source_target_pairs={{0,96},{32,0},{64,32},{96,64},{1,97},{33,1},{65,33},{97,65},{2,98}... | collective-permute-start | bytes 1032200 | tf_op jit(solution)/shard_map/ppermute | solution.py:251
  110.7 4.1 %all-to-all-start.2 = ((bf16[32,16,512]{2,1,0:T(8,128)(2,1)}), bf16[32,16,512]{2,1,0:T(8,128)(2,1)S(1)}, u32[]{:S(2)}, u32[]{:S(2)}) async-start(bf16[32,16,512]{2,1,0:T(8,128)(2,1)} %bitcast.22), calls=%async_computation.2 | async-start | bytes 1048576 | tf_op jit(solution)/shard_map/all_to_all | solution.py:308
  114.8 1.5 %collective-permute-done.12.refs_2_ = bf16[48,3584]{1,0:T(8,128)(2,1)S(1)} collective-permute-done((bf16[48,3584]{1,0:T(8,128)(2,1)}, bf16[48,3584]{1,0:T(8,128)(2,1)S(1)}, u32[]{:S(2)}, u32[]{:S(2)}) %collective-permute-start.12) | collective-permute-done | bytes 344096 | tf_op jit(solution)/shard_map/ppermute | solution.py:250
  116.4 3.2 %collective-permute-start.17 = (bf16[48,3584]{1,0:T(8,128)(2,1)S(1)}, bf16[48,3584]{1,0:T(8,128)(2,1)}, u32[]{:S(2)}, u32[]{:S(2)}) collective-permute-start(bf16[48,3584]{1,0:T(8,128)(2,1)S(1)} %collective-permute-done.15.refs_5_), channel_id=1, source_target_pairs={{0,96},{32,0},{64,32},{96,64},{1,97},{33,1},{65,33},{97,65},{2,98}... | collective-permute-start | bytes 1032200 | tf_op jit(solution)/shard_map/ppermute | solution.py:251
  119.6 7.6 %statistics.1 = (f32[3,512,512]{2,1,0:T(8,128)}, f32[3,512,512]{2,1,0:T(8,128)}) custom-call(s32[3]{0:T(128)S(1)} %select_reduce_fusion.rows_of, s32[3]{0:T(128)S(1)} %get-tuple-element.38.named, bf16[4,512,512]{2,1,0:T(8,128)(2,1)S(1)} %bitcast.37, f32[3,512,512]{2,1,0:T(8,128)} %bitcast.46, f32[3,512,512]{2,1,0:T(8,128)} %bitcast.47), custom_call_target="tpu_custom_call" | custom-call | flops 30000001024 | bytes 14155776 | tf_op jit(solution)/shard_map/statistics/pallas_call | solution.py:153
  127.9 3.2 %collective-permute-start.9 = (bf16[16,3584]{1,0:T(8,128)(2,1)S(1)}, bf16[16,3584]{1,0:T(8,128)(2,1)S(1)}, u32[]{:S(2)}, u32[]{:S(2)}) collective-permute-start(bf16[16,3584]{1,0:T(8,128)(2,1)S(1)} %get-tuple-element.60), channel_id=1, source_target_pairs={{0,96},{32,0},{64,32},{96,64},{1,97},{33,1},{65,33},{97,65},{2,98}... | collective-permute-start | bytes 344072 | tf_op jit(solution)/shard_map/ppermute | solution.py:251
  132.4 1.5 %collective-permute-done.6.refs_2_ = bf16[16,3584]{1,0:T(8,128)(2,1)S(1)} collective-permute-done((bf16[16,3584]{1,0:T(8,128)(2,1)S(1)}, bf16[16,3584]{1,0:T(8,128)(2,1)S(1)}, u32[]{:S(2)}, u32[]{:S(2)}) %collective-permute-start.6) | collective-permute-done | bytes 114720 | tf_op jit(solution)/shard_map/ppermute | solution.py:250
  134.2 0.9 collective-permute-start.10
  135.1 2.8 %collective-permute-start.11 = (bf16[16,3584]{1,0:T(8,128)(2,1)S(1)}, bf16[16,3584]{1,0:T(8,128)(2,1)S(1)}, u32[]{:S(2)}, u32[]{:S(2)}) collective-permute-start(bf16[16,3584]{1,0:T(8,128)(2,1)S(1)} %collective-permute-done.9.refs_5_), channel_id=1, source_target_pairs={{0,96},{32,0},{64,32},{96,64},{1,97},{33,1},{65,33},{97,65},{2,98}... | collective-permute-start | bytes 344072 | tf_op jit(solution)/shard_map/ppermute | solution.py:251
  137.9 3.1 %place.2.refs_8_ = bf16[64,28672]{1,0:T(8,128)(2,1)} custom-call(s32[4]{0:T(128)S(1)} %pad_add_fusion.groups, bf16[48,3584]{1,0:T(8,128)(2,1)} %get-tuple-element.51.refs_0_, bf16[48,3584]{1,0:T(8,128)(2,1)} %get-tuple-element.52.refs_1_, bf16[48,3584]{1,0:T(8,128)(2,1)S(1)} %collective-permute-done.12.refs_2_, ...), custom_call_target="tpu_custom_call" | custom-call | bytes 5505024 | tf_op jit(solution)/shard_map/place/pallas_call | solution.py:218
  141.1 1.5 %place.3 = bf16[64,28672]{1,0:T(8,128)(2,1)} custom-call(s32[4]{0:T(128)S(1)} %pad_add_fusion.groups, bf16[16,3584]{1,0:T(8,128)(2,1)S(1)} %get-tuple-element.57.refs_0_, bf16[16,3584]{1,0:T(8,128)(2,1)S(1)} %get-tuple-element.58.refs_1_, bf16[16,3584]{1,0:T(8,128)(2,1)S(1)} %collective-permute-done.6.refs_2_, ...), custom_call_target="tpu_custom_call", output_to_operand_aliasing={{}: (9, {})} | custom-call | bytes 1835008 | tf_op jit(solution)/shard_map/place/pallas_call | solution.py:218
  (40 shorter events, 4.2 us)
Async XLA Ops:
  2.5 15.6 %collective-permute-start = (bf16[32,7168]{1,0:T(8,128)(2,1)S(1)}, bf16[32,7168]{1,0:T(8,128)(2,1)}, u32[]{:S(2)}, u32[]{:S(2)}) collective-permute-start(bf16[32,7168]{1,0:T(8,128)(2,1)S(1)} %get-tuple-element.33.refs_0_), channel_id=1, source_target_pairs={{0,32},{32,64},{64,96},{96,0},{1,33},{33,65},{65,97},{97,1},{2,34}... | collective-permute-start | bytes 1376264 | tf_op jit(solution)/shard_map/ppermute | solution.py:250
  4.5 11.4 %copy-start.3 = (s32[4,56]{1,0:T(4,128)S(1)}, s32[4,56]{1,0:T(4,128)}, u32[]{:S(2)}) copy-start(s32[4,56]{1,0:T(4,128)} %param.7) | copy-start | bytes 2692
  4.5 13.6 %collective-permute-start.1 = (bf16[32,7168]{1,0:T(8,128)(2,1)S(1)}, bf16[32,7168]{1,0:T(8,128)(2,1)}, u32[]{:S(2)}, u32[]{:S(2)}) collective-permute-start(bf16[32,7168]{1,0:T(8,128)(2,1)S(1)} %get-tuple-element.34.refs_1_), channel_id=1, source_target_pairs={{0,96},{32,0},{64,32},{96,64},{1,97},{33,1},{65,33},{97,65},{2,98}... | collective-permute-start | bytes 1376264 | tf_op jit(solution)/shard_map/ppermute | solution.py:251
  9.4 18.3 %collective-permute-start.3 = (bf16[32,7168]{1,0:T(8,128)(2,1)}, bf16[32,7168]{1,0:T(8,128)(2,1)S(1)}, u32[]{:S(2)}, u32[]{:S(2)}) collective-permute-start(bf16[32,7168]{1,0:T(8,128)(2,1)} %get-tuple-element.36), channel_id=1, source_target_pairs={{0,32},{32,64},{64,96},{96,0},{1,33},{33,65},{65,97},{97,1},{2,34}... | collective-permute-start | bytes 1376264 | tf_op jit(solution)/shard_map/ppermute | solution.py:250
  9.5 26.9 %collective-permute-start.4 = (bf16[32,7168]{1,0:T(8,128)(2,1)}, bf16[32,7168]{1,0:T(8,128)(2,1)S(1)}, u32[]{:S(2)}, u32[]{:S(2)}) collective-permute-start(bf16[32,7168]{1,0:T(8,128)(2,1)} %get-tuple-element.39), channel_id=1, source_target_pairs={{0,96},{32,0},{64,32},{96,64},{1,97},{33,1},{65,33},{97,65},{2,98}... | collective-permute-start | bytes 1376264 | tf_op jit(solution)/shard_map/ppermute | solution.py:251
  18.1 1.0 copy-start
  21.3 15.0 %collective-permute-start.2 = (bf16[32,7168]{1,0:T(8,128)(2,1)}, bf16[32,7168]{1,0:T(8,128)(2,1)S(1)}, u32[]{:S(2)}, u32[]{:S(2)}) collective-permute-start(bf16[32,7168]{1,0:T(8,128)(2,1)} %get-tuple-element.35), channel_id=1, source_target_pairs={{0,96},{32,0},{64,32},{96,64},{1,97},{33,1},{65,33},{97,65},{2,98}... | collective-permute-start | bytes 1376264 | tf_op jit(solution)/shard_map/ppermute | solution.py:251
  24.7 12.1 %collective-permute-start.5 = (bf16[32,7168]{1,0:T(8,128)(2,1)}, bf16[32,7168]{1,0:T(8,128)(2,1)S(1)}, u32[]{:S(2)}, u32[]{:S(2)}) collective-permute-start(bf16[32,7168]{1,0:T(8,128)(2,1)} %get-tuple-element.40), channel_id=1, source_target_pairs={{0,32},{32,64},{64,96},{96,0},{1,33},{33,65},{65,97},{97,1},{2,34}... | collective-permute-start | bytes 1376264 | tf_op jit(solution)/shard_map/ppermute | solution.py:250
  37.7 35.5 %copy-start.1 = (bf16[1,3,512,512]{3,2,1,0:T(8,128)(2,1)S(1)}, bf16[1,3,512,512]{3,2,1,0:T(8,128)(2,1)}, u32[]{:S(2)}) copy-start(bf16[1,3,512,512]{3,2,1,0:T(8,128)(2,1)} %param.10) | copy-start | bytes 4718596
  37.7 35.4 %copy-start.2 = (bf16[1,3,512,512]{3,2,1,0:T(8,128)(2,1)S(1)}, bf16[1,3,512,512]{3,2,1,0:T(8,128)(2,1)}, u32[]{:S(2)}) copy-start(bf16[1,3,512,512]{3,2,1,0:T(8,128)(2,1)} %param.11) | copy-start | bytes 4718596
  104.0 12.4 %collective-permute-start.12 = (bf16[48,3584]{1,0:T(8,128)(2,1)}, bf16[48,3584]{1,0:T(8,128)(2,1)S(1)}, u32[]{:S(2)}, u32[]{:S(2)}) collective-permute-start(bf16[48,3584]{1,0:T(8,128)(2,1)} %get-tuple-element.61), channel_id=1, source_target_pairs={{0,32},{32,64},{64,96},{96,0},{1,33},{33,65},{65,97},{97,1},{2,34}... | collective-permute-start | bytes 1032200 | tf_op jit(solution)/shard_map/ppermute | solution.py:250
  105.2 11.1 %collective-permute-start.15 = (bf16[48,3584]{1,0:T(8,128)(2,1)}, bf16[48,3584]{1,0:T(8,128)(2,1)S(1)}, u32[]{:S(2)}, u32[]{:S(2)}) collective-permute-start(bf16[48,3584]{1,0:T(8,128)(2,1)} %get-tuple-element.62), channel_id=1, source_target_pairs={{0,96},{32,0},{64,32},{96,64},{1,97},{33,1},{65,33},{97,65},{2,98}... | collective-permute-start | bytes 1032200 | tf_op jit(solution)/shard_map/ppermute | solution.py:251
  108.7 19.2 %collective-permute-start.14 = (bf16[48,3584]{1,0:T(8,128)(2,1)}, bf16[48,3584]{1,0:T(8,128)(2,1)}, u32[]{:S(2)}, u32[]{:S(2)}) collective-permute-start(bf16[48,3584]{1,0:T(8,128)(2,1)} %get-tuple-element.51.refs_0_), channel_id=1, source_target_pairs={{0,96},{32,0},{64,32},{96,64},{1,97},{33,1},{65,33},{97,65},{2,98}... | collective-permute-start | bytes 1032200 | tf_op jit(solution)/shard_map/ppermute | solution.py:251
  110.5 21.1 %collective-permute-start.13 = (bf16[48,3584]{1,0:T(8,128)(2,1)}, bf16[48,3584]{1,0:T(8,128)(2,1)}, u32[]{:S(2)}, u32[]{:S(2)}) collective-permute-start(bf16[48,3584]{1,0:T(8,128)(2,1)} %get-tuple-element.52.refs_1_), channel_id=1, source_target_pairs={{0,32},{32,64},{64,96},{96,0},{1,33},{33,65},{65,97},{97,1},{2,34}... | collective-permute-start | bytes 1032200 | tf_op jit(solution)/shard_map/ppermute | solution.py:250
  110.7 16.5 %all-to-all-start.2 = ((bf16[32,16,512]{2,1,0:T(8,128)(2,1)}), bf16[32,16,512]{2,1,0:T(8,128)(2,1)S(1)}, u32[]{:S(2)}, u32[]{:S(2)}) async-start(bf16[32,16,512]{2,1,0:T(8,128)(2,1)} %bitcast.22), calls=%async_computation.2 | async-start | bytes 1048576 | tf_op jit(solution)/shard_map/all_to_all | solution.py:308
  116.3 18.8 %collective-permute-start.16 = (bf16[48,3584]{1,0:T(8,128)(2,1)S(1)}, bf16[48,3584]{1,0:T(8,128)(2,1)}, u32[]{:S(2)}, u32[]{:S(2)}) collective-permute-start(bf16[48,3584]{1,0:T(8,128)(2,1)S(1)} %collective-permute-done.12.refs_2_), channel_id=1, source_target_pairs={{0,32},{32,64},{64,96},{96,0},{1,33},{33,65},{65,97},{97,1},{2,34}... | collective-permute-start | bytes 1032200 | tf_op jit(solution)/shard_map/ppermute | solution.py:250
  116.4 21.5 %collective-permute-start.17 = (bf16[48,3584]{1,0:T(8,128)(2,1)S(1)}, bf16[48,3584]{1,0:T(8,128)(2,1)}, u32[]{:S(2)}, u32[]{:S(2)}) collective-permute-start(bf16[48,3584]{1,0:T(8,128)(2,1)S(1)} %collective-permute-done.15.refs_5_), channel_id=1, source_target_pairs={{0,96},{32,0},{64,32},{96,64},{1,97},{33,1},{65,33},{97,65},{2,98}... | collective-permute-start | bytes 1032200 | tf_op jit(solution)/shard_map/ppermute | solution.py:251
  127.8 6.1 %collective-permute-start.6 = (bf16[16,3584]{1,0:T(8,128)(2,1)S(1)}, bf16[16,3584]{1,0:T(8,128)(2,1)S(1)}, u32[]{:S(2)}, u32[]{:S(2)}) collective-permute-start(bf16[16,3584]{1,0:T(8,128)(2,1)S(1)} %get-tuple-element.59), channel_id=1, source_target_pairs={{0,32},{32,64},{64,96},{96,0},{1,33},{33,65},{65,97},{97,1},{2,34}... | collective-permute-start | bytes 344072 | tf_op jit(solution)/shard_map/ppermute | solution.py:250
  127.9 6.4 %collective-permute-start.9 = (bf16[16,3584]{1,0:T(8,128)(2,1)S(1)}, bf16[16,3584]{1,0:T(8,128)(2,1)S(1)}, u32[]{:S(2)}, u32[]{:S(2)}) collective-permute-start(bf16[16,3584]{1,0:T(8,128)(2,1)S(1)} %get-tuple-element.60), channel_id=1, source_target_pairs={{0,96},{32,0},{64,32},{96,64},{1,97},{33,1},{65,33},{97,65},{2,98}... | collective-permute-start | bytes 344072 | tf_op jit(solution)/shard_map/ppermute | solution.py:251
  131.7 9.4 %collective-permute-start.8 = (bf16[16,3584]{1,0:T(8,128)(2,1)S(1)}, bf16[16,3584]{1,0:T(8,128)(2,1)S(1)}, u32[]{:S(2)}, u32[]{:S(2)}) collective-permute-start(bf16[16,3584]{1,0:T(8,128)(2,1)S(1)} %get-tuple-element.57.refs_0_), channel_id=1, source_target_pairs={{0,96},{32,0},{64,32},{96,64},{1,97},{33,1},{65,33},{97,65},{2,98}... | collective-permute-start | bytes 344072 | tf_op jit(solution)/shard_map/ppermute | solution.py:251
  133.8 7.2 %collective-permute-start.7 = (bf16[16,3584]{1,0:T(8,128)(2,1)S(1)}, bf16[16,3584]{1,0:T(8,128)(2,1)S(1)}, u32[]{:S(2)}, u32[]{:S(2)}) collective-permute-start(bf16[16,3584]{1,0:T(8,128)(2,1)S(1)} %get-tuple-element.58.refs_1_), channel_id=1, source_target_pairs={{0,32},{32,64},{64,96},{96,0},{1,33},{33,65},{65,97},{97,1},{2,34}... | collective-permute-start | bytes 344072 | tf_op jit(solution)/shard_map/ppermute | solution.py:250
  134.2 6.8 %collective-permute-start.10 = (bf16[16,3584]{1,0:T(8,128)(2,1)S(1)}, bf16[16,3584]{1,0:T(8,128)(2,1)S(1)}, u32[]{:S(2)}, u32[]{:S(2)}) collective-permute-start(bf16[16,3584]{1,0:T(8,128)(2,1)S(1)} %collective-permute-done.6.refs_2_), channel_id=1, source_target_pairs={{0,32},{32,64},{64,96},{96,0},{1,33},{33,65},{65,97},{97,1},{2,34}... | collective-permute-start | bytes 344072 | tf_op jit(solution)/shard_map/ppermute | solution.py:250
  135.1 6.0 %collective-permute-start.11 = (bf16[16,3584]{1,0:T(8,128)(2,1)S(1)}, bf16[16,3584]{1,0:T(8,128)(2,1)S(1)}, u32[]{:S(2)}, u32[]{:S(2)}) collective-permute-start(bf16[16,3584]{1,0:T(8,128)(2,1)S(1)} %collective-permute-done.9.refs_5_), channel_id=1, source_target_pairs={{0,96},{32,0},{64,32},{96,64},{1,97},{33,1},{65,33},{97,65},{2,98}... | collective-permute-start | bytes 344072 | tf_op jit(solution)/shard_map/ppermute | solution.py:251

commit v6 on v5

--- a/solution.py
+++ b/solution.py
@@ -136,29 +136,56 @@
     )(rows_of, blocks, left_roots, right_roots)
 
 
-def gram_kernel(rows_of, named, blocks, left, right, new_left, new_right):
-    block = blocks[0]
-    holds = named[pl.program_id(0)] > 0
-    scale = 0.1 / block.shape[0]
-    gram = lax.dot_general(block, block, (((1,), (1,)), ((), ())), preferred_element_type=jnp.float32)
-    new_left[0] = 0.9 * left[0] + jnp.where(holds, scale * gram, 0.0)
-    gram = lax.dot_general(block, block, (((0,), (0,)), ((), ())), preferred_element_type=jnp.float32)
-    new_right[0] = 0.9 * right[0] + jnp.where(holds, scale * gram, 0.0)
+def gram_kernel(rows_of, named, blocks, left, right, new_left, new_right, held, sides, ins, outs):
+    capacity, size = held.shape[:2]
+    scale = 0.1 / size
+    factors, news = (left, right), (new_left, new_right)
+    arrivals, leaving = [], []
+    for slot in range(capacity):
+        copies = [pltpu.make_async_copy(blocks.at[rows_of[slot]], held.at[slot], ins.at[slot, 2])]
+        for side, factor in enumerate(factors):
+            copies.append(
+                pltpu.make_async_copy(factor.at[slot], sides.at[side, slot], ins.at[slot, side])
+            )
+        for copy in copies:
+            copy.start()
+        arrivals.append(copies)
+    for slot, copies in enumerate(arrivals):
+        copies[0].wait()
+        block = held[slot]
+        holds = named[slot] > 0
+        for side, new in enumerate(news):
+            axis = 1 - side
+            gram = lax.dot_general(
+                block, block, (((axis,), (axis,)), ((), ())), preferred_element_type=jnp.float32
+            )
+            copies[1 + side].wait()
+            sides[side, slot] = 0.9 * sides[side, slot] + jnp.where(holds, scale * gram, 0.0)
+            copy = pltpu.make_async_copy(sides.at[side, slot], new.at[slot], outs.at[slot, side])
+            copy.start()
+            leaving.append(copy)
+    for copy in leaving:
+        copy.wait()
 
 
 def statistics(rows_of, named, blocks, factor_left, factor_right):
     capacity, block_size = factor_left.shape[0], factor_left.shape[1]
-    at_row = lambda t, rows_of, named: (rows_of[t], 0, 0)
-    square = pl.BlockSpec((1, block_size, block_size), lambda t, rows_of, named: (t, 0, 0))
+    smem, hbm = pl.BlockSpec(memory_space=pltpu.SMEM), pl.BlockSpec(memory_space=pltpu.HBM)
+    arrays = [
+        pltpu.with_memory_space_constraint(array, pltpu.HBM)
+        for array in (blocks, factor_left, factor_right)
+    ]
     return pl.pallas_call(
         gram_kernel,
-        grid_spec=pltpu.PrefetchScalarGridSpec(
-            num_scalar_prefetch=2,
-            grid=(capacity,),
-            in_specs=[pl.BlockSpec((1, block_size, block_size), at_row), square, square],
-            out_specs=[square, square],
-        ),
         out_shape=[jax.ShapeDtypeStruct(factor_left.shape, jnp.float32)] * 2,
+        in_specs=[smem, smem, hbm, hbm, hbm],
+        out_specs=[any_spec(), any_spec()],
+        scratch_shapes=[
+            pltpu.VMEM((capacity, block_size, block_size), jnp.bfloat16),
+            pltpu.VMEM((2, capacity, block_size, block_size), jnp.float32),
+            pltpu.SemaphoreType.DMA((capacity, 3)),
+            pltpu.SemaphoreType.DMA((capacity, 2)),
+        ],
         compiler_params=params(),
         cost_estimate=pl.CostEstimate(
             flops=AHEAD,
@@ -166,13 +193,7 @@
             transcendentals=0,
         ),
         name="statistics",
-    )(
-        rows_of,
-        named,
-        blocks,
-        pltpu.with_memory_space_constraint(factor_left, pltpu.HBM),
-        pltpu.with_memory_space_constraint(factor_right, pltpu.HBM),
-    )
+    )(rows_of, named, *arrays)
 
 
 def pick_kernel(block_size, owners, slots, *refs):
@@ -198,6 +219,26 @@
         ),
         name="from_slots",
     )(owners, slots, *(pltpu.with_memory_space_constraint(a, pltpu.HBM) for a in after))
+
+
+def again_kernel(*refs):
+    count = len(refs) // 2
+    for given, out in zip(refs[:count], refs[count:], strict=True):
+        out[...] = given[...]
+
+
+def again(*arrays):
+    return pl.pallas_call(
+        again_kernel,
+        out_shape=[jax.ShapeDtypeStruct(array.shape, jnp.bfloat16) for array in arrays],
+        in_specs=[vmem_spec()] * len(arrays),
+        out_specs=[vmem_spec()] * len(arrays),
+        compiler_params=params(),
+        cost_estimate=pl.CostEstimate(
+            flops=0, bytes_accessed=4 * sum(array.size for array in arrays), transcendentals=0
+        ),
+        name="again",
+    )(*arrays)
 
 
 def place_kernel(start, groups, *refs):
@@ -305,6 +346,7 @@
         rows = out.shape[2]
         if before is not None:
             out, before = lax.optimization_barrier((out, before))
+            (out,) = again(out)
         returned = lax.all_to_all(
             out.reshape(num_shards, rows, block_size),
             "shard",
@@ -313,9 +355,8 @@
             tiled=True,
         )
         low, high = from_slots(owners, returned, () if before is None else (new_left,))
-        later, (low, high) = lax.optimization_barrier((owners, (low, high)))
         left_low, right_high = to_right(low), to_left(high)
-        own_low, own_high = before = from_slots(later, returned)
+        own_low, own_high = before = again(low, high)
         left_high, right_low = to_right(own_high), to_left(own_low)
         far_low, far_high = to_right(left_low), to_left(right_high)
         near = (own_low, own_high, left_low, left_high, right_low, right_high)

time: 143 us -> 141 us (0.986)
  Pallas kernels: 26.8 us -> 22.5 us
  waiting for transfers between devices: 16.7 us -> 18.9 us
    pallas_call x4 -> x2, Pallas kernels: 4.01 us -> 1.15 us  [from_slots(): pl.pallas_call(functools.partial(pick_kernel, block_size), out_shape=[jax...]
    ppermute x9, waiting for transfers between devices: 7.66 us -> 9.83 us  [body(): to_right = lambda a: lax.ppermute(a, 'replica', onward)]
    pallas_call x1 -> x4, Pallas kernels: 7.63 us -> 7.92 us  [the longest x1 7.03 us: statistics(): pl.pallas_call(gram_kernel, out_shape=[jax.ShapeDtypeStruct(factor_left.s...]
  transfers between devices with their start and end apart: 19 -> 19, of which waited for: 7 -> 9; matrix products, arithmetic and copies ran while one was open for 3% -> 3% of each run, Pallas kernels for 13% -> 11%
where the time goes in v6:
time: 141 us
  blocking collectives  61.7 us (44%)
  starting transfers between devices  31.6 us (22%)
  Pallas kernels  22.5 us (16%)
  waiting for transfers between devices  18.9 us (13%)
  local copies, waits for them, and re-layouts  4.34 us (3%)
    all_to_all x1, blocking collectives, body(): lax.all_to_all(slots, 'shard', split_axis=0, concat_axis=0, tiled=True)  35.4 us
    all_to_all x1, blocking collectives, body(): lax.all_to_all(out.reshape(num_shards, rows, block_size), 'shard', split_...  26.2 us
    ppermute x9, starting transfers between devices, body(): to_left = lambda a: lax.ppermute(a, 'replica', back)  22.6 us
    ppermute x9, waiting for transfers between devices, body(): to_right = lambda a: lax.ppermute(a, 'replica', onward)  9.83 us
    ppermute x9, waiting for transfers between devices, body(): to_left = lambda a: lax.ppermute(a, 'replica', back)  9.09 us
    pallas_call x1, Pallas kernels, statistics(): pl.pallas_call(gram_kernel, out_shape=[jax.ShapeDtypeStruct(factor_left.s...  7.03 us
    ppermute x9, starting transfers between devices, body(): to_right = lambda a: lax.ppermute(a, 'replica', onward)  4.98 us
    pallas_call x2, Pallas kernels, cut(): pl.pallas_call(functools.partial(cut_kernel, [(group, start) for group, s...  4.36 us
  transfers between devices with their start and end apart: 19, of which 9 were waited for; matrix products, arithmetic and copies ran while one was open for 3% of the time, Pallas kernels for 11%

profile of v6, /device:TPU:0, one launch (start us, length us, event | category | flops | bytes accessed | tf_op | source)
XLA Modules:
  0.0 140.9 jit_solution(13102778110854721530)
XLA Ops:
  0.7 1.7 %cut.2 = (bf16[32,7168]{1,0:T(8,128)(2,1)S(1)}, bf16[32,7168]{1,0:T(8,128)(2,1)S(1)}) custom-call(s32[4]{0:T(128)S(1)} %pad_add_fusion.groups, bf16[1,64,28672]{2,1,0:T(8,128)(2,1)} %grads.3), custom_call_target="tpu_custom_call" | custom-call | bytes 1835008 | tf_op jit(solution)/shard_map/cut/pallas_call | solution.py:42
  2.5 2.1 %collective-permute-start = (bf16[32,7168]{1,0:T(8,128)(2,1)S(1)}, bf16[32,7168]{1,0:T(8,128)(2,1)}, u32[]{:S(2)}, u32[]{:S(2)}) collective-permute-start(bf16[32,7168]{1,0:T(8,128)(2,1)S(1)} %get-tuple-element.27.refs_0_), channel_id=1, source_target_pairs={{0,32},{32,64},{64,96},{96,0},{1,33},{33,65},{65,97},{97,1},{2,34}... | collective-permute-start | bytes 1376264 | tf_op jit(solution)/shard_map/ppermute | solution.py:291
  4.5 2.2 %collective-permute-start.1 = (bf16[32,7168]{1,0:T(8,128)(2,1)S(1)}, bf16[32,7168]{1,0:T(8,128)(2,1)}, u32[]{:S(2)}, u32[]{:S(2)}) collective-permute-start(bf16[32,7168]{1,0:T(8,128)(2,1)S(1)} %get-tuple-element.28.refs_1_), channel_id=1, source_target_pairs={{0,96},{32,0},{64,32},{96,64},{1,97},{33,1},{65,33},{97,65},{2,98}... | collective-permute-start | bytes 1376264 | tf_op jit(solution)/shard_map/ppermute | solution.py:292
  6.8 2.6 %cut.3 = (bf16[32,7168]{1,0:T(8,128)(2,1)}, bf16[32,7168]{1,0:T(8,128)(2,1)}) custom-call(s32[4]{0:T(128)S(1)} %pad_add_fusion.groups, bf16[1,64,28672]{2,1,0:T(8,128)(2,1)} %grads.3, bf16[32,7168]{1,0:T(8,128)(2,1)S(1)} %get-tuple-element.27.refs_0_, bf16[32,7168]{1,0:T(8,128)(2,1)S(1)} %get-tuple-element.28.refs_1_), custom_call_target="tpu_custom_call" | custom-call | bytes 1835008 | tf_op jit(solution)/shard_map/cut/pallas_call | solution.py:42
  9.5 3.2 %collective-permute-start.4 = (bf16[32,7168]{1,0:T(8,128)(2,1)}, bf16[32,7168]{1,0:T(8,128)(2,1)S(1)}, u32[]{:S(2)}, u32[]{:S(2)}) collective-permute-start(bf16[32,7168]{1,0:T(8,128)(2,1)} %get-tuple-element.33), channel_id=1, source_target_pairs={{0,96},{32,0},{64,32},{96,64},{1,97},{33,1},{65,33},{97,65},{2,98}... | collective-permute-start | bytes 1376264 | tf_op jit(solution)/shard_map/ppermute | solution.py:292
  12.7 1.2 dynamic-slice_bitcast_fusion.own
  13.9 2.0 %dynamic-slice_bitcast_fusion.1 = (bf16[32,7168]{1,0:T(8,128)(2,1)S(1)}, bf16[32,7168]{1,0:T(8,128)(2,1)}) fusion(bf16[8,8,4,7168]{3,1,2,0:T(8,128)(2,1)} %bitcast.42, s32[]{:T(128)S(6)} %select_n.52, s32[]{:T(128)S(6)} %select_n.49), kind=kLoop, calls=%fused_computation.1 | loop fusion | bytes 1835016 | tf_op jit(solution)/shard_map/reshape | solution.py:328
  16.3 1.8 %collective-permute-done.passed_right = bf16[32,7168]{1,0:T(8,128)(2,1)} collective-permute-done((bf16[32,7168]{1,0:T(8,128)(2,1)S(1)}, bf16[32,7168]{1,0:T(8,128)(2,1)}, u32[]{:S(2)}, u32[]{:S(2)}) %collective-permute-start) | collective-permute-done | bytes 458784 | tf_op jit(solution)/shard_map/ppermute | solution.py:291
  18.1 1.0 copy-done.1
  19.1 2.2 %relays.1 = (bf16[32,7168]{1,0:T(8,128)(2,1)}, bf16[32,7168]{1,0:T(8,128)(2,1)}) custom-call(bf16[32,7168]{1,0:T(8,128)(2,1)S(1)} %copy-done.1, bf16[32,7168]{1,0:T(8,128)(2,1)} %collective-permute-done.passed_right, bf16[32,7168]{1,0:T(8,128)(2,1)S(1)} %get-tuple-element.54.behind, bf16[32,7168]{1,0:T(8,128)(2,1)} %collective-permute-done.1.passed_left), custom_call_target="tpu_custom_call" | custom-call | flops 30000001024 | bytes 2752512 | tf_op jit(solution)/shard_map/relays/pallas_call | solution.py:64
  21.3 3.4 %collective-permute-start.2 = (bf16[32,7168]{1,0:T(8,128)(2,1)}, bf16[32,7168]{1,0:T(8,128)(2,1)S(1)}, u32[]{:S(2)}, u32[]{:S(2)}) collective-permute-start(bf16[32,7168]{1,0:T(8,128)(2,1)} %get-tuple-element.29), channel_id=1, source_target_pairs={{0,96},{32,0},{64,32},{96,64},{1,97},{33,1},{65,33},{97,65},{2,98}... | collective-permute-start | bytes 1376264 | tf_op jit(solution)/shard_map/ppermute | solution.py:292
  25.4 2.3 %collective-permute-done.3.high_b = bf16[32,7168]{1,0:T(8,128)(2,1)S(1)} collective-permute-done((bf16[32,7168]{1,0:T(8,128)(2,1)}, bf16[32,7168]{1,0:T(8,128)(2,1)S(1)}, u32[]{:S(2)}, u32[]{:S(2)}) %collective-permute-start.3) | collective-permute-done | bytes 458784 | tf_op jit(solution)/shard_map/ppermute | solution.py:291
  27.7 8.7 %collective-permute-done.2.high_a = bf16[32,7168]{1,0:T(8,128)(2,1)S(1)} collective-permute-done((bf16[32,7168]{1,0:T(8,128)(2,1)}, bf16[32,7168]{1,0:T(8,128)(2,1)S(1)}, u32[]{:S(2)}, u32[]{:S(2)}) %collective-permute-start.2) | collective-permute-done | bytes 458784 | tf_op jit(solution)/shard_map/ppermute | solution.py:292
  36.8 0.9 to_slots.1
  37.7 35.4 %all_to_all.15 = bf16[32,64,512]{2,1,0:T(8,128)(2,1)S(1)} all-to-all(bf16[32,64,512]{2,1,0:T(8,128)(2,1)S(1)} %to_slots.1), channel_id=1, replica_groups=mesh['replica'=4,'shard'=32] {'shard'}, dimensions={0} | all-to-all | bytes 4194304 | tf_op jit(solution)/shard_map/all_to_all | solution.py:339
  73.2 2.3 %updates.1 = (bf16[4,8,48,512]{3,2,1,0:T(8,128)(2,1)S(1)}, bf16[4,8,16,512]{3,2,1,0:T(8,128)(2,1)S(1)}) custom-call(s32[3]{0:T(128)S(1)} %select_reduce_fusion.rows_of, bf16[4,512,512]{2,1,0:T(8,128)(2,1)S(1)} %bitcast.36, bf16[3,512,512]{2,1,0:T(8,128)(2,1)S(1)} %bitcast.39, bf16[3,512,512]{2,1,0:T(8,128)(2,1)S(1)} %bitcast.40), custom_call_target="tpu_custom_call" | custom-call | flops 1610612736 | bytes 6291456 | tf_op jit(solution)/shard_map/updates/pallas_call | solution.py:121
  75.5 26.2 %all_to_all.16.slots = bf16[32,48,512]{2,1,0:T(8,128)(2,1)S(1)} all-to-all(bf16[32,48,512]{2,1,0:T(8,128)(2,1)S(1)} %bitcast.38), channel_id=1, replica_groups=mesh['replica'=4,'shard'=32] {'shard'}, dimensions={0} | all-to-all | bytes 3145728 | tf_op jit(solution)/shard_map/all_to_all | solution.py:350
  102.4 1.3 collective-permute-start.12
  103.7 2.0 %collective-permute-start.15 = (bf16[48,3584]{1,0:T(8,128)(2,1)S(1)}, bf16[48,3584]{1,0:T(8,128)(2,1)S(1)}, u32[]{:S(2)}, u32[]{:S(2)}) collective-permute-start(bf16[48,3584]{1,0:T(8,128)(2,1)S(1)} %get-tuple-element.43.refs_1_), channel_id=1, source_target_pairs={{0,96},{32,0},{64,32},{96,64},{1,97},{33,1},{65,33},{97,65},{2,98}... | collective-permute-start | bytes 1032200 | tf_op jit(solution)/shard_map/ppermute | solution.py:292
  105.7 1.9 %collective-permute-start.14 = (bf16[48,3584]{1,0:T(8,128)(2,1)S(1)}, bf16[48,3584]{1,0:T(8,128)(2,1)S(1)}, u32[]{:S(2)}, u32[]{:S(2)}) collective-permute-start(bf16[48,3584]{1,0:T(8,128)(2,1)S(1)} %get-tuple-element.44.refs_0_), channel_id=1, source_target_pairs={{0,96},{32,0},{64,32},{96,64},{1,97},{33,1},{65,33},{97,65},{2,98}... | collective-permute-start | bytes 1032200 | tf_op jit(solution)/shard_map/ppermute | solution.py:292
  108.7 4.1 %all-to-all-start.2 = ((bf16[32,16,512]{2,1,0:T(8,128)(2,1)}), bf16[32,16,512]{2,1,0:T(8,128)(2,1)S(1)}, u32[]{:S(2)}, u32[]{:S(2)}) async-start(bf16[32,16,512]{2,1,0:T(8,128)(2,1)} %bitcast.22), calls=%async_computation.2 | async-start | bytes 1048576 | tf_op jit(solution)/shard_map/all_to_all | solution.py:350
  112.7 1.8 %collective-permute-done.12.refs_2_ = bf16[48,3584]{1,0:T(8,128)(2,1)S(1)} collective-permute-done((bf16[48,3584]{1,0:T(8,128)(2,1)S(1)}, bf16[48,3584]{1,0:T(8,128)(2,1)S(1)}, u32[]{:S(2)}, u32[]{:S(2)}) %collective-permute-start.12) | collective-permute-done | bytes 344096 | tf_op jit(solution)/shard_map/ppermute | solution.py:291
  114.6 3.2 %collective-permute-start.17 = (bf16[48,3584]{1,0:T(8,128)(2,1)S(1)}, bf16[48,3584]{1,0:T(8,128)(2,1)S(1)}, u32[]{:S(2)}, u32[]{:S(2)}) collective-permute-start(bf16[48,3584]{1,0:T(8,128)(2,1)S(1)} %collective-permute-done.15.refs_5_), channel_id=1, source_target_pairs={{0,96},{32,0},{64,32},{96,64},{1,97},{33,1},{65,33},{97,65},{2,98}... | collective-permute-start | bytes 1032200 | tf_op jit(solution)/shard_map/ppermute | solution.py:292
  117.8 7.0 %statistics.1 = (f32[3,512,512]{2,1,0:T(8,128)}, f32[3,512,512]{2,1,0:T(8,128)}) custom-call(s32[3]{0:T(128)S(1)} %select_reduce_fusion.rows_of, s32[3]{0:T(128)S(1)} %get-tuple-element.32.named, bf16[4,512,512]{2,1,0:T(8,128)(2,1)} %bitcast.37, f32[3,512,512]{2,1,0:T(8,128)} %bitcast.46, f32[3,512,512]{2,1,0:T(8,128)} %bitcast.47), custom_call_target="tpu_custom_call" | custom-call | flops 30000001024 | bytes 14155776 | tf_op jit(solution)/shard_map/statistics/pallas_call | solution.py:178
  125.5 3.2 %collective-permute-start.9 = (bf16[16,3584]{1,0:T(8,128)(2,1)S(1)}, bf16[16,3584]{1,0:T(8,128)(2,1)S(1)}, u32[]{:S(2)}, u32[]{:S(2)}) collective-permute-start(bf16[16,3584]{1,0:T(8,128)(2,1)S(1)} %get-tuple-element.48.refs_1_), channel_id=1, source_target_pairs={{0,96},{32,0},{64,32},{96,64},{1,97},{33,1},{65,33},{97,65},{2,98}... | collective-permute-start | bytes 344072 | tf_op jit(solution)/shard_map/ppermute | solution.py:292
  128.8 1.0 collective-permute-start.8
  129.7 1.9 %collective-permute-done.6.refs_2_ = bf16[16,3584]{1,0:T(8,128)(2,1)S(1)} collective-permute-done((bf16[16,3584]{1,0:T(8,128)(2,1)S(1)}, bf16[16,3584]{1,0:T(8,128)(2,1)S(1)}, u32[]{:S(2)}, u32[]{:S(2)}) %collective-permute-start.6) | collective-permute-done | bytes 114720 | tf_op jit(solution)/shard_map/ppermute | solution.py:291
  132.1 1.2 collective-permute-start.10
  133.3 2.5 %collective-permute-start.11 = (bf16[16,3584]{1,0:T(8,128)(2,1)S(1)}, bf16[16,3584]{1,0:T(8,128)(2,1)S(1)}, u32[]{:S(2)}, u32[]{:S(2)}) collective-permute-start(bf16[16,3584]{1,0:T(8,128)(2,1)S(1)} %collective-permute-done.9.refs_5_), channel_id=1, source_target_pairs={{0,96},{32,0},{64,32},{96,64},{1,97},{33,1},{65,33},{97,65},{2,98}... | collective-permute-start | bytes 344072 | tf_op jit(solution)/shard_map/ppermute | solution.py:292
  135.8 2.1 %place.2.refs_8_ = bf16[64,28672]{1,0:T(8,128)(2,1)} custom-call(s32[4]{0:T(128)S(1)} %pad_add_fusion.groups, bf16[48,3584]{1,0:T(8,128)(2,1)S(1)} %get-tuple-element.44.refs_0_, bf16[48,3584]{1,0:T(8,128)(2,1)S(1)} %get-tuple-element.45.refs_1_, bf16[48,3584]{1,0:T(8,128)(2,1)S(1)} %collective-permute-done.12.refs_2_, ...), custom_call_target="tpu_custom_call" | custom-call | bytes 5505024 | tf_op jit(solution)/shard_map/place/pallas_call | solution.py:259
  138.2 1.2 collective-permute-done.10.refs_6_
  139.4 1.5 %place.3 = bf16[64,28672]{1,0:T(8,128)(2,1)} custom-call(s32[4]{0:T(128)S(1)} %pad_add_fusion.groups, bf16[16,3584]{1,0:T(8,128)(2,1)S(1)} %get-tuple-element.49.refs_0_, bf16[16,3584]{1,0:T(8,128)(2,1)S(1)} %get-tuple-element.50.refs_1_, bf16[16,3584]{1,0:T(8,128)(2,1)S(1)} %collective-permute-done.6.refs_2_, ...), custom_call_target="tpu_custom_call", output_to_operand_aliasing={{}: (9, {})} | custom-call | bytes 1835008 | tf_op jit(solution)/shard_map/place/pallas_call | solution.py:259
  (43 shorter events, 4.7 us)
Async XLA Ops:
  2.5 15.6 %collective-permute-start = (bf16[32,7168]{1,0:T(8,128)(2,1)S(1)}, bf16[32,7168]{1,0:T(8,128)(2,1)}, u32[]{:S(2)}, u32[]{:S(2)}) collective-permute-start(bf16[32,7168]{1,0:T(8,128)(2,1)S(1)} %get-tuple-element.27.refs_0_), channel_id=1, source_target_pairs={{0,32},{32,64},{64,96},{96,0},{1,33},{33,65},{65,97},{97,1},{2,34}... | collective-permute-start | bytes 1376264 | tf_op jit(solution)/shard_map/ppermute | solution.py:291
  4.5 11.4 %copy-start.4 = (s32[4,56]{1,0:T(4,128)S(1)}, s32[4,56]{1,0:T(4,128)}, u32[]{:S(2)}) copy-start(s32[4,56]{1,0:T(4,128)} %param.7) | copy-start | bytes 2692
  4.5 13.6 %collective-permute-start.1 = (bf16[32,7168]{1,0:T(8,128)(2,1)S(1)}, bf16[32,7168]{1,0:T(8,128)(2,1)}, u32[]{:S(2)}, u32[]{:S(2)}) collective-permute-start(bf16[32,7168]{1,0:T(8,128)(2,1)S(1)} %get-tuple-element.28.refs_1_), channel_id=1, source_target_pairs={{0,96},{32,0},{64,32},{96,64},{1,97},{33,1},{65,33},{97,65},{2,98}... | collective-permute-start | bytes 1376264 | tf_op jit(solution)/shard_map/ppermute | solution.py:292
  9.4 18.3 %collective-permute-start.3 = (bf16[32,7168]{1,0:T(8,128)(2,1)}, bf16[32,7168]{1,0:T(8,128)(2,1)S(1)}, u32[]{:S(2)}, u32[]{:S(2)}) collective-permute-start(bf16[32,7168]{1,0:T(8,128)(2,1)} %get-tuple-element.30), channel_id=1, source_target_pairs={{0,32},{32,64},{64,96},{96,0},{1,33},{33,65},{65,97},{97,1},{2,34}... | collective-permute-start | bytes 1376264 | tf_op jit(solution)/shard_map/ppermute | solution.py:291
  9.5 26.9 %collective-permute-start.4 = (bf16[32,7168]{1,0:T(8,128)(2,1)}, bf16[32,7168]{1,0:T(8,128)(2,1)S(1)}, u32[]{:S(2)}, u32[]{:S(2)}) collective-permute-start(bf16[32,7168]{1,0:T(8,128)(2,1)} %get-tuple-element.33), channel_id=1, source_target_pairs={{0,96},{32,0},{64,32},{96,64},{1,97},{33,1},{65,33},{97,65},{2,98}... | collective-permute-start | bytes 1376264 | tf_op jit(solution)/shard_map/ppermute | solution.py:292
  18.1 1.0 copy-start.1
  21.3 15.0 %collective-permute-start.2 = (bf16[32,7168]{1,0:T(8,128)(2,1)}, bf16[32,7168]{1,0:T(8,128)(2,1)S(1)}, u32[]{:S(2)}, u32[]{:S(2)}) collective-permute-start(bf16[32,7168]{1,0:T(8,128)(2,1)} %get-tuple-element.29), channel_id=1, source_target_pairs={{0,96},{32,0},{64,32},{96,64},{1,97},{33,1},{65,33},{97,65},{2,98}... | collective-permute-start | bytes 1376264 | tf_op jit(solution)/shard_map/ppermute | solution.py:292
  24.7 12.1 %collective-permute-start.5 = (bf16[32,7168]{1,0:T(8,128)(2,1)}, bf16[32,7168]{1,0:T(8,128)(2,1)S(1)}, u32[]{:S(2)}, u32[]{:S(2)}) collective-permute-start(bf16[32,7168]{1,0:T(8,128)(2,1)} %get-tuple-element.34), channel_id=1, source_target_pairs={{0,32},{32,64},{64,96},{96,0},{1,33},{33,65},{65,97},{97,1},{2,34}... | collective-permute-start | bytes 1376264 | tf_op jit(solution)/shard_map/ppermute | solution.py:291
  37.7 35.5 %copy-start.2 = (bf16[1,3,512,512]{3,2,1,0:T(8,128)(2,1)S(1)}, bf16[1,3,512,512]{3,2,1,0:T(8,128)(2,1)}, u32[]{:S(2)}) copy-start(bf16[1,3,512,512]{3,2,1,0:T(8,128)(2,1)} %param.10) | copy-start | bytes 4718596
  37.7 35.5 %copy-start.3 = (bf16[1,3,512,512]{3,2,1,0:T(8,128)(2,1)S(1)}, bf16[1,3,512,512]{3,2,1,0:T(8,128)(2,1)}, u32[]{:S(2)}) copy-start(bf16[1,3,512,512]{3,2,1,0:T(8,128)(2,1)} %param.11) | copy-start | bytes 4718596
  73.2 28.6 %copy-start = (bf16[32,64,512]{2,1,0:T(8,128)(2,1)}, bf16[32,64,512]{2,1,0:T(8,128)(2,1)S(1)}, u32[]{:S(2)}) copy-start(bf16[32,64,512]{2,1,0:T(8,128)(2,1)S(1)} %all_to_all.15) | copy-start | bytes 6291460
  102.4 12.2 %collective-permute-start.12 = (bf16[48,3584]{1,0:T(8,128)(2,1)S(1)}, bf16[48,3584]{1,0:T(8,128)(2,1)S(1)}, u32[]{:S(2)}, u32[]{:S(2)}) collective-permute-start(bf16[48,3584]{1,0:T(8,128)(2,1)S(1)} %get-tuple-element.42.refs_0_), channel_id=1, source_target_pairs={{0,32},{32,64},{64,96},{96,0},{1,33},{33,65},{65,97},{97,1},{2,34}... | collective-permute-start | bytes 1032200 | tf_op jit(solution)/shard_map/ppermute | solution.py:291
  103.7 10.9 %collective-permute-start.15 = (bf16[48,3584]{1,0:T(8,128)(2,1)S(1)}, bf16[48,3584]{1,0:T(8,128)(2,1)S(1)}, u32[]{:S(2)}, u32[]{:S(2)}) collective-permute-start(bf16[48,3584]{1,0:T(8,128)(2,1)S(1)} %get-tuple-element.43.refs_1_), channel_id=1, source_target_pairs={{0,96},{32,0},{64,32},{96,64},{1,97},{33,1},{65,33},{97,65},{2,98}... | collective-permute-start | bytes 1032200 | tf_op jit(solution)/shard_map/ppermute | solution.py:292
  105.7 19.8 %collective-permute-start.14 = (bf16[48,3584]{1,0:T(8,128)(2,1)S(1)}, bf16[48,3584]{1,0:T(8,128)(2,1)S(1)}, u32[]{:S(2)}, u32[]{:S(2)}) collective-permute-start(bf16[48,3584]{1,0:T(8,128)(2,1)S(1)} %get-tuple-element.44.refs_0_), channel_id=1, source_target_pairs={{0,96},{32,0},{64,32},{96,64},{1,97},{33,1},{65,33},{97,65},{2,98}... | collective-permute-start | bytes 1032200 | tf_op jit(solution)/shard_map/ppermute | solution.py:292
  107.6 21.1 %collective-permute-start.13 = (bf16[48,3584]{1,0:T(8,128)(2,1)S(1)}, bf16[48,3584]{1,0:T(8,128)(2,1)S(1)}, u32[]{:S(2)}, u32[]{:S(2)}) collective-permute-start(bf16[48,3584]{1,0:T(8,128)(2,1)S(1)} %get-tuple-element.45.refs_1_), channel_id=1, source_target_pairs={{0,32},{32,64},{64,96},{96,0},{1,33},{33,65},{65,97},{97,1},{2,34}... | collective-permute-start | bytes 1032200 | tf_op jit(solution)/shard_map/ppermute | solution.py:291
  108.7 16.2 %all-to-all-start.2 = ((bf16[32,16,512]{2,1,0:T(8,128)(2,1)}), bf16[32,16,512]{2,1,0:T(8,128)(2,1)S(1)}, u32[]{:S(2)}, u32[]{:S(2)}) async-start(bf16[32,16,512]{2,1,0:T(8,128)(2,1)} %bitcast.22), calls=%async_computation.2 | async-start | bytes 1048576 | tf_op jit(solution)/shard_map/all_to_all | solution.py:350
  114.6 18.7 %collective-permute-start.16 = (bf16[48,3584]{1,0:T(8,128)(2,1)S(1)}, bf16[48,3584]{1,0:T(8,128)(2,1)S(1)}, u32[]{:S(2)}, u32[]{:S(2)}) collective-permute-start(bf16[48,3584]{1,0:T(8,128)(2,1)S(1)} %collective-permute-done.12.refs_2_), channel_id=1, source_target_pairs={{0,32},{32,64},{64,96},{96,0},{1,33},{33,65},{65,97},{97,1},{2,34}... | collective-permute-start | bytes 1032200 | tf_op jit(solution)/shard_map/ppermute | solution.py:291
  114.6 21.2 %collective-permute-start.17 = (bf16[48,3584]{1,0:T(8,128)(2,1)S(1)}, bf16[48,3584]{1,0:T(8,128)(2,1)S(1)}, u32[]{:S(2)}, u32[]{:S(2)}) collective-permute-start(bf16[48,3584]{1,0:T(8,128)(2,1)S(1)} %collective-permute-done.15.refs_5_), channel_id=1, source_target_pairs={{0,96},{32,0},{64,32},{96,64},{1,97},{33,1},{65,33},{97,65},{2,98}... | collective-permute-start | bytes 1032200 | tf_op jit(solution)/shard_map/ppermute | solution.py:292
  125.4 6.2 %collective-permute-start.6 = (bf16[16,3584]{1,0:T(8,128)(2,1)S(1)}, bf16[16,3584]{1,0:T(8,128)(2,1)S(1)}, u32[]{:S(2)}, u32[]{:S(2)}) collective-permute-start(bf16[16,3584]{1,0:T(8,128)(2,1)S(1)} %get-tuple-element.47.refs_0_), channel_id=1, source_target_pairs={{0,32},{32,64},{64,96},{96,0},{1,33},{33,65},{65,97},{97,1},{2,34}... | collective-permute-start | bytes 344072 | tf_op jit(solution)/shard_map/ppermute | solution.py:291
  125.5 6.6 %collective-permute-start.9 = (bf16[16,3584]{1,0:T(8,128)(2,1)S(1)}, bf16[16,3584]{1,0:T(8,128)(2,1)S(1)}, u32[]{:S(2)}, u32[]{:S(2)}) collective-permute-start(bf16[16,3584]{1,0:T(8,128)(2,1)S(1)} %get-tuple-element.48.refs_1_), channel_id=1, source_target_pairs={{0,96},{32,0},{64,32},{96,64},{1,97},{33,1},{65,33},{97,65},{2,98}... | collective-permute-start | bytes 344072 | tf_op jit(solution)/shard_map/ppermute | solution.py:292
  128.8 9.2 %collective-permute-start.8 = (bf16[16,3584]{1,0:T(8,128)(2,1)S(1)}, bf16[16,3584]{1,0:T(8,128)(2,1)S(1)}, u32[]{:S(2)}, u32[]{:S(2)}) collective-permute-start(bf16[16,3584]{1,0:T(8,128)(2,1)S(1)} %get-tuple-element.49.refs_0_), channel_id=1, source_target_pairs={{0,96},{32,0},{64,32},{96,64},{1,97},{33,1},{65,33},{97,65},{2,98}... | collective-permute-start | bytes 344072 | tf_op jit(solution)/shard_map/ppermute | solution.py:292
  131.7 6.5 %collective-permute-start.7 = (bf16[16,3584]{1,0:T(8,128)(2,1)S(1)}, bf16[16,3584]{1,0:T(8,128)(2,1)S(1)}, u32[]{:S(2)}, u32[]{:S(2)}) collective-permute-start(bf16[16,3584]{1,0:T(8,128)(2,1)S(1)} %get-tuple-element.50.refs_1_), channel_id=1, source_target_pairs={{0,32},{32,64},{64,96},{96,0},{1,33},{33,65},{65,97},{97,1},{2,34}... | collective-permute-start | bytes 344072 | tf_op jit(solution)/shard_map/ppermute | solution.py:291
  132.1 7.3 %collective-permute-start.10 = (bf16[16,3584]{1,0:T(8,128)(2,1)S(1)}, bf16[16,3584]{1,0:T(8,128)(2,1)S(1)}, u32[]{:S(2)}, u32[]{:S(2)}) collective-permute-start(bf16[16,3584]{1,0:T(8,128)(2,1)S(1)} %collective-permute-done.6.refs_2_), channel_id=1, source_target_pairs={{0,32},{32,64},{64,96},{96,0},{1,33},{33,65},{65,97},{97,1},{2,34}... | collective-permute-start | bytes 344072 | tf_op jit(solution)/shard_map/ppermute | solution.py:291
  133.3 6.2 %collective-permute-start.11 = (bf16[16,3584]{1,0:T(8,128)(2,1)S(1)}, bf16[16,3584]{1,0:T(8,128)(2,1)S(1)}, u32[]{:S(2)}, u32[]{:S(2)}) collective-permute-start(bf16[16,3584]{1,0:T(8,128)(2,1)S(1)} %collective-permute-done.9.refs_5_), channel_id=1, source_target_pairs={{0,96},{32,0},{64,32},{96,64},{1,97},{33,1},{65,33},{97,65},{2,98}... | collective-permute-start | bytes 344072 | tf_op jit(solution)/shard_map/ppermute | solution.py:292
